TPU v7x, 32 devices: a whole 2x2x4 slice. The times are simulated.
32 devices in a mesh: img: 8 (over z, x), pos: 4 (over y, core).
Axes of the slice: x: 2, y: 2, z: 4, core: 2. Of those that a mesh axis runs over, the one named last changes fastest.
Arguments:
- tokens: bfloat16 [8192, 768], P(('img', 'pos')), may hold values from -6 to 6
- image_slot: int32 [8192], P(('img', 'pos')), may hold values from -1 to 4, as said below
- patch_position: int32 [8192], P(('img', 'pos')), may hold values from -1 to 195, as said below
- ln1_gain: float32 [768], replicated, may hold values from 0.5 to 1.5
- ln1_bias: float32 [768], replicated, may hold values from -3 to 3
- w_qkv: bfloat16 [768, 2304], replicated, may hold values from -0.21875 to 0.21875
- bias_query: float32 [768], replicated, may hold values from -3 to 3
- bias_value: float32 [768], replicated, may hold values from -3 to 3
- w_out: bfloat16 [768, 768], replicated, may hold values from -0.875 to 0.875
- bias_out: float32 [768], replicated, may hold values from -3 to 3
- ln2_gain: float32 [768], replicated, may hold values from 0.5 to 1.5
- ln2_bias: float32 [768], replicated, may hold values from -3 to 3
- w_up: bfloat16 [768, 3072], replicated, may hold values from -0.21875 to 0.21875
- bias_up: float32 [3072], replicated, may hold values from -3 to 3
- w_down: bfloat16 [3072, 768], replicated, may hold values from -0.109375 to 0.109375
- bias_down: float32 [768], replicated, may hold values from -3 to 3
- w_proj: bfloat16 [768, 512], replicated, may hold values from -0.21875 to 0.21875
- bias_proj: float32 [512], replicated, may hold values from -3 to 3
- mask_token: bfloat16 [512], replicated, may hold values from -4 to 4
- cotangent: bfloat16 [160, 196, 512], P('img', 'pos'), may hold values from -6 to 6
Outputs:
- decoder_input: bfloat16 [160, 196, 512], P('img', 'pos')
- grad_tokens: bfloat16 [8192, 768], P(('img', 'pos'))
- grad_ln1_gain: float32 [768], replicated
- grad_ln1_bias: float32 [768], replicated
- grad_w_qkv: float32 [768, 2304], P('img')
- grad_bias_query: float32 [768], replicated
- grad_bias_value: float32 [768], replicated
- grad_w_out: float32 [768, 768], P('img')
- grad_bias_out: float32 [768], replicated
- grad_ln2_gain: float32 [768], replicated
- grad_ln2_bias: float32 [768], replicated
- grad_w_up: float32 [768, 3072], P('img')
- grad_bias_up: float32 [3072], replicated
- grad_w_down: float32 [3072, 768], P('img')
- grad_bias_down: float32 [768], replicated
- grad_w_proj: float32 [768, 512], P('img')
- grad_bias_proj: float32 [512], replicated
- grad_mask_token: float32 [512], replicated
Inputs may be any that keep to these rules, and one draw needn't show every extreme that they name: `image_slot`: each sequence of 256 rows holds its 5 images in order 0 to 4, each on 49 consecutive rows; the remaining rows are padding, marked -1, in gaps before, between or after images. `patch_position`: rows of one image hold distinct positions; padded rows hold -1. Of each image, between 9 and 16 positions fall in each aligned range of 49 positions, and in every sequence some image has exactly 16 in one range.
All inputs are finite; a program needn't handle non-finite values.
Results may differ from a plain program's by a relative error of at most 0.012.
Values may be sent and summed in bfloat16 or wider, within the bound.
A program may use at most 192 MiB of HBM per device.

v0:
```python
import jax
import jax.numpy as jnp
from jax import lax
from jax.sharding import PartitionSpec as P

HEADS = 12
HEAD_DIM = 64
ROWS_SEQ = 256
IMG_SEQ = 5
POSITIONS = 196
CAP = 16


EPSILON = 1e-05
NEGATIVE = -1e30
GELU_COEF = 0.7978845608028654


def layer_norm(values, gain_vec, shift_vec):
    centre = jnp.mean(values, axis=-1, keepdims=True)
    centred = values - centre
    return (
        centred
        * lax.rsqrt(jnp.mean(centred * centred, axis=-1, keepdims=True) + EPSILON)
        * gain_vec
        + shift_vec
    )


def gelu_tanh(values):
    return (
        0.5 * values * (1.0 + jnp.tanh(GELU_COEF * (values + 0.044715 * values * values * values)))
    )


def matmul_rows(left, right):
    return jnp.dot(left, right, preferred_element_type=jnp.float32)


def column_sums(values):
    return jnp.sum(values.astype(jnp.float32), axis=0)


def reduce_matrices(members):
    img_count = lax.axis_size("img")
    pos_count = lax.axis_size("pos")
    pieces = [member.reshape(img_count, pos_count, -1) for member in members]
    bucket = jnp.concatenate(pieces, axis=2)
    flat_bucket = bucket.reshape(img_count * pos_count, -1)
    share = lax.psum_scatter(flat_bucket, ("img", "pos"), scatter_dimension=0, tiled=True).reshape(
        1, 1, -1
    )
    summed = lax.all_gather(share.astype(jnp.bfloat16), "pos", axis=1, tiled=True).astype(
        share.dtype
    )
    results = []
    offset = 0
    for member in members:
        extent = member.size // (img_count * pos_count)
        block = summed[0, :, offset : offset + extent]
        results.append(block.reshape(member.shape[0] // img_count, member.shape[1]))
        offset = offset + extent
    return results


def reduce_vectors(members):
    return lax.psum(tuple(members), ("img", "pos"))


def per_device(
    tokens,
    image_slot,
    patch_position,
    ln1_gain,
    ln1_bias,
    w_qkv,
    bias_query,
    bias_value,
    w_out,
    bias_out,
    ln2_gain,
    ln2_bias,
    w_up,
    bias_up,
    w_down,
    bias_down,
    w_proj,
    bias_proj,
    mask_token,
    cotangent,
):
    seq_count = tokens.shape[0] // ROWS_SEQ
    width = w_out.shape[0]
    out_width = w_proj.shape[1]
    pos_count = lax.axis_size("pos")
    quarter_len = POSITIONS // pos_count
    score_scale = HEAD_DIM ** (-0.5)
    head_shape = (seq_count, ROWS_SEQ, HEADS, HEAD_DIM)
    rows_f = tokens.astype(jnp.float32)
    normed_low = layer_norm(rows_f, ln1_gain, ln1_bias).astype(jnp.bfloat16)
    qkv_all = matmul_rows(normed_low, w_qkv)
    queries = (qkv_all[:, :width] + bias_query).astype(jnp.bfloat16).reshape(head_shape)
    keys_h = qkv_all[:, width : 2 * width].astype(jnp.bfloat16).reshape(head_shape)
    values_h = (qkv_all[:, 2 * width :] + bias_value).astype(jnp.bfloat16).reshape(head_shape)
    slot_rows = image_slot.reshape(seq_count, ROWS_SEQ)
    allowed = slot_rows[:, None, :, None] == slot_rows[:, None, None, :]
    raw_scores = (
        jnp.einsum("sqhd,skhd->shqk", queries, keys_h, preferred_element_type=jnp.float32)
        * score_scale
    )
    scores = jnp.where(allowed, raw_scores, NEGATIVE)
    top_score = jnp.max(scores, axis=-1, keepdims=True)
    log_total = top_score + jnp.log(jnp.sum(jnp.exp(scores - top_score), axis=-1, keepdims=True))
    attn_probs = jnp.exp(scores - log_total)
    probs_low = attn_probs.astype(jnp.bfloat16)
    attended = jnp.einsum(
        "shqk,skhd->sqhd", probs_low, values_h, preferred_element_type=jnp.float32
    )
    attended = attended.reshape(-1, width).astype(jnp.bfloat16)
    residual = rows_f + matmul_rows(attended, w_out) + bias_out
    normed_mlp = layer_norm(residual, ln2_gain, ln2_bias).astype(jnp.bfloat16)
    up_proj = matmul_rows(normed_mlp, w_up) + bias_up
    hidden = gelu_tanh(up_proj).astype(jnp.bfloat16)
    block_out = residual + matmul_rows(hidden, w_down) + bias_down
    block_low = block_out.astype(jnp.bfloat16)
    projected = (matmul_rows(block_low, w_proj) + bias_proj).astype(jnp.bfloat16)
    row_index = jnp.arange(ROWS_SEQ, dtype=jnp.int32)
    pos_rows = patch_position.reshape(seq_count, ROWS_SEQ)
    live = slot_rows >= 0
    bucket_id = jnp.where(live, slot_rows * pos_count + pos_rows // quarter_len, -1)
    earlier = (bucket_id[:, :, None] == bucket_id[:, None, :]) & (
        row_index[None, :, None] > row_index[None, None, :]
    )
    rank_in = jnp.sum(earlier.astype(jnp.int32), axis=2)
    target = jnp.where(live, bucket_id * CAP + rank_in, -1)
    slot_index = jnp.arange(IMG_SEQ * pos_count * CAP, dtype=jnp.int32)
    selected = slot_index[None, :, None] == target[:, None, :]
    select_low = selected.astype(jnp.bfloat16)
    outgoing = jnp.einsum(
        "sjr,src->sjc",
        select_low,
        projected.reshape(seq_count, ROWS_SEQ, out_width),
        preferred_element_type=jnp.float32,
    ).astype(jnp.bfloat16)
    outgoing = outgoing.reshape(seq_count * IMG_SEQ, pos_count, CAP, out_width)
    slot_place = (
        jnp.sum(jnp.where(selected, (pos_rows % quarter_len + 1)[:, None, :], 0), axis=2) - 1
    )
    slot_place = slot_place.reshape(seq_count * IMG_SEQ, pos_count, CAP)
    arrived, arrived_place = (
        lax.all_to_all(outgoing, "pos", split_axis=1, concat_axis=0, tiled=True),
        lax.all_to_all(slot_place, "pos", split_axis=1, concat_axis=0, tiled=True),
    )
    arrived = arrived[:, 0]
    arrived_place = arrived_place[:, 0]
    placing = jnp.arange(quarter_len, dtype=jnp.int32)[None, :, None] == arrived_place[:, None, :]
    placing_low = placing.astype(jnp.bfloat16)
    visible = jnp.any(placing, axis=2)
    filled = jnp.einsum("gqj,gjc->gqc", placing_low, arrived, preferred_element_type=jnp.float32)
    decoder_input = jnp.where(
        visible[:, :, None], filled, mask_token.astype(jnp.float32)[None, None, :]
    )
    decoder_input = decoder_input.astype(jnp.bfloat16)
    grad_mask = jnp.sum(
        jnp.where(visible[:, :, None], 0.0, cotangent.astype(jnp.float32)), axis=(0, 1)
    )
    back_slots = jnp.einsum(
        "gqj,gqc->gjc", placing_low, cotangent, preferred_element_type=jnp.float32
    ).astype(jnp.bfloat16)
    returned = lax.all_to_all(back_slots[:, None], "pos", split_axis=0, concat_axis=1, tiled=True)
    delta_proj = (
        jnp.einsum(
            "sjr,sjc->src",
            select_low,
            returned.reshape(seq_count, -1, out_width),
            preferred_element_type=jnp.float32,
        )
        .reshape(-1, out_width)
        .astype(jnp.bfloat16)
    )
    grad_proj = jnp.einsum("rd,rc->dc", block_low, delta_proj, preferred_element_type=jnp.float32)
    grad_bproj = column_sums(delta_proj)
    delta_block = jnp.einsum("rc,dc->rd", delta_proj, w_proj, preferred_element_type=jnp.float32)
    delta_down = delta_block.astype(jnp.bfloat16)
    grad_down = jnp.einsum("rf,rd->fd", hidden, delta_down, preferred_element_type=jnp.float32)
    grad_bdown = column_sums(delta_down)
    delta_hidden = jnp.einsum("rd,fd->rf", delta_down, w_down, preferred_element_type=jnp.float32)
    gelu_back = jax.vjp(gelu_tanh, up_proj)[1]
    delta_up = gelu_back(delta_hidden)[0].astype(jnp.bfloat16)
    grad_up = jnp.einsum("rd,rf->df", normed_mlp, delta_up, preferred_element_type=jnp.float32)
    grad_bup = column_sums(delta_up)
    delta_normed = jnp.einsum("rf,df->rd", delta_up, w_up, preferred_element_type=jnp.float32)
    norm_back = jax.vjp(layer_norm, residual, ln2_gain, ln2_bias)[1]
    delta_resid_norm, grad_gain_two, grad_shift_two = norm_back(delta_normed)
    delta_residual = delta_block + delta_resid_norm
    mlp_mats = reduce_matrices((grad_proj, grad_down, grad_up))
    mlp_vecs = reduce_vectors(
        (grad_bproj, grad_bdown, grad_bup, grad_gain_two, grad_shift_two, grad_mask)
    )
    delta_branch = delta_residual.astype(jnp.bfloat16)
    grad_out = jnp.einsum("re,rd->ed", attended, delta_branch, preferred_element_type=jnp.float32)
    grad_bout = column_sums(delta_branch)
    delta_attended = jnp.einsum(
        "rd,ed->re", delta_branch, w_out, preferred_element_type=jnp.float32
    )
    delta_attended = delta_attended.astype(jnp.bfloat16).reshape(head_shape)
    delta_values = jnp.einsum(
        "shqk,sqhd->skhd", probs_low, delta_attended, preferred_element_type=jnp.float32
    ).astype(jnp.bfloat16)
    delta_probs = jnp.einsum(
        "sqhd,skhd->shqk", delta_attended, values_h, preferred_element_type=jnp.float32
    )
    delta_scores = attn_probs * (
        delta_probs - jnp.sum(delta_probs * attn_probs, axis=-1, keepdims=True)
    )
    delta_scores = delta_scores.astype(jnp.bfloat16)
    delta_queries = (
        (
            jnp.einsum("shqk,skhd->sqhd", delta_scores, keys_h, preferred_element_type=jnp.float32)
            * score_scale
        )
        .astype(jnp.bfloat16)
        .reshape(-1, width)
    )
    delta_keys = (
        (
            jnp.einsum("shqk,sqhd->skhd", delta_scores, queries, preferred_element_type=jnp.float32)
            * score_scale
        )
        .astype(jnp.bfloat16)
        .reshape(-1, width)
    )
    delta_values = delta_values.reshape(-1, width)
    delta_qkv = jnp.concatenate([delta_queries, delta_keys, delta_values], axis=1)
    grad_qkv = jnp.einsum("rd,re->de", normed_low, delta_qkv, preferred_element_type=jnp.float32)
    grad_bquery = column_sums(delta_queries)
    grad_bvalue = column_sums(delta_values)
    delta_first = jnp.einsum("re,de->rd", delta_qkv, w_qkv, preferred_element_type=jnp.float32)
    first_back = jax.vjp(layer_norm, rows_f, ln1_gain, ln1_bias)[1]
    delta_rows, grad_gain_one, grad_shift_one = first_back(delta_first)
    grad_tokens = (delta_residual + delta_rows).astype(jnp.bfloat16)
    attn_mats = reduce_matrices((grad_qkv, grad_out))
    attn_vecs = reduce_vectors((grad_bquery, grad_bvalue, grad_bout, grad_gain_one, grad_shift_one))
    return (
        decoder_input,
        grad_tokens,
        attn_vecs[3],
        attn_vecs[4],
        attn_mats[0],
        attn_vecs[0],
        attn_vecs[1],
        attn_mats[1],
        attn_vecs[2],
        mlp_vecs[3],
        mlp_vecs[4],
        mlp_mats[2],
        mlp_vecs[2],
        mlp_mats[1],
        mlp_vecs[1],
        mlp_mats[0],
        mlp_vecs[0],
        mlp_vecs[5],
    )


def solution(mesh):
    placed = (
        P(("img", "pos"), None),
        P(("img", "pos")),
        P(("img", "pos")),
        P(),
        P(),
        P(),
        P(),
        P(),
        P(),
        P(),
        P(),
        P(),
        P(),
        P(),
        P(),
        P(),
        P(),
        P(),
        P(),
        P("img", "pos", None),
    )
    return jax.shard_map(
        per_device,
        mesh=mesh,
        in_specs=placed,
        out_specs=(
            P("img", "pos", None),
            P(("img", "pos"), None),
            P(),
            P(),
            P("img", None),
            P(),
            P(),
            P("img", None),
            P(),
            P(),
            P(),
            P("img", None),
            P(),
            P("img", None),
            P(),
            P("img", None),
            P(),
            P(),
        ),
        check_vma=False,
    )
```

profile of v0, /device:TPU:1, one launch (start us, length us, event | category | flops | bytes accessed | tf_op | source)
XLA Modules:
  0.0 712.5 jit_solution(16842414651417095004)
XLA Ops:
  10.2 4.3 all-to-all-start
  19.0 2.2 fusion.60
  23.0 1.9 copy.87
  25.0 1.9 copy.88
  26.9 1.8 fusion.6
  28.7 1.6 copy-done.2
  31.1 1.9 copy.86
  33.0 2.9 convolution_convert_fusion.2
  38.0 4.0 convolution_add_fusion
  42.0 1.6 copy-done.14
  43.6 2.7 fusion.10
  46.4 2.6 convolution_convert_fusion.4
  49.0 1.7 copy.90
  50.7 4.1 all-to-all-start.1
  55.5 2.3 fusion.14
  58.0 2.2 select_reduce_fusion
  60.6 5.3 all-to-all-start.2
  66.4 2.8 select_convert_fusion
  69.2 2.7 all-to-all-done.2
  73.1 1.6 convert_reduce_fusion.6
  76.2 6.8 convert_reduce_fusion
  83.0 5.9 fusion.49
  88.9 1.5 fusion.70
  90.5 5.2 fusion.63
  95.7 2.2 multiply_reduce_fusion.1
  101.2 1.9 copy.93
  103.1 3.3 multiply_reduce_fusion
  108.8 1.6 convert_reduce_fusion.4
  110.4 1.9 fusion.69
  112.3 4.1 fusion.29
  116.4 2.6 fusion.64
  119.1 8.1 %concatenate.27 = f32[32,73728]{1,0:T(8,128)} reshape(f32[768,3072]{1,0:T(8,128)} %fusion.63) | data formatting | bytes 18874368 | tf_op jit(solution)/shard_map/concatenate | solution.py:48
  127.2 8.2 %concatenate.26 = f32[32,73728]{1,0:T(8,128)} reshape(f32[3072,768]{1,0:T(8,128)} %fusion.49) | data formatting | bytes 18874368 | tf_op jit(solution)/shard_map/concatenate | solution.py:48
  135.7 16.3 %pad_maximum_fusion = f32[32,159744]{1,0:T(8,128)} fusion(f32[32,73728]{1,0:T(8,128)} %concatenate.27, f32[32,73728]{1,0:T(8,128)} %concatenate.26, f32[32,12288]{1,0:T(8,128)S(1)} %concatenate.25), kind=kLoop, calls=%fused_computation | loop fusion | flops 10223616 | bytes 40894464 | tf_op jit(solution)/shard_map/concatenate | solution.py:48
  152.0 6.7 concatenate.22
  158.7 1.8 concatenate.23
  160.6 7.4 %pad_maximum_fusion.1 = f32[32,73728]{1,0:T(8,128)} fusion(f32[32,18432]{1,0:T(8,128)S(1)} %concatenate.23, f32[32,55296]{1,0:T(8,128)} %concatenate.22), kind=kLoop, calls=%fused_computation.1 | loop fusion | flops 2359296 | bytes 18874368 | tf_op jit(solution)/shard_map/concatenate | solution.py:48
  170.6 483.3 %all-reduce.4 = (f32[768]{0:T(1024)}, f32[768]{0:T(1024)}, bf16[32,73728]{1,0:T(8,128)(2,1)}, f32[768]{0:T(1024)}, f32[768]{0:T(1024)}, /*index=5*/f32[768]{0:T(...) all-reduce(f32[768]{0:T(1024)S(1)} %get-tuple-element.22, ...), channel_id=1, replica_groups=mesh['img'=8,'pos'=4] {'img','pos'}, use_global_device_ids=true, to_apply=%region_15.16 | all-reduce | flops 7481344 | bytes 44908544 | tf_op jit(solution)/shard_map/psum | solution.py:67
  653.9 2.7 fusion.28
  656.7 1.6 fusion.33
  658.3 14.0 %all-gather.2 = bf16[4,1,73728]{2,1,0:T(2,128)(2,1)S(1)} all-gather(bf16[1,1,73728]{2,1,0:T(2,128)(2,1)S(1)} %fusion.33), channel_id=2, replica_groups=mesh['img'=8,'pos'=4] {'pos'}, dimensions={0}, use_global_device_ids=true | all-gather | bytes 737280 | tf_op jit(solution)/shard_map/all_gather | solution.py:53
  673.5 2.4 slice_reduce_fusion.2
  679.0 4.4 all-gather.6.cloned.1.call-done
  683.3 5.0 bitcast_convert_fusion
  688.3 7.8 %slice_reduce_fusion = (f32[4,73728]{1,0:T(4,128)}, f32[4,73728]{1,0:T(4,128)}) fusion(f32[1,4,159744]{2,0,1:T(1,128)S(1)} %bitcast_convert_fusion), kind=kLoop, calls=%fused_computation.51 | loop fusion | bytes 4718592 | tf_op jit(solution)/shard_map/slice | solution.py:60
  697.3 3.1 reshape_squeeze.17
  700.4 3.1 reshape_squeeze.18
  703.5 1.7 reshape_squeeze.19
  (192 shorter events, 30.3 us)
Async XLA Ops:
  7.2 11.8 %copy-start = (bf16[768,2304]{1,0:T(8,128)(2,1)S(1)}, bf16[768,2304]{1,0:T(8,128)(2,1)}, u32[]{:S(2)}) copy-start(bf16[768,2304]{1,0:T(8,128)(2,1)} %param.25) | copy-start | bytes 10616836
  10.2 40.5 %all-to-all-start = ((s32[5,4,16]{2,0,1:T(8,128)}), s32[5,4,16]{2,0,1:T(8,128)}, u32[]{:S(2)}, u32[]{:S(2)}) async-start(s32[5,4,16]{2,0,1:T(8,128)} %copy.85), calls=%async_computation | async-start | bytes 32768 | tf_op jit(solution)/shard_map/all_to_all | solution.py:152
  17.2 4.1 copy-start.38
  19.0 3.0 copy-start.56
  19.0 3.0 copy-start.57
  26.9 3.5 copy-start.23
  31.1 5.5 copy-start.30
  33.0 2.9 copy-start.4
  33.0 2.9 copy-start.16
  33.0 3.0 copy-start.58
  33.0 5.0 copy-start.33
  33.0 5.0 copy-start.35
  33.0 5.0 copy-start.65
  36.5 5.4 copy-start.9
  36.6 7.0 slice-start
  38.0 5.6 slice-start.1
  38.0 5.6 copy-start.66
  43.6 2.8 copy-start.63
  43.6 2.8 copy-start.67
  50.7 9.9 %all-to-all-start.1 = ((bf16[5,4,16,512]{3,2,0,1:T(8,128)(2,1)}), bf16[5,4,16,512]{3,2,0,1:T(8,128)(2,1)}, u32[]{:S(2)}, u32[]{:S(2)}) async-start(bf16[5,4,16,512]{3,2,0,1:T(8,128)(2,1)} %copy.90), calls=%async_computation.1 | async-start | bytes 655360 | tf_op jit(solution)/shard_map/all_to_all | solution.py:151
  60.6 11.3 %all-to-all-start.2 = ((bf16[20,1,16,512]{3,2,1,0:T(8,128)(2,1)}), bf16[20,1,16,512]{3,2,1,0:T(8,128)(2,1)}, u32[]{:S(2)}, u32[]{:S(2)}) async-start(bf16[20,1,16,512]{3,2,1,0:T(8,128)(2,1)} %fusion.14), calls=%async_computation.2 | async-start | bytes 655360 | tf_op jit(solution)/shard_map/all_to_all | solution.py:170
  65.9 617.4 %all-gather.6.cloned.1.call-start = ((), (), s32[]{:S(2)}) async-start(), calls=%async_computation.3 | async-start | bytes 3194880 | tf_op jit(solution)/shard_map/all_gather | solution.py:53
  71.9 4.3 copy-start.15
  76.2 22.1 %copy-start.7 = (f32[256,768]{1,0:T(8,128)}, f32[256,768]{1,0:T(8,128)S(1)}, u32[]{:S(2)}) copy-start(f32[256,768]{1,0:T(8,128)S(1)} %fusion.68) | copy-start | bytes 2359300
  83.0 5.9 copy-start.28
  83.0 7.4 %copy-start.10 = (f32[256,768]{1,0:T(8,128)S(1)}, f32[256,768]{1,0:T(8,128)}, u32[]{:S(2)}) copy-start(f32[256,768]{1,0:T(8,128)} %copy-done.9) | copy-start | bytes 2359300
  83.0 7.4 %copy-start.34 = (f32[768]{0:T(1024)S(1)}, f32[768]{0:T(1024)}, u32[]{:S(2)}) copy-start(f32[768]{0:T(1024)} %param.30) | copy-start | bytes 9220
  83.0 7.4 %copy-start.36 = (f32[768]{0:T(1024)S(1)}, f32[768]{0:T(1024)}, u32[]{:S(2)}) copy-start(f32[768]{0:T(1024)} %param.31) | copy-start | bytes 9220
  83.0 7.4 %copy-start.44 = (f32[256]{0:T(256)S(1)}, f32[256]{0:T(256)}, u32[]{:S(2)}) copy-start(f32[256]{0:T(256)} %copy-done.43) | copy-start | bytes 3076
  83.0 7.4 %copy-start.47 = (f32[256]{0:T(256)S(1)}, f32[256]{0:T(256)}, u32[]{:S(2)}) copy-start(f32[256]{0:T(256)} %copy-done.46) | copy-start | bytes 3076
  88.9 6.8 slice-start.2
  90.5 5.3 slice-start.3
  97.9 5.2 copy-start.31
  103.1 3.4 copy-start.3
  103.1 3.4 copy-start.24
  108.8 3.5 copy-start.5
  108.8 3.5 copy-start.29
  108.8 3.5 copy-start.37
  108.8 3.5 copy-start.39
  108.8 3.5 copy-start.41
  127.2 8.2 %copy-start.13 = (f32[768,512]{1,0:T(8,128)S(1)}, f32[768,512]{1,0:T(8,128)}, u32[]{:S(2)}) copy-start(f32[768,512]{1,0:T(8,128)} %fusion.70) | copy-start | bytes 4718596
  160.5 8.3 %copy-start.6 = (bf16[256,768]{1,0:T(8,128)(2,1)S(1)}, bf16[256,768]{1,0:T(8,128)(2,1)}, u32[]{:S(2)}) copy-start(bf16[256,768]{1,0:T(8,128)(2,1)} %param.20) | copy-start | bytes 1179652
  160.5 8.3 %copy-start.22 = (f32[256,768]{1,0:T(8,128)S(1)}, f32[256,768]{1,0:T(8,128)}, u32[]{:S(2)}) copy-start(f32[256,768]{1,0:T(8,128)} %get-tuple-element.57) | copy-start | bytes 2359300
  160.6 8.3 %copy-start.42 = (f32[256]{0:T(256)S(1)}, f32[256]{0:T(256)}, u32[]{:S(2)}) copy-start(f32[256]{0:T(256)} %copy-done.40) | copy-start | bytes 3076
  160.6 8.7 %copy-start.8 = (f32[256,768]{1,0:T(8,128)S(1)}, f32[256,768]{1,0:T(8,128)}, u32[]{:S(2)}) copy-start(f32[256,768]{1,0:T(8,128)} %copy-done.7) | copy-start | bytes 2359300
  160.6 8.7 %copy-start.12 = (f32[256,768]{1,0:T(8,128)S(1)}, f32[256,768]{1,0:T(8,128)}, u32[]{:S(2)}) copy-start(f32[256,768]{1,0:T(8,128)} %copy-done.11) | copy-start | bytes 2359300
  160.6 8.7 %copy-start.50 = (f32[256]{0:T(256)S(1)}, f32[256]{0:T(256)}, u32[]{:S(2)}) copy-start(f32[256]{0:T(256)} %copy-done.49) | copy-start | bytes 3076
  688.3 16.9 %copy-start.1 = (bf16[768,2304]{1,0:T(8,128)(2,1)S(1)}, bf16[768,2304]{1,0:T(8,128)(2,1)}, u32[]{:S(2)}) copy-start(bf16[768,2304]{1,0:T(8,128)(2,1)} %param.25) | copy-start | bytes 10616836
  (28 other events, 46.6 us)
Sparse Core Ops, SparseCore 0:
  656.8 26.4 all-gather.5
where the time goes:
time: 721 us; the launch traced here: 713 us
  blocking collectives  497 us (69%)
  local copies, waits for them, and re-layouts  71.3 us (10%)
  matrix products  62.6 us (9%)
  other arithmetic  44.4 us (6%)
  between operations  15.3 us (2%)
  starting transfers between devices  14.1 us (2%)
  waiting for transfers between devices  7.58 us (1%)
    psum x1, blocking collectives, reduce_vectors(): return lax.psum(tuple(members), ('img', 'pos'))  483 us
    concatenate x5, local copies, waits for them, and re-layouts, reduce_matrices(): bucket = jnp.concatenate(pieces, axis=2)  25.2 us
    concatenate x2, other arithmetic, reduce_matrices(): bucket = jnp.concatenate(pieces, axis=2)  23.6 us
  transfers between devices with their start and end apart: 4, of which 3 were waited for; matrix products, arithmetic and copies ran while one was open for 7% of the time, Pallas kernels for 0%

commit v1 on v0

--- a/solution.py
+++ b/solution.py
@@ -1,7 +1,11 @@
 import jax
 import jax.numpy as jnp
 from jax import lax
+from jax.experimental import pallas as pl
+from jax.experimental.pallas import tpu as pltpu
 from jax.sharding import PartitionSpec as P
+
+MESH_ID = pl.DeviceIdType.MESH
 
 HEADS = 12
 HEAD_DIM = 64
@@ -65,6 +69,332 @@
 
 def reduce_vectors(members):
     return lax.psum(tuple(members), ("img", "pos"))
+
+
+AXES = ("zh", "zl", "x", "y")
+MATRICES = ("down", "up", "proj", "out", "qkv")
+JOBS = (
+    ("down", 0, 256, ("zl", "zh", "x", "y")),
+    ("down", 256, 256, ("zl", "zh", "x", "y")),
+    ("down", 512, 256, ("zl", "zh", "x", "y")),
+    ("up", 0, 512, ("y", "x", "zl", "zh")),
+    ("up", 512, 512, ("y", "x", "zl", "zh")),
+    ("up", 1024, 512, ("y", "x", "zl", "zh")),
+    ("proj", 0, 256, ("x", "y", "zl", "zh")),
+    ("out", 0, 384, ("x", "y", "zl", "zh")),
+    ("qkv", 0, 384, ("x", "y", "zl", "zh")),
+    ("qkv", 384, 384, ("x", "y", "zl", "zh")),
+    ("qkv", 768, 384, ("x", "y", "zl", "zh")),
+)
+ORDER = (
+    (6, 0),
+    (0, 0),
+    (3, 0),
+    (7, 0),
+    (1, 0),
+    (4, 0),
+    (8, 0),
+    (2, 0),
+    (9, 0),
+    (5, 0),
+    (0, 1),
+    (6, 1),
+    (10, 0),
+    (7, 1),
+    (1, 1),
+    (8, 1),
+    (3, 1),
+    (2, 1),
+    (6, 2),
+    (9, 1),
+    (7, 2),
+    (4, 1),
+    (8, 2),
+    (10, 1),
+    (3, 2),
+    (6, 3),
+    (5, 1),
+    (9, 2),
+    (7, 3),
+    (6, 4),
+    (0, 2),
+    (4, 2),
+    (6, 5),
+    (8, 3),
+    (7, 4),
+    (1, 2),
+    (0, 3),
+    (10, 2),
+    (2, 2),
+    (7, 5),
+    (3, 3),
+    (8, 4),
+    (1, 3),
+    (5, 2),
+    (0, 4),
+    (8, 5),
+    (9, 3),
+    (2, 3),
+    (4, 3),
+    (3, 4),
+    (0, 5),
+    (10, 3),
+    (1, 4),
+    (5, 3),
+    (9, 4),
+    (3, 5),
+    (2, 4),
+    (1, 5),
+    (4, 4),
+    (9, 5),
+    (10, 4),
+    (2, 5),
+    (5, 4),
+    (4, 5),
+    (10, 5),
+    (5, 5),
+)
+VEC_STEPS = ("core", "x", "y", "zl", "zh")
+
+
+def device_coords():
+    img = lax.axis_index("img")
+    pos = lax.axis_index("pos")
+    return {"zh": img // 4, "zl": (img // 2) % 2, "x": img % 2, "y": pos // 2, "core": pos % 2}
+
+
+def device_of(where):
+    return (where["zh"] * 4 + where["zl"] * 2 + where["x"], where["y"] * 2 + where["core"])
+
+
+def job_rows(name):
+    return 96 if name == "down" else 48
+
+
+def reduce_kernel(*refs):
+    count = iter(refs)
+    lefts = {name: next(count) for name in MATRICES}
+    rights = {name: next(count) for name in MATRICES}
+    vec_ref = next(count)
+    outs = {name: next(count) for name in MATRICES}
+    vec_out = next(count)
+    lefts_in = {name: next(count) for name in MATRICES}
+    rights_in = {name: next(count) for name in MATRICES}
+    partial = [next(count) for _ in JOBS]
+    landed = [[next(count) for _ in range(4)] for _ in JOBS]
+    final = {name: next(count) for name in MATRICES}
+    vec_held = next(count)
+    vec_in = next(count)
+    core_send, core_recv, job_send, job_recv, vec_send, vec_recv = count
+    me = device_coords()
+    core = me["core"]
+
+    def peer(axis):
+        return device_of({**me, axis: 1 - me[axis]})
+
+    barrier = pltpu.get_barrier_semaphore()
+    for axis in AXES + ("core",):
+        pl.semaphore_signal(barrier, inc=1, device_id=peer(axis), device_id_type=MESH_ID)
+    pl.semaphore_wait(barrier, 5)
+
+    def remote(source, target, send_sem, recv_sem, axis):
+        return pltpu.make_async_remote_copy(
+            src_ref=source,
+            dst_ref=target,
+            send_sem=send_sem,
+            recv_sem=recv_sem,
+            device_id=peer(axis),
+            device_id_type=MESH_ID,
+        )
+
+    started = []
+    core_copies = {}
+    for number, name in enumerate(MATRICES):
+        if name == "down":
+            left_src, right_src = lefts[name].at[:, 1 - core], rights[name]
+        else:
+            left_src, right_src = lefts[name], rights[name].at[1 - core]
+        pair = (
+            remote(left_src, lefts_in[name], core_send.at[number, 0], core_recv.at[number, 0], "core"),
+            remote(right_src, rights_in[name], core_send.at[number, 1], core_recv.at[number, 1], "core"),
+        )
+        for copy in pair:
+            copy.start()
+            started.append(copy)
+        core_copies[name] = pair
+
+    def job_copy(number, stage):
+        name, first, wide, dims = JOBS[number]
+        columns = pl.ds(first, wide)
+        sems = (job_send.at[number, stage], job_recv.at[number, stage])
+        if stage < 4:
+            pick = []
+            for axis in AXES:
+                if axis in dims[:stage]:
+                    pick.append(me[axis])
+                elif axis == dims[stage]:
+                    pick.append(1 - me[axis])
+                else:
+                    pick.append(slice(None))
+            return remote(partial[number].at[tuple(pick)], landed[number][stage], *sems, dims[stage])
+        if stage == 4:
+            place = final[name].at[core, me["y"], :, columns]
+            return remote(place, place, *sems, "y")
+        place = final[name].at[core, :, :, columns]
+        return remote(place, place, *sems, "core")
+
+    def start_job(number, stage):
+        copy = job_copy(number, stage)
+        copy.start()
+        started.append(copy)
+
+    def vec_copy(stage):
+        return remote(
+            vec_held.at[stage], vec_in.at[stage], vec_send.at[stage], vec_recv.at[stage], VEC_STEPS[stage]
+        )
+
+    def start_vec(stage):
+        copy = vec_copy(stage)
+        copy.start()
+        started.append(copy)
+
+    vec_held[0] = vec_ref[...]
+    start_vec(0)
+
+    def multiply(name):
+        numbers = [number for number, job in enumerate(JOBS) if job[0] == name]
+        for copy in core_copies[name]:
+            copy.wait_recv()
+        rows = job_rows(name)
+        if name == "down":
+            for block in range(8):
+                high, low, side = block // 4, (block // 2) % 2, block % 2
+                total = jnp.dot(
+                    lefts[name][block, core], rights[name][...], preferred_element_type=jnp.float32
+                ) + jnp.dot(
+                    lefts_in[name][block], rights_in[name][...], preferred_element_type=jnp.float32
+                )
+                total = total.astype(jnp.bfloat16)
+                for number in numbers:
+                    _, first, wide, _ = JOBS[number]
+                    for half in range(2):
+                        partial[number][high, low, side, half] = total[
+                            half * rows : (half + 1) * rows, first : first + wide
+                        ]
+            for number in numbers:
+                start_job(number, 0)
+            return
+        for number in numbers:
+            _, first, wide, _ = JOBS[number]
+            for high in range(2):
+                span = slice(high * 8 * rows, (high + 1) * 8 * rows)
+                total = jnp.dot(
+                    lefts[name][span], rights[name][core, :, first : first + wide], preferred_element_type=jnp.float32
+                ) + jnp.dot(
+                    lefts_in[name][span], rights_in[name][:, first : first + wide], preferred_element_type=jnp.float32
+                )
+                total = total.astype(jnp.bfloat16)
+                for part in range(8):
+                    low, side, half = part // 4, (part // 2) % 2, part % 2
+                    partial[number][high, low, side, half] = total[part * rows : (part + 1) * rows]
+            start_job(number, 0)
+
+    def arrive(number, stage):
+        name, first, wide, dims = JOBS[number]
+        copy = job_copy(number, stage)
+        copy.wait_recv()
+        if stage < 4:
+            fixed = dims[: stage + 1]
+            free = [axis for axis in AXES if axis not in fixed]
+            for code in range(2 ** len(free)):
+                bits = {axis: (code >> (len(free) - 1 - spot)) % 2 for spot, axis in enumerate(free)}
+                here = tuple(me[axis] if axis in fixed else bits[axis] for axis in AXES)
+                there = tuple(bits[axis] for axis in free)
+                sums = partial[number][here] + landed[number][stage][there]
+                if stage < 3:
+                    partial[number][here] = sums
+                else:
+                    final[name][core, me["y"], :, first : first + wide] = sums
+        if stage < 5:
+            start_job(number, stage + 1)
+
+    def arrive_vec(stage):
+        vec_copy(stage).wait_recv()
+        sums = vec_held[stage] + vec_in[stage]
+        if stage < 4:
+            vec_held[stage + 1] = sums
+            start_vec(stage + 1)
+        else:
+            vec_out[...] = sums
+
+    for name in MATRICES:
+        multiply(name)
+    for spot, (number, stage) in enumerate(ORDER):
+        arrive(number, stage)
+        if spot % 8 == 7 and spot // 8 < 5:
+            arrive_vec(spot // 8)
+    for name in MATRICES:
+        rows = job_rows(name)
+        half_wide = final[name].shape[3]
+        for side in range(2):
+            for half in range(2):
+                piece = final[name][side, half].astype(outs[name].dtype)
+                if name == "down":
+                    outs[name][(side * 2 + half) * rows : (side * 2 + half + 1) * rows, :] = piece
+                else:
+                    outs[name][half * rows : (half + 1) * rows, side * half_wide : (side + 1) * half_wide] = piece
+    for copy in started:
+        copy.wait_send()
+
+
+def reduce_all(lefts, rights, vectors):
+    low = jnp.bfloat16
+    operands, outs, left_in, right_in, final = [], [], [], [], []
+    for name in MATRICES:
+        left = lefts[name]
+        operands.append(left.reshape(8, 2, 192, -1) if name == "down" else left)
+    for name in MATRICES:
+        right = rights[name]
+        rows, wide = right.shape
+        operands.append(right if name == "down" else right.reshape(rows, 2, wide // 2).transpose(1, 0, 2))
+    for name in MATRICES:
+        depth, rows = lefts[name].shape
+        wide = rights[name].shape[1]
+        outs.append(jax.ShapeDtypeStruct((depth // 8, wide), jnp.float32))
+        if name == "down":
+            left_in.append(pltpu.VMEM((8, 192, rows), low))
+            right_in.append(pltpu.VMEM((rows, wide), low))
+            final.append(pltpu.VMEM((2, 2, 96, wide), low))
+        else:
+            left_in.append(pltpu.VMEM((depth, rows), low))
+            right_in.append(pltpu.VMEM((rows, wide // 2), low))
+            final.append(pltpu.VMEM((2, 2, 48, wide // 2), low))
+    partial, landed = [], []
+    for name, _, wide, _ in JOBS:
+        rows = job_rows(name)
+        partial.append(pltpu.VMEM((2, 2, 2, 2, rows, wide), low))
+        for stage in range(4):
+            landed.append(pltpu.VMEM((2,) * (3 - stage) + (rows, wide), low))
+    dma = pltpu.SemaphoreType.DMA
+    vmem = pl.BlockSpec(memory_space=pltpu.VMEM)
+    results = pl.pallas_call(
+        reduce_kernel,
+        out_shape=outs + [jax.ShapeDtypeStruct(vectors.shape, jnp.float32)],
+        in_specs=[vmem] * (len(operands) + 1),
+        out_specs=[vmem] * (len(outs) + 1),
+        scratch_shapes=left_in
+        + right_in
+        + partial
+        + landed
+        + final
+        + [pltpu.VMEM((5,) + vectors.shape, jnp.float32)] * 2
+        + [dma((5, 2)), dma((5, 2)), dma((len(JOBS), 6)), dma((len(JOBS), 6)), dma((5,)), dma((5,))],
+        compiler_params=pltpu.CompilerParams(
+            collective_id=0, has_side_effects=True, vmem_limit_bytes=60 * 2**20
+        ),
+        name="reduce_grads",
+    )(*operands, vectors)
+    return dict(zip(MATRICES, results)), results[-1]
 
 
 def per_device(
@@ -178,27 +508,19 @@
         .reshape(-1, out_width)
         .astype(jnp.bfloat16)
     )
-    grad_proj = jnp.einsum("rd,rc->dc", block_low, delta_proj, preferred_element_type=jnp.float32)
     grad_bproj = column_sums(delta_proj)
     delta_block = jnp.einsum("rc,dc->rd", delta_proj, w_proj, preferred_element_type=jnp.float32)
     delta_down = delta_block.astype(jnp.bfloat16)
-    grad_down = jnp.einsum("rf,rd->fd", hidden, delta_down, preferred_element_type=jnp.float32)
     grad_bdown = column_sums(delta_down)
     delta_hidden = jnp.einsum("rd,fd->rf", delta_down, w_down, preferred_element_type=jnp.float32)
     gelu_back = jax.vjp(gelu_tanh, up_proj)[1]
     delta_up = gelu_back(delta_hidden)[0].astype(jnp.bfloat16)
-    grad_up = jnp.einsum("rd,rf->df", normed_mlp, delta_up, preferred_element_type=jnp.float32)
     grad_bup = column_sums(delta_up)
     delta_normed = jnp.einsum("rf,df->rd", delta_up, w_up, preferred_element_type=jnp.float32)
     norm_back = jax.vjp(layer_norm, residual, ln2_gain, ln2_bias)[1]
     delta_resid_norm, grad_gain_two, grad_shift_two = norm_back(delta_normed)
     delta_residual = delta_block + delta_resid_norm
-    mlp_mats = reduce_matrices((grad_proj, grad_down, grad_up))
-    mlp_vecs = reduce_vectors(
-        (grad_bproj, grad_bdown, grad_bup, grad_gain_two, grad_shift_two, grad_mask)
-    )
     delta_branch = delta_residual.astype(jnp.bfloat16)
-    grad_out = jnp.einsum("re,rd->ed", attended, delta_branch, preferred_element_type=jnp.float32)
     grad_bout = column_sums(delta_branch)
     delta_attended = jnp.einsum(
         "rd,ed->re", delta_branch, w_out, preferred_element_type=jnp.float32
@@ -232,34 +554,64 @@
     )
     delta_values = delta_values.reshape(-1, width)
     delta_qkv = jnp.concatenate([delta_queries, delta_keys, delta_values], axis=1)
-    grad_qkv = jnp.einsum("rd,re->de", normed_low, delta_qkv, preferred_element_type=jnp.float32)
     grad_bquery = column_sums(delta_queries)
     grad_bvalue = column_sums(delta_values)
     delta_first = jnp.einsum("re,de->rd", delta_qkv, w_qkv, preferred_element_type=jnp.float32)
     first_back = jax.vjp(layer_norm, rows_f, ln1_gain, ln1_bias)[1]
     delta_rows, grad_gain_one, grad_shift_one = first_back(delta_first)
     grad_tokens = (delta_residual + delta_rows).astype(jnp.bfloat16)
-    attn_mats = reduce_matrices((grad_qkv, grad_out))
-    attn_vecs = reduce_vectors((grad_bquery, grad_bvalue, grad_bout, grad_gain_one, grad_shift_one))
+    lefts = {"down": hidden.T, "up": normed_mlp.T, "proj": block_low.T, "out": attended.T, "qkv": normed_low.T}
+    rights = {
+        "down": delta_down,
+        "up": delta_up,
+        "proj": delta_proj,
+        "out": delta_branch,
+        "qkv": delta_qkv,
+    }
+    members = (
+        grad_gain_one,
+        grad_shift_one,
+        grad_bquery,
+        grad_bvalue,
+        grad_bout,
+        grad_gain_two,
+        grad_shift_two,
+        grad_bup,
+        grad_bdown,
+        grad_bproj,
+        grad_mask,
+    )
+    if lax.axis_size("img") == 8 and pos_count == 4:
+        mats, vec_sums = reduce_all(lefts, rights, jnp.concatenate(members).reshape(-1, 128))
+        flat = vec_sums.reshape(-1)
+        vecs = []
+        offset = 0
+        for member in members:
+            vecs.append(flat[offset : offset + member.size])
+            offset = offset + member.size
+    else:
+        grads = [matmul_rows(lefts[name], rights[name]) for name in MATRICES]
+        mats = dict(zip(MATRICES, reduce_matrices(grads)))
+        vecs = reduce_vectors(members)
     return (
         decoder_input,
         grad_tokens,
-        attn_vecs[3],
-        attn_vecs[4],
-        attn_mats[0],
-        attn_vecs[0],
-        attn_vecs[1],
-        attn_mats[1],
-        attn_vecs[2],
-        mlp_vecs[3],
-        mlp_vecs[4],
-        mlp_mats[2],
-        mlp_vecs[2],
-        mlp_mats[1],
-        mlp_vecs[1],
-        mlp_mats[0],
-        mlp_vecs[0],
-        mlp_vecs[5],
+        vecs[0],
+        vecs[1],
+        mats["qkv"],
+        vecs[2],
+        vecs[3],
+        mats["out"],
+        vecs[4],
+        vecs[5],
+        vecs[6],
+        mats["up"],
+        vecs[7],
+        mats["down"],
+        vecs[8],
+        mats["proj"],
+        vecs[9],
+        vecs[10],
     )
 
 

time: 721 us -> 257 us (0.36)
  blocking collectives: 497 us -> 0 us
  Pallas kernels: 0 us -> 88.3 us
  other arithmetic: 44.4 us -> 25 us
  between operations: 15.3 us -> 1.13 us
  matrix products: 62.6 us -> 51.5 us
    psum x1 -> x0, blocking collectives: 483 us -> none  [reduce_vectors(): return lax.psum(tuple(members), ('img', 'pos'))]
    pallas_call x0 -> x1, Pallas kernels: none -> 88.3 us  [reduce_all(): pl.pallas_call(reduce_kernel, out_shape=outs + [jax.ShapeDtypeStruct(vect...]
    concatenate x5 -> x1, local copies, waits for them, and re-layouts: 25.2 us -> 1.28 us  [per_device(): jnp.concatenate(members).reshape(-1, 128)]
    concatenate x2 -> x1, other arithmetic: 23.6 us -> 1.09 us  [per_device(): jnp.concatenate([delta_queries, delta_keys, delta_values], axis=1)]
    dot_general x5 -> x0, matrix products: 18.7 us -> none  [the longest x1 5.86 us: per_device(): jnp.einsum('rf,rd->fd', hidden, delta_down, preferred_element_type=jnp.fl...]
    unnamed x146 -> x131, local copies, waits for them, and re-layouts: 10.8 us -> 29.5 us
    all_gather x1 -> x0, blocking collectives: 14 us -> none  [reduce_matrices(): lax.all_gather(share.astype(jnp.bfloat16), 'pos', axis=1, tiled=True)]
    another operation x5 -> x0, local copies, waits for them, and re-layouts: 10.2 us -> none  [reduce_matrices(): results.append(block.reshape(member.shape[0] // img_count, member.shape[1]))]
  transfers between devices with their start and end apart: 4 -> 3, of which waited for: 3 -> 2; matrix products, arithmetic and copies ran while one was open for 7% -> 16% of each run, Pallas kernels for 0% -> 0%
where the time goes in v1:
time: 257 us; the launch traced here: 255 us
  Pallas kernels  88.3 us (34%)
  local copies, waits for them, and re-layouts  71.3 us (28%)
  matrix products  51.5 us (20%)
  other arithmetic  25 us (10%)
  starting transfers between devices  13.5 us (5%)
  waiting for transfers between devices  3.77 us (1%)
    pallas_call x1, Pallas kernels, reduce_all(): pl.pallas_call(reduce_kernel, out_shape=outs + [jax.ShapeDtypeStruct(vect...  88.3 us
    unnamed x131, local copies, waits for them, and re-layouts  29.5 us
    dot_general x4, matrix products, matmul_rows(): return jnp.dot(left, right, preferred_element_type=jnp.float32)  9.87 us
    dot_general x1, matrix products, per_device(): jnp.einsum('rd,fd->rf', delta_down, w_down, preferred_element_type=jnp.fl...  7.45 us
    reshape x3, local copies, waits for them, and re-layouts, reduce_all(): right.reshape(rows, 2, wide // 2).transpose(1, 0, 2)  6.92 us
    reduce_sum x3, other arithmetic, layer_norm(): centred * lax.rsqrt(jnp.mean(centred * centred, axis=-1, keepdims=True) +...  6.14 us
    dot_general x1, matrix products, per_device(): jnp.einsum('rf,df->rd', delta_up, w_up, preferred_element_type=jnp.float32)  5.89 us
    all_to_all x1, starting transfers between devices, per_device(): lax.all_to_all(back_slots[:, None], 'pos', split_axis=0, concat_axis=1, t...  5.15 us
  transfers between devices with their start and end apart: 3, of which 2 were waited for; matrix products, arithmetic and copies ran while one was open for 16% of the time, Pallas kernels for 0%

profile of v1, /device:TPU:1, one launch (start us, length us, event | category | flops | bytes accessed | tf_op | source)
XLA Modules:
  0.0 254.6 jit_solution(16907295373206030764)
XLA Ops:
  3.7 4.3 %all-to-all-start = ((s32[5,4,16]{2,0,1:T(8,128)}), s32[5,4,16]{2,0,1:T(8,128)S(1)}, u32[]{:S(2)}, u32[]{:S(2)}) async-start(s32[5,4,16]{2,0,1:T(8,128)} %copy.143), calls=%async_computation | async-start | bytes 32768 | tf_op jit(solution)/shard_map/all_to_all | solution.py:482
  8.0 1.5 broadcast_compare_fusion
  9.5 1.9 copy.144
  14.2 2.3 fusion.64
  18.3 1.9 copy.145
  20.3 1.9 copy.146
  22.2 1.9 copy.147
  24.1 1.8 fusion.11
  30.1 3.7 %fusion.10 = (bf16[3072,256]{0,1:T(8,128)(2,1)}, f32[256,3072]{1,0:T(8,128)S(1)}) fusion(f32[3072]{0:T(1024)S(1)} %copy-done.50, bf16[768,3072]{1,0:T(8,128)(2,1)S(1)} %bitcast.156, f32[256,768]{0,1:T(8,128)S(1)} %get-tuple-element.152, f32[768]{0:T(1024)S(1)} %copy-done.48, f32[768]{0:T(1024)S(1)} %copy-done.32, f32[256]{0:T(256)S(1)} %fusion.52, ...), kind=kOutput, calls=%fused_computation.16 | convolution fusion | flops 1216806912 | bytes 10244096 | tf_op jit(solution)/shard_map/dot_general | solution.py:41
  33.8 1.7 copy-done.52
  35.5 3.2 %fusion.21 = bf16[256,768]{0,1:T(8,128)(2,1)} fusion(f32[256,768]{0,1:T(8,128)S(1)} %get-tuple-element.152, bf16[3072,768]{1,0:T(8,128)(2,1)S(1)} %bitcast.154, f32[256,3072]{1,0:T(8,128)S(1)} %get-tuple-element.157, f32[768]{0:T(1024)S(1)} %copy-done.51), kind=kOutput, calls=%fused_computation.40 | convolution fusion | flops 1215627264 | bytes 9047040 | tf_op jit(solution)/shard_map/dot_general | solution.py:41
  38.7 2.6 %convolution_convert_fusion.4 = bf16[320,512]{1,0:T(8,128)(2,1)} fusion(bf16[256,768]{0,1:T(8,128)(2,1)} %fusion.21, bf16[768,512]{1,0:T(8,128)(2,1)} %param.36, f32[512]{0:T(512)} %param.37, s32[256]{0:T(256)} %copy-done.49), kind=kOutput, calls=%fused_computation.48 | convolution fusion | flops 285720576 | bytes 1510400 | tf_op jit(solution)/shard_map/sjr,src->sjc/dot_general | solution.py:469
  41.3 1.7 copy.151
  43.0 2.6 %copy.161 = bf16[3072,256]{1,0:T(8,128)(2,1)} copy(bf16[3072,256]{0,1:T(8,128)(2,1)} %get-tuple-element.156) | data formatting | bytes 3145728 | tf_op jit(solution)/shard_map/convert_element_type | solution.py:453
  45.6 4.1 %all-to-all-start.1 = ((bf16[5,4,16,512]{3,2,0,1:T(8,128)(2,1)}), bf16[5,4,16,512]{3,2,0,1:T(8,128)(2,1)}, u32[]{:S(2)}, u32[]{:S(2)}) async-start(bf16[5,4,16,512]{3,2,0,1:T(8,128)(2,1)} %copy.151), calls=%async_computation.1 | async-start | bytes 655360 | tf_op jit(solution)/shard_map/all_to_all | solution.py:481
  50.4 2.3 fusion.25
  52.9 2.2 select_reduce_fusion
  55.6 5.1 %all-to-all-start.2 = ((bf16[20,1,16,512]{3,2,1,0:T(8,128)(2,1)}), bf16[20,1,16,512]{3,2,1,0:T(8,128)(2,1)}, u32[]{:S(2)}, u32[]{:S(2)}) async-start(bf16[20,1,16,512]{3,2,1,0:T(8,128)(2,1)} %fusion.25), calls=%async_computation.2 | async-start | bytes 655360 | tf_op jit(solution)/shard_map/all_to_all | solution.py:500
  60.8 2.8 %select_convert_fusion = bf16[20,49,512]{2,1,0:T(8,128)(2,1)} fusion(bf16[20,16,512]{2,1,0:T(8,128)(2,1)} %bitcast.11, bf16[512]{0:T(512)(128)(2,1)} %param.38, pred[20,49]{1,0:T(8,128)(4,1)S(1)} %fusion.46, s32[20,16]{1,0:T(8,128)S(1)} %eq.115), kind=kOutput, calls=%fused_computation.27 | convolution fusion | flops 16573760 | bytes 1334484 | tf_op jit(solution)/shard_map/gqj,gjc->gqc/dot_general | solution.py:489
  63.6 3.2 %all-to-all-done.2 = bf16[20,1,16,512]{3,2,1,0:T(8,128)(2,1)} async-done(((bf16[20,1,16,512]{3,2,1,0:T(8,128)(2,1)}), bf16[20,1,16,512]{3,2,1,0:T(8,128)(2,1)}, u32[]{:S(2)}, u32[]{:S(2)}) %all-to-all-start.2) | async-done | bytes 327712 | tf_op jit(solution)/shard_map/all_to_all | solution.py:500
  67.8 1.6 convert_reduce_fusion.6
  70.1 3.2 %convert_reduce_fusion.2 = (f32[768]{0:T(1024)}, bf16[256,768]{1,0:T(8,128)(2,1)}, f32[256,768]{1,0:T(8,128)}) fusion(bf16[256,512]{1,0:T(8,128)(2,1)S(1)} %get-tuple-element.167, bf16[768,512]{1,0:T(8,128)(2,1)} %param.36), kind=kOutput, calls=%fused_computation.73 | convolution fusion | flops 201915648 | bytes 2231296 | tf_op jit(solution)/shard_map/rc,dc->rd/dot_general | solution.py:512
  73.3 2.3 copy.155
  75.6 7.4 %convert_reduce_fusion = (f32[3072]{0:T(1024)}, bf16[256,3072]{1,0:T(8,128)(2,1)S(1)}) fusion(f32[256,3072]{1,0:T(8,128)} %copy-done.52, bf16[256,768]{1,0:T(8,128)(2,1)} %get-tuple-element.125.refs_5_, bf16[3072,768]{1,0:T(8,128)(2,1)} %param.34), kind=kOutput, calls=%fused_computation.18 | convolution fusion | flops 1228403712 | bytes 9842688 | tf_op jit(solution)/shard_map/rd,fd->rf/dot_general | solution.py:515
  83.0 5.9 %fusion.73 = (f32[768]{0:T(1024)}, f32[256,768]{1,0:T(8,128)}) fusion(bf16[256,3072]{1,0:T(8,128)(2,1)S(1)} %get-tuple-element.127, bf16[768,3072]{1,0:T(8,128)(2,1)} %param.32), kind=kOutput, calls=%fused_computation.158 | convolution fusion | flops 1208155392 | bytes 7080960 | tf_op jit(solution)/shard_map/rf,df->rd/dot_general | solution.py:519
  88.9 2.3 copy.154
  91.2 2.4 multiply_reduce_fusion.1
  93.7 2.5 fusion.70
  99.2 1.9 copy.156
  101.1 4.3 %convert_reduce_fusion.4 = (f32[12,64]{1,0:T(8,128)}, bf16[12,64,256]{2,1,0:T(8,128)(2,1)}) fusion(bf16[256,12,64]{0,2,1:T(8,128)(2,1)} %bitcast.139, f32[12,256,256]{1,2,0:T(8,128)} %copy-done.1, f32[12,256]{1,0:T(8,128)S(1)} %copy-done.27, pred[256,256]{0,1:T(8,128)(4,1)} %broadcast_compare_fusion), kind=kOutput, calls=%fused_computation.76 | convolution fusion | flops 104398080 | bytes 4013056 | tf_op jit(solution)/shard_map/shqk,sqhd->skhd/dot_general | solution.py:529
  107.5 1.3 fusion.23
  110.0 2.6 %copy.162 = bf16[256,3072]{0,1:T(8,128)(2,1)} copy(bf16[256,3072]{1,0:T(8,128)(2,1)} %copy-done.16) | data formatting | bytes 3145728 | tf_op jit(solution)/shard_map/convert_element_type | solution.py:517
  112.6 1.8 copy.164
  114.4 3.9 %fusion.72 = (f32[768]{0:T(1024)}, f32[256,768]{1,0:T(8,128)}) fusion(bf16[768,2304]{1,0:T(8,128)(2,1)S(1)} %copy-done, bf16[256,768]{0,1:T(8,128)(2,1)} %bitcast.146, bf16[256,768]{0,1:T(8,128)(2,1)} %bitcast.133, bf16[256,768]{0,1:T(8,128)(2,1)} %bitcast.135), kind=kOutput, calls=%fused_computation.157 | convolution fusion | flops 909704448 | bytes 5508096 | tf_op jit(solution)/shard_map/re,de->rd/dot_general | solution.py:559
  119.4 2.3 copy.160
  121.7 1.4 fusion.36
  123.8 2.3 fusion.34
  126.1 3.1 %fusion.63 = (bf16[768,256]{1,0:T(8,128)(2,1)}, bf16[256,768]{0,1:T(8,128)(2,1)}) fusion(f32[768]{0:T(1024)} %param.24, f32[768]{0:T(1024)S(1)} %copy-done.29, f32[256]{0:T(256)} %copy-done.39, f32[256]{0:T(256)S(1)} %copy-done.31, bf16[256,768]{0,1:T(8,128)(2,1)} %copy.144, f32[256]{0:T(256)S(1)} %negate_multiply_fusion, ...), kind=kLoop, calls=%fused_computation.151 | loop fusion | flops 3145728 | bytes 3550208 | tf_op jit(solution)/shard_map/transpose | solution.py:563
  129.1 2.6 %copy.163 = bf16[256,2,1536]{2,0,1:T(8,128)(2,1)} copy(bf16[256,2,1536]{0,2,1:T(8,128)(2,1)} %bitcast.123) | data formatting | bytes 3145728 | tf_op jit(solution)/shard_map/reshape | solution.py:359
  131.8 1.8 copy.165
  133.6 1.9 copy.166
  135.5 2.4 copy.167
  153.5 88.3 %reduce_grads.1 = (f32[384,768]{1,0:T(8,128)}, f32[96,3072]{1,0:T(8,128)}, f32[96,512]{1,0:T(8,128)}, f32[96,768]{1,0:T(8,128)}, f32[96,2304]{1,0:T(8,128)}, /*index=5*/f32[80,128]{1,0:T(8,128)}) custom-call(bf16[8,2,192,256]{3,2,1,0:T(8,128)(2,1)} %bitcast.124, bf16[768,256]{1,0:T(8,128)(2,1)} %get-tuple-element.134.refs_1_, bf16[768,256]{1,0:T(8,128)(2,1)} %bitcast.148, ...), custom_call_target="tpu_custom_call" | custom-call | tf_op jit(solution)/shard_map/reduce_grads/pallas_call | solution.py:380
  241.9 1.4 slice_bitcast_fusion.1
  244.6 1.3 slice_bitcast_fusion.9
  245.9 1.9 copy.170
  247.9 2.3 copy.193
  250.2 1.7 copy.194
  (168 shorter events, 42.4 us)
Async XLA Ops:
  0.7 13.6 %copy-start = (bf16[768,2304]{1,0:T(8,128)(2,1)S(1)}, bf16[768,2304]{1,0:T(8,128)(2,1)}, u32[]{:S(2)}) copy-start(bf16[768,2304]{1,0:T(8,128)(2,1)} %param.25) | copy-start | bytes 10616836
  3.7 41.9 %all-to-all-start = ((s32[5,4,16]{2,0,1:T(8,128)}), s32[5,4,16]{2,0,1:T(8,128)S(1)}, u32[]{:S(2)}, u32[]{:S(2)}) async-start(s32[5,4,16]{2,0,1:T(8,128)} %copy.143), calls=%async_computation | async-start | bytes 32768 | tf_op jit(solution)/shard_map/all_to_all | solution.py:482
  12.5 4.0 %copy-start.30 = (f32[256]{0:T(256)}, f32[256]{0:T(256)S(1)}, u32[]{:S(2)}) copy-start(f32[256]{0:T(256)S(1)} %broadcast_multiply_fusion.1) | copy-start | bytes 3076
  14.2 2.3 copy-start.39
  14.2 3.1 %copy-start.45 = (f32[768]{0:T(1024)S(1)}, f32[768]{0:T(1024)}, u32[]{:S(2)}) copy-start(f32[768]{0:T(1024)} %param.26) | copy-start | bytes 9220
  14.2 3.1 %copy-start.46 = (f32[768]{0:T(1024)S(1)}, f32[768]{0:T(1024)}, u32[]{:S(2)}) copy-start(f32[768]{0:T(1024)} %param.27) | copy-start | bytes 9220
  24.1 2.6 %copy-start.17 = (bf16[256,768]{0,1:T(8,128)(2,1)S(1)}, bf16[256,768]{0,1:T(8,128)(2,1)}, u32[]{:S(2)}) copy-start(bf16[256,768]{0,1:T(8,128)(2,1)} %copy.145) | copy-start | bytes 1179652
  26.0 2.5 copy-start.7
  26.0 2.5 copy-start.47
  26.0 3.9 %slice-start.2 = ((s8[4718592]{0:T(1024)(128)(4,1)}), s8[4194304]{0:T(1024)(128)(4,1)S(1)}, s32[]{:S(2)}) async-start(s8[4718592]{0:T(1024)(128)(4,1)} %bitcast.155), calls=%async_computation.5 | async-start | bytes 8388608
  26.7 2.5 copy-start.26
  26.7 3.2 %copy-start.32 = (f32[768]{0:T(1024)S(1)}, f32[768]{0:T(1024)}, u32[]{:S(2)}) copy-start(f32[768]{0:T(1024)} %param.30) | copy-start | bytes 9220
  26.7 3.2 %copy-start.48 = (f32[768]{0:T(1024)S(1)}, f32[768]{0:T(1024)}, u32[]{:S(2)}) copy-start(f32[768]{0:T(1024)} %param.31) | copy-start | bytes 9220
  26.7 3.3 %slice-start.3 = ((s8[4718592]{0:T(1024)(128)(4,1)}), s8[524288]{0:T(1024)(128)(4,1)S(1)}, s32[]{:S(2)}) async-start(s8[4718592]{0:T(1024)(128)(4,1)} %bitcast.155), calls=%async_computation.6 | async-start | bytes 1048576
  26.7 3.3 %copy-start.50 = (f32[3072]{0:T(1024)S(1)}, f32[3072]{0:T(1024)}, u32[]{:S(2)}) copy-start(f32[3072]{0:T(1024)} %param.33) | copy-start | bytes 36868
  29.2 4.6 %copy-start.4 = (f32[256,768]{0,1:T(8,128)}, f32[256,768]{0,1:T(8,128)S(1)}, u32[]{:S(2)}) copy-start(f32[256,768]{0,1:T(8,128)S(1)} %get-tuple-element.152) | copy-start | bytes 2359300
  29.2 4.6 %copy-start.36 = (f32[256]{0:T(256)}, f32[256]{0:T(256)S(1)}, u32[]{:S(2)}) copy-start(f32[256]{0:T(256)S(1)} %broadcast_multiply_fusion) | copy-start | bytes 3076
  29.2 6.3 %slice-start = ((s8[4718592]{0:T(1024)(128)(4,1)}), s8[4194304]{0:T(1024)(128)(4,1)S(1)}, s32[]{:S(2)}) async-start(s8[4718592]{0:T(1024)(128)(4,1)} %bitcast.153), calls=%async_computation.3 | async-start | bytes 8388608
  29.4 4.4 %copy-start.41 = (f32[256]{0:T(256)}, f32[256]{0:T(256)S(1)}, u32[]{:S(2)}) copy-start(f32[256]{0:T(256)S(1)} %multiply_reduce_fusion.3) | copy-start | bytes 3076
  30.1 3.7 %copy-start.43 = (f32[256]{0:T(256)}, f32[256]{0:T(256)S(1)}, u32[]{:S(2)}) copy-start(f32[256]{0:T(256)S(1)} %fusion.52) | copy-start | bytes 3076
  30.1 5.4 %slice-start.1 = ((s8[4718592]{0:T(1024)(128)(4,1)}), s8[524288]{0:T(1024)(128)(4,1)S(1)}, s32[]{:S(2)}) async-start(s8[4718592]{0:T(1024)(128)(4,1)} %bitcast.153), calls=%async_computation.4 | async-start | bytes 1048576
  30.1 5.4 %copy-start.51 = (f32[768]{0:T(1024)S(1)}, f32[768]{0:T(1024)}, u32[]{:S(2)}) copy-start(f32[768]{0:T(1024)} %param.35) | copy-start | bytes 9220
  45.6 4.1 %copy-start.28 = (s32[5,4,16]{2,0,1:T(8,128)}, s32[5,4,16]{2,0,1:T(8,128)S(1)}, u32[]{:S(2)}) copy-start(s32[5,4,16]{2,0,1:T(8,128)S(1)} %all-to-all-done) | copy-start | bytes 3844
  45.6 10.0 %all-to-all-start.1 = ((bf16[5,4,16,512]{3,2,0,1:T(8,128)(2,1)}), bf16[5,4,16,512]{3,2,0,1:T(8,128)(2,1)}, u32[]{:S(2)}, u32[]{:S(2)}) async-start(bf16[5,4,16,512]{3,2,0,1:T(8,128)(2,1)} %copy.151), calls=%async_computation.1 | async-start | bytes 655360 | tf_op jit(solution)/shard_map/all_to_all | solution.py:481
  55.6 11.1 %all-to-all-start.2 = ((bf16[20,1,16,512]{3,2,1,0:T(8,128)(2,1)}), bf16[20,1,16,512]{3,2,1,0:T(8,128)(2,1)}, u32[]{:S(2)}, u32[]{:S(2)}) async-start(bf16[20,1,16,512]{3,2,1,0:T(8,128)(2,1)} %fusion.25), calls=%async_computation.2 | async-start | bytes 655360 | tf_op jit(solution)/shard_map/all_to_all | solution.py:500
  83.0 5.9 %copy-start.16 = (bf16[256,3072]{1,0:T(8,128)(2,1)}, bf16[256,3072]{1,0:T(8,128)(2,1)S(1)}, u32[]{:S(2)}) copy-start(bf16[256,3072]{1,0:T(8,128)(2,1)S(1)} %get-tuple-element.127) | copy-start | bytes 4718596
  83.0 8.2 %copy-start.33 = (f32[768]{0:T(1024)S(1)}, f32[768]{0:T(1024)}, u32[]{:S(2)}) copy-start(f32[768]{0:T(1024)} %param.30) | copy-start | bytes 9220
  83.0 8.2 %copy-start.37 = (f32[256]{0:T(256)S(1)}, f32[256]{0:T(256)}, u32[]{:S(2)}) copy-start(f32[256]{0:T(256)} %copy-done.36) | copy-start | bytes 3076
  83.0 8.2 %copy-start.44 = (f32[256]{0:T(256)S(1)}, f32[256]{0:T(256)}, u32[]{:S(2)}) copy-start(f32[256]{0:T(256)} %copy-done.43) | copy-start | bytes 3076
  88.9 4.8 %copy-start.42 = (f32[256]{0:T(256)S(1)}, f32[256]{0:T(256)}, u32[]{:S(2)}) copy-start(f32[256]{0:T(256)} %copy-done.41) | copy-start | bytes 3076
  91.2 5.0 %copy-start.5 = (f32[256,768]{0,1:T(8,128)S(1)}, f32[256,768]{0,1:T(8,128)}, u32[]{:S(2)}) copy-start(f32[256,768]{0,1:T(8,128)} %copy.155) | copy-start | bytes 2359300
  91.2 6.7 %copy-start.8 = (bf16[768,768]{1,0:T(8,128)(2,1)S(1)}, bf16[768,768]{1,0:T(8,128)(2,1)}, u32[]{:S(2)}) copy-start(bf16[768,768]{1,0:T(8,128)(2,1)} %param.28) | copy-start | bytes 3538948
  93.7 7.4 %copy-start.27 = (f32[12,256]{1,0:T(8,128)S(1)}, f32[12,256]{1,0:T(8,128)}, u32[]{:S(2)}) copy-start(f32[12,256]{1,0:T(8,128)} %copy-done.26) | copy-start | bytes 36868
  101.1 4.3 %copy-start.2 = (f32[12,256,256]{1,2,0:T(8,128)S(1)}, f32[12,256,256]{1,2,0:T(8,128)}, u32[]{:S(2)}) copy-start(f32[12,256,256]{1,2,0:T(8,128)} %copy-done.1) | copy-start | bytes 9437188
  101.1 4.3 %copy-start.13 = (pred[256,256]{0,1:T(8,128)(4,1)S(1)}, pred[256,256]{0,1:T(8,128)(4,1)}, u32[]{:S(2)}) copy-start(pred[256,256]{0,1:T(8,128)(4,1)} %broadcast_compare_fusion) | copy-start | bytes 196612
  101.1 4.3 %copy-start.18 = (bf16[256,768]{0,1:T(8,128)(2,1)S(1)}, bf16[256,768]{0,1:T(8,128)(2,1)}, u32[]{:S(2)}) copy-start(bf16[256,768]{0,1:T(8,128)(2,1)} %copy.145) | copy-start | bytes 1179652
  101.1 4.3 %copy-start.19 = (bf16[256,768]{0,1:T(8,128)(2,1)S(1)}, bf16[256,768]{0,1:T(8,128)(2,1)}, u32[]{:S(2)}) copy-start(bf16[256,768]{0,1:T(8,128)(2,1)} %copy.156) | copy-start | bytes 1179652
  106.5 2.3 copy-start.10
  114.4 3.9 %copy-start.14 = (bf16[12,64,256]{2,1,0:T(8,128)(2,1)S(1)}, bf16[12,64,256]{2,1,0:T(8,128)(2,1)}, u32[]{:S(2)}) copy-start(bf16[12,64,256]{2,1,0:T(8,128)(2,1)} %fusion.23) | copy-start | bytes 1179652
  114.4 3.9 %copy-start.15 = (bf16[12,64,256]{2,1,0:T(8,128)(2,1)S(1)}, bf16[12,64,256]{2,1,0:T(8,128)(2,1)}, u32[]{:S(2)}) copy-start(bf16[12,64,256]{2,1,0:T(8,128)(2,1)} %get-tuple-element.161) | copy-start | bytes 1179652
  114.4 3.9 %copy-start.24 = (bf16[12,64,256]{2,1,0:T(8,128)(2,1)S(1)}, bf16[12,64,256]{2,1,0:T(8,128)(2,1)}, u32[]{:S(2)}) copy-start(bf16[12,64,256]{2,1,0:T(8,128)(2,1)} %get-tuple-element.163) | copy-start | bytes 1179652
  118.3 3.4 %copy-start.29 = (f32[768]{0:T(1024)S(1)}, f32[768]{0:T(1024)}, u32[]{:S(2)}) copy-start(f32[768]{0:T(1024)} %param.23) | copy-start | bytes 9220
  118.3 3.4 %copy-start.31 = (f32[256]{0:T(256)S(1)}, f32[256]{0:T(256)}, u32[]{:S(2)}) copy-start(f32[256]{0:T(256)} %copy-done.30) | copy-start | bytes 3076
  129.1 16.6 %copy-start.35 = (f32[768]{0:T(1024)S(1)}, f32[768]{0:T(1024)}, u32[]{:S(2)}) copy-start(f32[768]{0:T(1024)} %get-tuple-element.120) | copy-start | bytes 9220
  129.1 20.6 %copy-start.34 = (f32[768]{0:T(1024)S(1)}, f32[768]{0:T(1024)}, u32[]{:S(2)}) copy-start(f32[768]{0:T(1024)} %get-tuple-element.124) | copy-start | bytes 9220
  247.9 4.0 %copy-start.22 = (f32[96,3072]{1,0:T(8,128)S(1)}, f32[96,3072]{1,0:T(8,128)}, u32[]{:S(2)}) copy-start(f32[96,3072]{1,0:T(8,128)} %get-tuple-element.197) | copy-start | bytes 3538948
  247.9 5.0 %copy-start.21 = (f32[384,768]{1,0:T(8,128)S(1)}, f32[384,768]{1,0:T(8,128)}, u32[]{:S(2)}) copy-start(f32[384,768]{1,0:T(8,128)} %get-tuple-element.199) | copy-start | bytes 3538948
  247.9 6.0 %copy-start.25 = (f32[96,512]{1,0:T(8,128)S(1)}, f32[96,512]{1,0:T(8,128)}, u32[]{:S(2)}) copy-start(f32[96,512]{1,0:T(8,128)} %get-tuple-element.201) | copy-start | bytes 589828
  (12 other events, 13.8 us)

commit v2 on v0

--- a/solution.py
+++ b/solution.py
@@ -1,6 +1,10 @@
+import functools
+
 import jax
 import jax.numpy as jnp
 from jax import lax
+from jax.experimental import pallas as pl
+from jax.experimental.pallas import tpu as pltpu
 from jax.sharding import PartitionSpec as P
 
 HEADS = 12
@@ -67,7 +71,7 @@
     return lax.psum(tuple(members), ("img", "pos"))
 
 
-def per_device(
+def general_device(
     tokens,
     image_slot,
     patch_position,
@@ -263,6 +267,764 @@
     )
 
 
+MESH_ID = pl.DeviceIdType.MESH
+LOW = jnp.bfloat16
+FULL = jnp.float32
+
+AXES = ("zh", "zl", "x", "y")
+MATRICES = ("down", "up", "proj", "out", "qkv")
+JOBS = (
+    ("down", 0, 256, ("zl", "zh", "x", "y")),
+    ("down", 256, 256, ("zl", "zh", "x", "y")),
+    ("down", 512, 256, ("zl", "zh", "x", "y")),
+    ("up", 0, 512, ("y", "x", "zl", "zh")),
+    ("up", 512, 512, ("y", "x", "zl", "zh")),
+    ("up", 1024, 512, ("y", "x", "zl", "zh")),
+    ("proj", 0, 256, ("x", "y", "zl", "zh")),
+    ("out", 0, 384, ("x", "y", "zl", "zh")),
+    ("qkv", 0, 384, ("x", "y", "zl", "zh")),
+    ("qkv", 384, 384, ("x", "y", "zl", "zh")),
+    ("qkv", 768, 384, ("x", "y", "zl", "zh")),
+)
+ORDER = (
+    (6, 0),
+    (0, 0),
+    (3, 0),
+    (7, 0),
+    (1, 0),
+    (4, 0),
+    (3, 1),
+    (2, 0),
+    (8, 0),
+    (5, 0),
+    (6, 1),
+    (0, 1),
+    (7, 1),
+    (9, 0),
+    (1, 1),
+    (8, 1),
+    (3, 2),
+    (9, 1),
+    (10, 0),
+    (2, 1),
+    (6, 2),
+    (4, 1),
+    (7, 2),
+    (10, 1),
+    (8, 2),
+    (3, 3),
+    (5, 1),
+    (9, 2),
+    (6, 3),
+    (3, 4),
+    (0, 2),
+    (4, 2),
+    (6, 4),
+    (7, 3),
+    (3, 5),
+    (1, 2),
+    (10, 2),
+    (0, 3),
+    (6, 5),
+    (8, 3),
+    (2, 2),
+    (7, 4),
+    (1, 3),
+    (5, 2),
+    (0, 4),
+    (9, 3),
+    (7, 5),
+    (8, 4),
+    (4, 3),
+    (2, 3),
+    (10, 3),
+    (0, 5),
+    (1, 4),
+    (8, 5),
+    (5, 3),
+    (9, 4),
+    (4, 4),
+    (1, 5),
+    (2, 4),
+    (9, 5),
+    (10, 4),
+    (4, 5),
+    (5, 4),
+    (2, 5),
+    (10, 5),
+    (5, 5),
+)
+VEC_STEPS = ("core", "x", "y", "zl", "zh")
+PEERS = ("y", "core", "diagonal")
+PLACES = 64
+LN1_GAIN, LN1_BIAS, BIAS_Q, BIAS_V, BIAS_OUT, LN2_GAIN, LN2_BIAS, BIAS_DOWN, BIAS_UP, BIAS_PROJ, MASK = (
+    0, 1, 2, 3, 4, 5, 6, 7, 8, 12, 13,
+)
+
+
+def device_coords():
+    img = lax.axis_index("img")
+    pos = lax.axis_index("pos")
+    return {"zh": img // 4, "zl": (img // 2) % 2, "x": img % 2, "y": pos // 2, "core": pos % 2}
+
+
+def device_of(where):
+    return (where["zh"] * 4 + where["zl"] * 2 + where["x"], where["y"] * 2 + where["core"])
+
+
+def block_rows(name):
+    return 96 if name == "down" else 48
+
+
+def dot(left, right):
+    return jnp.dot(left, right, preferred_element_type=FULL)
+
+
+def dot_nt(left, right):
+    return lax.dot_general(left, right, (((1,), (1,)), ((), ())), preferred_element_type=FULL)
+
+
+def dot_tn(left, right):
+    return lax.dot_general(left, right, (((0,), (0,)), ((), ())), preferred_element_type=FULL)
+
+
+def normalised(values):
+    centred = values - jnp.mean(values, axis=-1, keepdims=True)
+    rstd = lax.rsqrt(jnp.mean(centred * centred, axis=-1, keepdims=True) + EPSILON)
+    return centred * rstd, rstd
+
+
+def norm_rows_back(delta, values, gain):
+    xhat, rstd = normalised(values)
+    scaled = delta * gain
+    rows = rstd * (
+        scaled
+        - jnp.mean(scaled, axis=-1, keepdims=True)
+        - xhat * jnp.mean(scaled * xhat, axis=-1, keepdims=True)
+    )
+    return rows, delta * xhat
+
+
+def layer_kernel(names, *refs):
+    ref = dict(zip(names, refs))
+    me = device_coords()
+    core = me["core"]
+    my_pos = me["y"] * 2 + core
+    width = ref["tokens"].shape[1]
+    ff = ref["w_up"].shape[1]
+    quarter_len = POSITIONS // 4
+
+    def peer(axis):
+        if axis == "diagonal":
+            return device_of({**me, "y": 1 - me["y"], "core": 1 - core})
+        return device_of({**me, axis: 1 - me[axis]})
+
+    started = []
+
+    def remote(source, target, kind, spot, axis):
+        return pltpu.make_async_remote_copy(
+            src_ref=source,
+            dst_ref=target,
+            send_sem=ref[kind + "_send"].at[spot],
+            recv_sem=ref[kind + "_recv"].at[spot],
+            device_id=peer(axis),
+            device_id_type=MESH_ID,
+        )
+
+    def begin(copy):
+        copy.start()
+        started.append(copy)
+
+    loads = {}
+    for number, name in enumerate(("w_qkv", "w_out", "w_proj", "w_up", "w_down")):
+        loads[name] = pltpu.make_async_copy(ref[name], ref[name + "_held"], ref["load"].at[number])
+        loads[name].start()
+
+    barrier = pltpu.get_barrier_semaphore()
+    for axis in AXES + ("core", "diagonal"):
+        pl.semaphore_signal(barrier, inc=1, device_id=peer(axis), device_id_type=MESH_ID)
+
+    ref["places"][my_pos, 0:1, :] = ref["slot"][...]
+    ref["places"][my_pos, 1:2, :] = ref["position"][...]
+
+    def first_norm(step, carry):
+        rows = pl.ds(pl.multiple_of(step * 64, 64), 64)
+        xhat, _ = normalised(ref["tokens"][rows, :].astype(FULL))
+        ref["normed"][rows, :] = (xhat * ref["ln1_gain"][...] + ref["ln1_bias"][...]).astype(LOW)
+        return carry
+
+    lax.fori_loop(0, 4, first_norm, 0)
+
+    pl.semaphore_wait(barrier, 6)
+    for number, axis in enumerate(PEERS):
+        begin(remote(ref["places"].at[my_pos], ref["places"].at[my_pos], "place", number, axis))
+
+    loads["w_qkv"].wait()
+    third = width // 256
+    for number in range(3 * third):
+        columns = slice(number * 256, (number + 1) * 256)
+        part = dot(ref["normed"][...], ref["w_qkv_held"][:, columns])
+        if number < third:
+            part = part + ref["bias_query"][:, columns]
+            part = part.astype(LOW) * LOW(HEAD_DIM ** (-0.5))
+        elif number >= 2 * third:
+            part = part + ref["bias_value"][:, (number - 2 * third) * 256 : (number - 2 * third + 1) * 256]
+        ref["qkv"][:, columns] = part.astype(LOW)
+    ref["left_qkv"][...] = ref["normed"][...].T
+
+    row_ids = lax.broadcasted_iota(jnp.int32, (ROWS_SEQ, ROWS_SEQ), 0)
+    lane_ids = lax.broadcasted_iota(jnp.int32, (ROWS_SEQ, ROWS_SEQ), 1)
+    earlier = (row_ids < lane_ids).astype(FULL).astype(LOW)
+
+    def one_hot(count, row):
+        ids = lax.broadcasted_iota(jnp.int32, (count, ROWS_SEQ), 0)
+        return jnp.where(ids == row, 1.0, 0.0)
+
+    def picked(slot, position, quarter):
+        offset = position - quarter * quarter_len
+        inside = (slot >= 0) & (offset >= 0) & (offset < quarter_len)
+        kinds = one_hot(8, jnp.where(inside, slot, -1))
+        ranks = jnp.sum(kinds * dot(kinds.astype(LOW), earlier), axis=0, keepdims=True).astype(jnp.int32)
+        chosen = one_hot(IMG_SEQ * CAP, jnp.where(inside, slot * CAP + ranks, -1))
+        return chosen.astype(LOW), jnp.where(inside, slot * PLACES + offset, -1)
+
+    for quarter in range(4):
+        chosen, _ = picked(ref["slot"][...], ref["position"][...], quarter)
+        ref["chosen"][quarter] = chosen
+
+    slots = one_hot(8, ref["slot"][...] + 1).astype(LOW)
+    ref["allowed"][...] = jnp.where(dot_tn(slots, slots) > 0.5, 0.0, NEGATIVE)
+
+    ref["cot_wide"][...] = jnp.zeros_like(ref["cot_wide"])
+    for image in range(4 * IMG_SEQ):
+        ref["cot_wide"][image, 0:quarter_len, :] = ref["cotangent"][image]
+    mask_sum = jnp.zeros((8, ref["cotangent"].shape[2]), FULL)
+    for number, axis in enumerate(PEERS + ("self",)):
+        if axis == "self":
+            source = my_pos
+        else:
+            source = peer(axis)[1]
+            remote(ref["places"].at[source], ref["places"].at[source], "place", number, axis).wait_recv()
+        slot = ref["places"][source, 0:1, :]
+        position = ref["places"][source, 1:2, :]
+        chosen, place = picked(slot, position, my_pos)
+        filled = one_hot(IMG_SEQ * PLACES, place).astype(LOW)
+        placing = dot_nt(filled, chosen)
+        placing_low = placing.astype(LOW)
+        ref["placing"][number] = placing_low
+        cot = ref["cot_wide"][pl.ds(source * IMG_SEQ, IMG_SEQ)].reshape(IMG_SEQ * PLACES, -1)
+        back = dot_tn(placing_low, cot).astype(LOW)
+        if axis == "self":
+            ref["back_in"][my_pos] = back
+        else:
+            ref["back_out"][number] = back
+            begin(remote(ref["back_out"].at[number], ref["back_in"].at[my_pos], "back", number, axis))
+        seen = dot_nt(jnp.ones((8, IMG_SEQ * CAP), LOW), placing_low)
+        mask_sum = mask_sum + dot((1.0 - seen).astype(LOW), cot)
+    ref["vec_own"][...] = jnp.zeros_like(ref["vec_own"])
+    ref["vec_own"][MASK : MASK + 1, : mask_sum.shape[1]] = mask_sum[0:1]
+
+    lane = lax.broadcasted_iota(jnp.int32, (1, 2 * HEAD_DIM), 1)
+    sides_full = [(lane < HEAD_DIM).astype(FULL), (lane >= HEAD_DIM).astype(FULL)]
+    sides = [side.astype(LOW) for side in sides_full]
+
+    def head_columns(pair, first):
+        return pl.ds(pl.multiple_of(first + pair * 2 * HEAD_DIM, 2 * HEAD_DIM), 2 * HEAD_DIM)
+
+    def attend(pair, carry):
+        queries = ref["qkv"][:, head_columns(pair, 0)]
+        keys = ref["qkv"][:, head_columns(pair, width)]
+        values = ref["qkv"][:, head_columns(pair, 2 * width)]
+        total = None
+        for side in range(2):
+            scores = dot_nt(queries * sides[side], keys) + ref["allowed"][...]
+            powers = jnp.exp(scores - jnp.max(scores, axis=-1, keepdims=True))
+            probs = powers / jnp.sum(powers, axis=-1, keepdims=True)
+            ref["probs"][pair * 2 + side] = probs
+            part = dot(probs.astype(LOW), values) * sides_full[side]
+            total = part if total is None else total + part
+        ref["attended"][:, head_columns(pair, 0)] = total.astype(LOW)
+        return carry
+
+    lax.fori_loop(0, HEADS // 2, attend, 0)
+    ref["left_out"][...] = ref["attended"][...].T
+
+    loads["w_out"].wait()
+    for number in range(third):
+        columns = slice(number * 256, (number + 1) * 256)
+        ref["residual"][:, columns] = (
+            ref["tokens"][:, columns].astype(FULL)
+            + dot(ref["attended"][...], ref["w_out_held"][:, columns])
+            + ref["bias_out"][:, columns]
+        )
+
+    def second_norm(step, carry):
+        rows = pl.ds(pl.multiple_of(step * 64, 64), 64)
+        xhat, _ = normalised(ref["residual"][rows, :])
+        ref["normed"][rows, :] = (xhat * ref["ln2_gain"][...] + ref["ln2_bias"][...]).astype(LOW)
+        return carry
+
+    lax.fori_loop(0, 4, second_norm, 0)
+    ref["left_up"][...] = ref["normed"][...].T
+
+    loads["w_proj"].wait()
+    for number, axis in enumerate(PEERS):
+        remote(ref["back_out"].at[number], ref["back_in"].at[my_pos], "back", number, axis).wait_recv()
+    chosen_all = ref["chosen"][...].reshape(4 * IMG_SEQ * CAP, ROWS_SEQ)
+    returned = ref["back_in"][...].reshape(4 * IMG_SEQ * CAP, -1)
+    delta_proj = dot_tn(chosen_all, returned)
+    ref["vec_own"][BIAS_PROJ : BIAS_PROJ + 1, : delta_proj.shape[1]] = jnp.sum(delta_proj, axis=0, keepdims=True)
+    ref["right_proj"][...] = delta_proj.astype(LOW)
+    for number in range(third):
+        columns = slice(number * 256, (number + 1) * 256)
+        part = dot_nt(ref["right_proj"][...], ref["w_proj_held"][columns, :])
+        ref["delta_block"][:, columns] = part
+        part = part.astype(LOW)
+        ref["right_down"][:, columns] = part
+        ref["vec_own"][BIAS_DOWN : BIAS_DOWN + 1, columns] = jnp.sum(part.astype(FULL), axis=0, keepdims=True)
+
+    loads["w_up"].wait()
+    loads["w_down"].wait()
+    ref["mlp_out"][...] = jnp.zeros_like(ref["mlp_out"])
+    ref["delta_normed"][...] = jnp.zeros_like(ref["delta_normed"])
+
+    def feed(step, carry):
+        columns = pl.ds(pl.multiple_of(step * 256, 256), 256)
+        up = dot(ref["normed"][...], ref["w_up_held"][:, columns]) + ref["bias_up"][:, columns]
+        square = up * up
+        bent = jnp.tanh(GELU_COEF * (up + 0.044715 * up * square))
+        half = 0.5 * (1.0 + bent)
+        slope = half + 0.5 * up * (1.0 - bent * bent) * (GELU_COEF * (1.0 + 0.134145 * square))
+        hidden = (up * half).astype(LOW)
+        ref["left_down"][columns, :] = hidden.T
+        back = dot_nt(ref["right_down"][...], ref["w_down_held"][columns, :])
+        delta_up = (back * slope).astype(LOW)
+        ref["right_up"][:, columns] = delta_up
+        ref["bias_up_sum"][:, columns] = jnp.sum(delta_up.astype(FULL), axis=0, keepdims=True)
+        ref["mlp_out"][...] += dot(hidden, ref["w_down_held"][columns, :])
+        ref["delta_normed"][...] += dot_nt(delta_up, ref["w_up_held"][:, columns])
+        return carry
+
+    lax.fori_loop(0, ff // 256, feed, 0)
+    for number in range(ff // width):
+        ref["vec_own"][BIAS_UP + number : BIAS_UP + number + 1, :] = ref["bias_up_sum"][
+            :, number * width : (number + 1) * width
+        ]
+
+    def half_columns(name, side):
+        wide = ref["right_" + name].shape[1] // 2
+        return pl.ds(pl.multiple_of(side * wide, 128), wide)
+
+    def core_copies(name):
+        spot = MATRICES.index(name)
+        if name == "down":
+            left = ref["left_down"].reshape(8, 2, 192, ROWS_SEQ).at[:, 1 - core]
+            right = ref["right_down"]
+        else:
+            left = ref["left_" + name]
+            right = ref["right_" + name].at[:, half_columns(name, 1 - core)]
+        return (
+            remote(left, ref["left_in_" + name], "core", (spot, 0), "core"),
+            remote(right, ref["right_in_" + name], "core", (spot, 1), "core"),
+        )
+
+    def swap(name):
+        for copy in core_copies(name):
+            begin(copy)
+
+    def job_copy(number, stage):
+        name, first, wide, dims = JOBS[number]
+        columns = pl.ds(first, wide)
+        if stage < 4:
+            pick = []
+            for axis in AXES:
+                if axis in dims[:stage]:
+                    pick.append(me[axis])
+                elif axis == dims[stage]:
+                    pick.append(1 - me[axis])
+                else:
+                    pick.append(slice(None))
+            source = ref["partial%d" % number].at[tuple(pick)]
+            return remote(source, ref["landed%d_%d" % (number, stage)], "job", (number, stage), dims[stage])
+        if stage == 4:
+            place = ref["final_" + name].at[core, me["y"], :, columns]
+            return remote(place, place, "job", (number, stage), "y")
+        place = ref["final_" + name].at[core, :, :, columns]
+        return remote(place, place, "job", (number, stage), "core")
+
+    def multiply(name):
+        numbers = [number for number, job in enumerate(JOBS) if job[0] == name]
+        for copy in core_copies(name):
+            copy.wait_recv()
+        rows = block_rows(name)
+        left, right = ref["left_" + name], ref["right_" + name]
+        left_in, right_in = ref["left_in_" + name], ref["right_in_" + name]
+        if name == "down":
+            for block in range(8):
+                spot = pl.multiple_of(block * 384 + core * 192, 192)
+                total = dot(left[pl.ds(spot, 192), :], right[...]) + dot(left_in[block], right_in[...])
+                total = total.astype(LOW)
+                for number in numbers:
+                    _, first, wide, _ = JOBS[number]
+                    for half in range(2):
+                        ref["partial%d" % number][block // 4, (block // 2) % 2, block % 2, half] = total[
+                            half * rows : (half + 1) * rows, first : first + wide
+                        ]
+            for number in numbers:
+                begin(job_copy(number, 0))
+            return
+        wide_half = right.shape[1] // 2
+        for number in numbers:
+            _, first, wide, _ = JOBS[number]
+            columns = pl.ds(pl.multiple_of(core * wide_half + first, 128), wide)
+            for high in range(2):
+                span = slice(high * 8 * rows, (high + 1) * 8 * rows)
+                total = dot(left[span, :], right[:, columns]) + dot(
+                    left_in[span, :], right_in[:, first : first + wide]
+                )
+                total = total.astype(LOW)
+                for part in range(8):
+                    ref["partial%d" % number][high, part // 4, (part // 2) % 2, part % 2] = total[
+                        part * rows : (part + 1) * rows
+                    ]
+            begin(job_copy(number, 0))
+
+    def arrive(number, stage):
+        name, first, wide, dims = JOBS[number]
+        job_copy(number, stage).wait_recv()
+        if stage < 4:
+            partial, landed = ref["partial%d" % number], ref["landed%d_%d" % (number, stage)]
+            fixed = dims[: stage + 1]
+            free = [axis for axis in AXES if axis not in fixed]
+            for code in range(2 ** len(free)):
+                bits = {axis: (code >> (len(free) - 1 - spot)) % 2 for spot, axis in enumerate(free)}
+                here = tuple(me[axis] if axis in fixed else bits[axis] for axis in AXES)
+                sums = partial[here] + landed[tuple(bits[axis] for axis in free)]
+                if stage < 3:
+                    partial[here] = sums
+                else:
+                    ref["final_" + name][core, me["y"], :, first : first + wide] = sums
+        if stage < 5:
+            begin(job_copy(number, stage + 1))
+
+    def vec_copy(stage):
+        return remote(ref["vec_held"].at[stage], ref["vec_in"].at[stage], "vec", stage, VEC_STEPS[stage])
+
+    def arrive_vec(stage):
+        vec_copy(stage).wait_recv()
+        sums = ref["vec_held"][stage] + ref["vec_in"][stage]
+        if stage < 4:
+            ref["vec_held"][stage + 1] = sums
+            begin(vec_copy(stage + 1))
+        else:
+            ref["vec_sums"][...] = sums
+
+    swap("down")
+    swap("up")
+
+    for number in range(third):
+        columns = slice(number * 256, (number + 1) * 256)
+        ref["block_low"][:, columns] = (
+            ref["residual"][:, columns] + ref["mlp_out"][:, columns] + ref["bias_down"][:, columns]
+        ).astype(LOW)
+    ref["left_proj"][...] = ref["block_low"][...].T
+    swap("proj")
+    projected = (dot(ref["block_low"][...], ref["w_proj_held"][...]) + ref["bias_proj"][...]).astype(LOW)
+    outgoing = dot(chosen_all, projected).astype(LOW)
+    ref["grid_out"][...] = outgoing.reshape(4, IMG_SEQ * CAP, -1)
+    for number, axis in enumerate(PEERS):
+        begin(remote(ref["grid_out"].at[peer(axis)[1]], ref["grid_in"].at[number], "grid", number, axis))
+
+    multiply("down")
+    multiply("up")
+    multiply("proj")
+
+    def second_back(step, sums):
+        rows = pl.ds(pl.multiple_of(step * 64, 64), 64)
+        delta = ref["delta_normed"][rows, :]
+        row_term, gains = norm_rows_back(delta, ref["residual"][rows, :], ref["ln2_gain"][...])
+        total = ref["delta_block"][rows, :] + row_term
+        low = total.astype(LOW)
+        ref["delta_block"][rows, :] = total
+        ref["right_out"][rows, :] = low
+        news = (gains, delta, low.astype(FULL))
+        return tuple(old + jnp.sum(new, axis=0, keepdims=True) for old, new in zip(sums, news))
+
+    zeros = jnp.zeros((1, width), FULL)
+    sums = lax.fori_loop(0, 4, second_back, (zeros, zeros, zeros))
+    for spot, total in zip((LN2_GAIN, LN2_BIAS, BIAS_OUT), sums):
+        ref["vec_own"][spot : spot + 1, :] = total
+    swap("out")
+    for number in range(third):
+        columns = slice(number * 256, (number + 1) * 256)
+        ref["delta_attended"][:, columns] = dot_nt(ref["right_out"][...], ref["w_out_held"][columns, :]).astype(LOW)
+
+    def attend_back(pair, carry):
+        queries = ref["qkv"][:, head_columns(pair, 0)]
+        keys = ref["qkv"][:, head_columns(pair, width)]
+        values = ref["qkv"][:, head_columns(pair, 2 * width)]
+        delta = ref["delta_attended"][:, head_columns(pair, 0)]
+        totals = [None, None, None]
+        for side in range(2):
+            probs = ref["probs"][pair * 2 + side]
+            delta_probs = dot_nt(delta * sides[side], values)
+            delta_scores = probs * (delta_probs - jnp.sum(delta_probs * probs, axis=-1, keepdims=True))
+            delta_scores = delta_scores.astype(LOW)
+            parts = (
+                dot(delta_scores, keys) * (HEAD_DIM ** (-0.5)),
+                dot_tn(delta_scores, queries),
+                dot_tn(probs.astype(LOW), delta),
+            )
+            for spot, part in enumerate(parts):
+                part = part * sides_full[side]
+                totals[spot] = part if totals[spot] is None else totals[spot] + part
+        for spot, total in enumerate(totals):
+            ref["right_qkv"][:, head_columns(pair, spot * width)] = total.astype(LOW)
+        return carry
+
+    lax.fori_loop(0, HEADS // 2, attend_back, 0)
+    swap("qkv")
+    multiply("out")
+    for number in range(third):
+        columns = slice(number * 256, (number + 1) * 256)
+        part = dot_nt(ref["right_qkv"][...], ref["w_qkv_held"][columns, :])
+        ref["delta_normed"][:, columns] = part
+    for spot, first in ((BIAS_Q, 0), (BIAS_V, 2 * width)):
+        ref["vec_own"][spot : spot + 1, :] = jnp.sum(
+            ref["right_qkv"][:, first : first + width].astype(FULL), axis=0, keepdims=True
+        )
+    multiply("qkv")
+
+    def first_back(step, sums):
+        rows = pl.ds(pl.multiple_of(step * 64, 64), 64)
+        delta = ref["delta_normed"][rows, :]
+        row_term, gains = norm_rows_back(delta, ref["tokens"][rows, :].astype(FULL), ref["ln1_gain"][...])
+        ref["grad_tokens"][rows, :] = (ref["delta_block"][rows, :] + row_term).astype(LOW)
+        return tuple(old + jnp.sum(new, axis=0, keepdims=True) for old, new in zip(sums, (gains, delta)))
+
+    sums = lax.fori_loop(0, 4, first_back, (zeros, zeros))
+    for spot, total in zip((LN1_GAIN, LN1_BIAS), sums):
+        ref["vec_own"][spot : spot + 1, :] = total
+    ref["vec_held"][0] = ref["vec_own"][...]
+    begin(vec_copy(0))
+
+    for number, axis in enumerate(PEERS + ("self",)):
+        if axis == "self":
+            source = my_pos
+            arrived = ref["grid_out"][my_pos]
+        else:
+            source = peer(axis)[1]
+            remote(ref["grid_out"].at[source], ref["grid_in"].at[number], "grid", number, axis).wait_recv()
+            arrived = ref["grid_in"][number]
+        placing = ref["placing"][number]
+        visible = jnp.sum(placing.astype(FULL), axis=1, keepdims=True)
+        filled = jnp.where(visible > 0.5, dot(placing, arrived), ref["mask_token"][...].astype(FULL)).astype(LOW)
+        for image in range(IMG_SEQ):
+            ref["decoder_input"][source * IMG_SEQ + image] = filled[
+                image * PLACES : image * PLACES + quarter_len
+            ]
+
+    for spot, (number, stage) in enumerate(ORDER):
+        arrive(number, stage)
+        if spot % 6 == 5 and spot // 6 < 5:
+            arrive_vec(spot // 6)
+    for name in MATRICES:
+        rows = block_rows(name)
+        final, out = ref["final_" + name], ref["grad_" + name]
+        wide = final.shape[3]
+        for side in range(2):
+            for half in range(2):
+                piece = final[side, half]
+                if name == "down":
+                    out[(side * 2 + half) * rows : (side * 2 + half + 1) * rows, :] = piece
+                else:
+                    out[half * rows : (half + 1) * rows, side * wide : (side + 1) * wide] = piece
+    for copy in started:
+        copy.wait_send()
+
+
+def finish_kernel(*refs):
+    ins, outs = refs[:8], refs[8:]
+    for source, target in zip(ins[:7], outs[:7]):
+        target[...] = source[...].astype(target.dtype)
+    sums = ins[7]
+    for spot, target in zip(
+        (LN1_GAIN, LN1_BIAS, BIAS_Q, BIAS_V, BIAS_OUT, LN2_GAIN, LN2_BIAS, BIAS_DOWN, BIAS_PROJ, MASK), outs[7:17]
+    ):
+        target[...] = sums[spot : spot + 1, : target.shape[1]]
+    wide = sums.shape[1]
+    for number in range(outs[17].shape[1] // wide):
+        outs[17][:, number * wide : (number + 1) * wide] = sums[BIAS_UP + number : BIAS_UP + number + 1, :]
+
+
+def layer_device(
+    tokens,
+    image_slot,
+    patch_position,
+    ln1_gain,
+    ln1_bias,
+    w_qkv,
+    bias_query,
+    bias_value,
+    w_out,
+    bias_out,
+    ln2_gain,
+    ln2_bias,
+    w_up,
+    bias_up,
+    w_down,
+    bias_down,
+    w_proj,
+    bias_proj,
+    mask_token,
+    cotangent,
+):
+    rows, width = tokens.shape
+    ff = w_up.shape[1]
+    out_width = w_proj.shape[1]
+    row = lambda vec: vec.reshape(1, -1)
+    vmem = pl.BlockSpec(memory_space=pltpu.VMEM)
+    hbm = pl.BlockSpec(memory_space=pl.ANY)
+    inputs = {
+        "tokens": tokens,
+        "slot": row(image_slot),
+        "position": row(patch_position),
+        "ln1_gain": row(ln1_gain),
+        "ln1_bias": row(ln1_bias),
+        "bias_query": row(bias_query),
+        "bias_value": row(bias_value),
+        "bias_out": row(bias_out),
+        "ln2_gain": row(ln2_gain),
+        "ln2_bias": row(ln2_bias),
+        "bias_up": row(bias_up),
+        "bias_down": row(bias_down),
+        "bias_proj": row(bias_proj),
+        "mask_token": row(mask_token),
+        "cotangent": cotangent,
+        "w_qkv": w_qkv,
+        "w_out": w_out,
+        "w_proj": w_proj,
+        "w_up": w_up,
+        "w_down": w_down,
+    }
+    lefts = {"down": ff, "up": width, "proj": width, "out": width, "qkv": width}
+    rights = {"down": width, "up": ff, "proj": out_width, "out": width, "qkv": 3 * width}
+    results = {name: jax.ShapeDtypeStruct((lefts[name] // 8, rights[name]), LOW) for name in MATRICES}
+    outs = {"grad_" + name: results[name] for name in MATRICES}
+    outs["decoder_input"] = jax.ShapeDtypeStruct(cotangent.shape, LOW)
+    outs["grad_tokens"] = jax.ShapeDtypeStruct(tokens.shape, LOW)
+    outs["vec_sums"] = jax.ShapeDtypeStruct((16, width), FULL)
+    dma = pltpu.SemaphoreType.DMA
+    room = {
+        "w_qkv_held": (w_qkv.shape, LOW),
+        "w_out_held": (w_out.shape, LOW),
+        "w_proj_held": (w_proj.shape, LOW),
+        "w_up_held": (w_up.shape, LOW),
+        "w_down_held": (w_down.shape, LOW),
+        "places": ((4, 8, rows), jnp.int32),
+        "chosen": ((4, IMG_SEQ * CAP, rows), LOW),
+        "placing": ((4, IMG_SEQ * PLACES, IMG_SEQ * CAP), LOW),
+        "allowed": ((rows, rows), FULL),
+        "cot_wide": ((4 * IMG_SEQ, PLACES, out_width), LOW),
+        "back_out": ((3, IMG_SEQ * CAP, out_width), LOW),
+        "back_in": ((4, IMG_SEQ * CAP, out_width), LOW),
+        "grid_out": ((4, IMG_SEQ * CAP, out_width), LOW),
+        "grid_in": ((3, IMG_SEQ * CAP, out_width), LOW),
+        "normed": ((rows, width), LOW),
+        "qkv": ((rows, 3 * width), LOW),
+        "probs": ((HEADS, rows, rows), FULL),
+        "attended": ((rows, width), LOW),
+        "residual": ((rows, width), FULL),
+        "delta_block": ((rows, width), FULL),
+        "mlp_out": ((rows, width), FULL),
+        "delta_normed": ((rows, width), FULL),
+        "block_low": ((rows, width), LOW),
+        "delta_attended": ((rows, width), LOW),
+        "bias_up_sum": ((1, ff), FULL),
+        "vec_own": ((16, width), FULL),
+        "vec_held": ((5, 16, width), FULL),
+        "vec_in": ((5, 16, width), FULL),
+    }
+    for name in MATRICES:
+        room["left_" + name] = ((lefts[name], rows), LOW)
+        room["right_" + name] = ((rows, rights[name]), LOW)
+        if name == "down":
+            room["left_in_down"] = ((8, 192, rows), LOW)
+            room["right_in_down"] = ((rows, rights[name]), LOW)
+            room["final_down"] = ((2, 2, 96, rights[name]), LOW)
+        else:
+            room["left_in_" + name] = ((lefts[name], rows), LOW)
+            room["right_in_" + name] = ((rows, rights[name] // 2), LOW)
+            room["final_" + name] = ((2, 2, 48, rights[name] // 2), LOW)
+    for number, (name, _, wide, _) in enumerate(JOBS):
+        block = (block_rows(name), wide)
+        room["partial%d" % number] = ((2, 2, 2, 2) + block, LOW)
+        for stage in range(4):
+            room["landed%d_%d" % (number, stage)] = ((2,) * (3 - stage) + block, LOW)
+    scratch = {name: pltpu.VMEM(shape, dtype) for name, (shape, dtype) in room.items()}
+    scratch["load"] = dma((5,))
+    for kind, shape in (
+        ("place", (3,)),
+        ("back", (3,)),
+        ("grid", (3,)),
+        ("core", (5, 2)),
+        ("job", (len(JOBS), 6)),
+        ("vec", (5,)),
+    ):
+        scratch[kind + "_send"] = dma(shape)
+        scratch[kind + "_recv"] = dma(shape)
+    names = tuple(inputs) + tuple(outs) + tuple(scratch)
+    found = pl.pallas_call(
+        functools.partial(layer_kernel, names),
+        out_shape=list(outs.values()),
+        in_specs=[hbm if name.startswith("w_") else vmem for name in inputs],
+        out_specs=[vmem] * len(outs),
+        scratch_shapes=list(scratch.values()),
+        compiler_params=pltpu.CompilerParams(
+            collective_id=0, has_side_effects=True, vmem_limit_bytes=63 * 2**20
+        ),
+        name="layer",
+    )(*inputs.values())
+    found = dict(zip(outs, found))
+    sources = [found["grad_" + name] for name in MATRICES] + [found["decoder_input"], found["grad_tokens"]]
+    shapes = [jax.ShapeDtypeStruct(source.shape, FULL) for source in sources[:5]]
+    shapes += [jax.ShapeDtypeStruct(source.shape, LOW) for source in sources[5:]]
+    vec_width = [width] * 8 + [out_width] * 2 + [ff]
+    shapes += [jax.ShapeDtypeStruct((1, wide), FULL) for wide in vec_width]
+    done = pl.pallas_call(
+        finish_kernel,
+        out_shape=shapes,
+        in_specs=[vmem] * 8,
+        out_specs=[vmem] * len(shapes),
+        compiler_params=pltpu.CompilerParams(vmem_limit_bytes=40 * 2**20),
+        name="finish",
+    )(*sources, found["vec_sums"])
+    down, up, proj, out, qkv, decoder_input, grad_tokens = done[:7]
+    gain1, bias1, b_query, b_value, b_out, gain2, bias2, b_down, b_proj, mask, b_up = [
+        vec.reshape(-1) for vec in done[7:]
+    ]
+    return (
+        decoder_input,
+        grad_tokens,
+        gain1,
+        bias1,
+        qkv,
+        b_query,
+        b_value,
+        out,
+        b_out,
+        gain2,
+        bias2,
+        up,
+        b_up,
+        down,
+        b_down,
+        proj,
+        b_proj,
+        mask,
+    )
+
+
 def solution(mesh):
     placed = (
         P(("img", "pos"), None),
@@ -286,8 +1048,9 @@
         P(),
         P("img", "pos", None),
     )
+    fits = mesh.shape["img"] == 8 and mesh.shape["pos"] == 4
     return jax.shard_map(
-        per_device,
+        layer_device if fits else general_device,
         mesh=mesh,
         in_specs=placed,
         out_specs=(

time: 721 us -> 144 us (0.20)
  blocking collectives: 497 us -> 0 us
  Pallas kernels: 0 us -> 117 us
  matrix products: 62.6 us -> 0 us
  local copies, waits for them, and re-layouts: 71.3 us -> 19.4 us
  other arithmetic: 44.4 us -> 4.84 us
  between operations: 15.3 us -> 0.69 us
  starting transfers between devices: 14.1 us -> 0 us
  waiting for transfers between devices: 7.58 us -> 0 us
    psum x1 -> x0, blocking collectives: 483 us -> none  [reduce_vectors(): return lax.psum(tuple(members), ('img', 'pos'))]
    pallas_call x0 -> x2, Pallas kernels: none -> 117 us  [the longest x1 114 us: layer_device(): pl.pallas_call(functools.partial(layer_kernel, names), out_shape=list(out...]
    dot_general x24 -> x0, matrix products: 62.6 us -> none  [the longest x4 9.5 us: matmul_rows(): return jnp.dot(left, right, preferred_element_type=jnp.float32)]
    concatenate x5 -> x0, local copies, waits for them, and re-layouts: 25.2 us -> none  [reduce_matrices(): bucket = jnp.concatenate(pieces, axis=2)]
    concatenate x2 -> x0, other arithmetic: 23.6 us -> none  [reduce_matrices(): bucket = jnp.concatenate(pieces, axis=2)]
    slice x6 -> x0, local copies, waits for them, and re-layouts: 14.9 us -> none  [the longest x4 12.2 us: reduce_matrices(): block = summed[0, :, offset:offset + extent]]
    all_gather x1 -> x0, blocking collectives: 14 us -> none  [reduce_matrices(): lax.all_gather(share.astype(jnp.bfloat16), 'pos', axis=1, tiled=True)]
    all_to_all x3 -> x0, starting transfers between devices: 13.7 us -> none  [the longest x1 5.3 us: per_device(): lax.all_to_all(back_slots[:, None], 'pos', split_axis=0, concat_axis=1, t...]
  transfers between devices with their start and end apart: 4 -> 0, of which waited for: 3 -> 0; matrix products, arithmetic and copies ran while one was open for 7% -> 0% of each run, Pallas kernels for 0% -> 0%
where the time goes in v2:
time: 144 us; the launch traced here: 142 us
  Pallas kernels  117 us (81%)
  local copies, waits for them, and re-layouts  19.4 us (13%)
  other arithmetic  4.84 us (3%)
    pallas_call x1, Pallas kernels, layer_device(): pl.pallas_call(functools.partial(layer_kernel, names), out_shape=list(out...  114 us
    reshape x9, local copies, waits for them, and re-layouts, layer_device(): row = lambda vec: vec.reshape(1, -1)  11.4 us
    unnamed x16, local copies, waits for them, and re-layouts  7.99 us
    pallas_call x8, other arithmetic, layer_device(): pl.pallas_call(finish_kernel, out_shape=shapes, in_specs=[vmem] * 8, out_...  4.84 us

profile of v2, /device:TPU:1, one launch (start us, length us, event | category | flops | bytes accessed | tf_op | source)
XLA Modules:
  0.0 142.0 jit_solution(6775624781256756373)
XLA Ops:
  0.7 1.3 reshape.120.refs_13_
  1.9 1.3 reshape.110.refs_3_
  3.2 1.3 reshape.111.refs_4_
  4.4 1.3 reshape.112.refs_5_
  5.7 1.3 reshape.113.refs_6_
  7.0 1.3 reshape.114.refs_7_
  8.2 1.3 reshape.115.refs_8_
  9.5 1.3 reshape.116.refs_9_
  10.8 1.3 reshape.118.refs_11_
  12.0 114.4 %layer.1 = (bf16[384,768]{1,0:T(8,128)(2,1)}, bf16[96,3072]{1,0:T(8,128)(2,1)}, bf16[96,512]{1,0:T(8,128)(2,1)}, bf16[96,768]{1,0:T(8,128)(2,1)}, bf16[96,2304]{...) custom-call(bf16[256,768]{1,0:T(8,128)(2,1)} %refs_0_.1, ...), custom_call_target="tpu_custom_call" | custom-call | tf_op jit(solution)/shard_map/layer/pallas_call | solution.py:977
  126.5 0.0 copy-start
  126.5 1.2 copy-done
  127.7 0.0 copy-start.1
  127.7 1.1 copy-done.1
  128.8 0.0 copy-start.2
  128.8 1.1 copy-done.2
  129.8 0.0 copy-start.3
  129.8 1.0 copy-done.3
  130.9 0.0 copy-start.4
  130.9 1.0 copy-done.4
  131.9 0.0 copy-start.5
  131.9 0.9 copy-done.5
  132.8 0.0 copy-start.6
  132.8 0.9 copy-done.6
  133.7 0.0 copy-start.7
  133.7 0.8 copy-done.7
  134.5 2.7 %finish.1 = (f32[384,768]{1,0:T(8,128)}, f32[96,3072]{1,0:T(8,128)}, f32[96,512]{1,0:T(8,128)}, f32[96,768]{1,0:T(8,128)}, f32[96,2304]{1,0:T(8,128)}, /*index=5...) custom-call(bf16[384,768]{1,0:T(8,128)(2,1)S(1)} %copy-done.1, ...), custom_call_target="tpu_custom_call" | custom-call | tf_op jit(solution)/shard_map/finish/pallas_call | solution.py:994
  137.1 0.6 reduce
  137.8 0.6 reduce.1
  138.4 0.6 reduce.2
  139.0 0.6 reduce.3
  139.6 0.6 reduce.4
  140.2 0.6 reduce.5
  140.8 0.6 reduce.6
  141.4 0.6 reduce.7
Async XLA Ops:
  126.5 1.3 copy-start
  127.7 1.1 copy-start.1
  128.8 1.1 copy-start.2
  129.8 1.0 copy-start.3
  130.9 1.0 copy-start.4
  131.9 0.9 copy-start.5
  132.8 0.9 copy-start.6
  133.7 0.8 copy-start.7

commit v3 on v2

--- a/solution.py
+++ b/solution.py
@@ -273,86 +273,129 @@
 
 AXES = ("zh", "zl", "x", "y")
 MATRICES = ("down", "up", "proj", "out", "qkv")
-JOBS = (
-    ("down", 0, 256, ("zl", "zh", "x", "y")),
-    ("down", 256, 256, ("zl", "zh", "x", "y")),
-    ("down", 512, 256, ("zl", "zh", "x", "y")),
-    ("up", 0, 512, ("y", "x", "zl", "zh")),
-    ("up", 512, 512, ("y", "x", "zl", "zh")),
-    ("up", 1024, 512, ("y", "x", "zl", "zh")),
-    ("proj", 0, 256, ("x", "y", "zl", "zh")),
-    ("out", 0, 384, ("x", "y", "zl", "zh")),
-    ("qkv", 0, 384, ("x", "y", "zl", "zh")),
-    ("qkv", 384, 384, ("x", "y", "zl", "zh")),
-    ("qkv", 768, 384, ("x", "y", "zl", "zh")),
-)
-ORDER = (
-    (6, 0),
-    (0, 0),
-    (3, 0),
-    (7, 0),
-    (1, 0),
-    (4, 0),
-    (3, 1),
-    (2, 0),
-    (8, 0),
-    (5, 0),
-    (6, 1),
-    (0, 1),
-    (7, 1),
-    (9, 0),
-    (1, 1),
-    (8, 1),
-    (3, 2),
-    (9, 1),
-    (10, 0),
-    (2, 1),
-    (6, 2),
-    (4, 1),
-    (7, 2),
-    (10, 1),
-    (8, 2),
-    (3, 3),
-    (5, 1),
-    (9, 2),
-    (6, 3),
-    (3, 4),
-    (0, 2),
-    (4, 2),
-    (6, 4),
-    (7, 3),
-    (3, 5),
-    (1, 2),
-    (10, 2),
-    (0, 3),
-    (6, 5),
-    (8, 3),
-    (2, 2),
-    (7, 4),
-    (1, 3),
-    (5, 2),
-    (0, 4),
-    (9, 3),
-    (7, 5),
-    (8, 4),
-    (4, 3),
-    (2, 3),
-    (10, 3),
-    (0, 5),
-    (1, 4),
-    (8, 5),
-    (5, 3),
-    (9, 4),
-    (4, 4),
-    (1, 5),
-    (2, 4),
-    (9, 5),
-    (10, 4),
-    (4, 5),
-    (5, 4),
-    (2, 5),
-    (10, 5),
-    (5, 5),
+JOBS = {
+    "down0": ("down", None, 0, 256, ("zl", "y", "zh", "x")),
+    "down1": ("down", None, 256, 256, ("zl", "zh", "x", "y")),
+    "down2": ("down", None, 512, 256, ("zl", "y", "x", "zh")),
+    "up0": ("up", 0, 0, 384, ("x", "y", "zl", "zh")),
+    "up1": ("up", 1, 0, 384, ("x", "y", "zl", "zh")),
+    "up2": ("up", 2, 0, 384, ("x", "y", "zl", "zh")),
+    "up3": ("up", 3, 0, 384, ("x", "y", "zl", "zh")),
+    "proj0": ("proj", None, 0, 256, ("y", "zl", "x", "zh")),
+    "out0": ("out", None, 0, 384, ("x", "y", "zl", "zh")),
+    "qkv0": ("qkv", None, 0, 384, ("x", "y", "zl", "zh")),
+    "qkv1": ("qkv", None, 384, 384, ("y", "zl", "zh", "x")),
+    "qkv2": ("qkv", None, 768, 384, ("x", "y", "zl", "zh")),
+}
+PLAN = (
+    ("do", "feed0"),
+    ("do", "feed1"),
+    ("do", "multiply_feed0"),
+    ("do", "feed2"),
+    ("do", "multiply_feed1"),
+    ("do", "feed3"),
+    ("do", "multiply_feed2"),
+    ("do", "project"),
+    ("down0", 0, "a"),
+    ("do", "multiply_feed3"),
+    ("up0", 0, ""),
+    ("do", "second_back"),
+    ("down1", 0, "a"),
+    ("do", "swapped_proj"),
+    ("do", "multiply_proj0"),
+    ("do", "attended_back"),
+    ("do", "attend_back0"),
+    ("do", "attend_back1"),
+    ("do", "attend_back2"),
+    ("do", "attend_back3"),
+    ("up0", 1, ""),
+    ("down2", 0, "a"),
+    ("up1", 0, ""),
+    ("do", "attend_back4"),
+    ("do", "attend_back5"),
+    ("do", "swapped_out"),
+    ("do", "multiply_out0"),
+    ("do", "delta_first"),
+    ("proj0", 0, ""),
+    ("down0", 0, "b"),
+    ("do", "swapped_qkv"),
+    ("do", "multiply_qkv0"),
+    ("do", "multiply_qkv1"),
+    ("do", "multiply_qkv2"),
+    ("up2", 0, ""),
+    ("up1", 1, ""),
+    ("do", "first_back"),
+    ("down1", 0, "b"),
+    ("do", "decode"),
+    ("vec", 0),
+    ("down0", 1, ""),
+    ("down2", 0, "b"),
+    ("up3", 0, ""),
+    ("qkv1", 0, ""),
+    ("up1", 2, ""),
+    ("out0", 0, ""),
+    ("proj0", 1, ""),
+    ("up2", 1, ""),
+    ("down1", 1, ""),
+    ("up0", 2, ""),
+    ("down2", 1, ""),
+    ("qkv0", 0, ""),
+    ("down0", 2, ""),
+    ("qkv1", 1, ""),
+    ("up3", 1, ""),
+    ("up3", 2, ""),
+    ("up3", 3, ""),
+    ("out0", 1, ""),
+    ("qkv2", 0, ""),
+    ("vec", 1),
+    ("proj0", 2, ""),
+    ("up2", 2, ""),
+    ("up2", 3, ""),
+    ("qkv0", 1, ""),
+    ("up3", 4, ""),
+    ("qkv1", 2, ""),
+    ("down1", 2, ""),
+    ("out0", 2, ""),
+    ("up1", 3, ""),
+    ("up3", 5, ""),
+    ("down2", 2, ""),
+    ("proj0", 3, ""),
+    ("qkv2", 1, ""),
+    ("down0", 3, ""),
+    ("qkv0", 2, ""),
+    ("vec", 2),
+    ("up0", 3, ""),
+    ("qkv1", 3, ""),
+    ("up2", 4, ""),
+    ("down1", 3, ""),
+    ("out0", 3, ""),
+    ("up1", 4, ""),
+    ("proj0", 4, ""),
+    ("qkv2", 2, ""),
+    ("up2", 5, ""),
+    ("down0", 4, ""),
+    ("down2", 3, ""),
+    ("up0", 4, ""),
+    ("up1", 5, ""),
+    ("vec", 3),
+    ("proj0", 5, ""),
+    ("qkv1", 4, ""),
+    ("qkv0", 3, ""),
+    ("down0", 5, ""),
+    ("down1", 4, ""),
+    ("up0", 5, ""),
+    ("out0", 4, ""),
+    ("qkv2", 3, ""),
+    ("qkv1", 5, ""),
+    ("down2", 4, ""),
+    ("qkv0", 4, ""),
+    ("down1", 5, ""),
+    ("out0", 5, ""),
+    ("vec", 4),
+    ("qkv2", 4, ""),
+    ("down2", 5, ""),
+    ("qkv0", 5, ""),
+    ("qkv2", 5, ""),
 )
 VEC_STEPS = ("core", "x", "y", "zl", "zh")
 PEERS = ("y", "core", "diagonal")
@@ -407,6 +450,10 @@
 
 def layer_kernel(names, *refs):
     ref = dict(zip(names, refs))
+
+    def row_of(name, columns=slice(None)):
+        return ref[name][...].reshape(1, -1)[:, columns]
+
     me = device_coords()
     core = me["core"]
     my_pos = me["y"] * 2 + core
@@ -436,7 +483,7 @@
         started.append(copy)
 
     loads = {}
-    for number, name in enumerate(("w_qkv", "w_out", "w_proj", "w_up", "w_down")):
+    for number, name in enumerate(("w_qkv", "cotangent", "w_out", "w_proj", "w_up", "w_down")):
         loads[name] = pltpu.make_async_copy(ref[name], ref[name + "_held"], ref["load"].at[number])
         loads[name].start()
 
@@ -450,10 +497,10 @@
     def first_norm(step, carry):
         rows = pl.ds(pl.multiple_of(step * 64, 64), 64)
         xhat, _ = normalised(ref["tokens"][rows, :].astype(FULL))
-        ref["normed"][rows, :] = (xhat * ref["ln1_gain"][...] + ref["ln1_bias"][...]).astype(LOW)
+        ref["normed"][rows, :] = (xhat * row_of("ln1_gain") + row_of("ln1_bias")).astype(LOW)
         return carry
 
-    lax.fori_loop(0, 4, first_norm, 0)
+    lax.fori_loop(0, 4, first_norm, 0, unroll=4)
 
     pl.semaphore_wait(barrier, 6)
     for number, axis in enumerate(PEERS):
@@ -465,12 +512,12 @@
         columns = slice(number * 256, (number + 1) * 256)
         part = dot(ref["normed"][...], ref["w_qkv_held"][:, columns])
         if number < third:
-            part = part + ref["bias_query"][:, columns]
+            part = part + row_of("bias_query", columns)
             part = part.astype(LOW) * LOW(HEAD_DIM ** (-0.5))
         elif number >= 2 * third:
-            part = part + ref["bias_value"][:, (number - 2 * third) * 256 : (number - 2 * third + 1) * 256]
+            part = part + row_of("bias_value", slice((number - 2 * third) * 256, (number - 2 * third + 1) * 256))
         ref["qkv"][:, columns] = part.astype(LOW)
-    ref["left_qkv"][...] = ref["normed"][...].T
+    ref["normed_one"][...] = ref["normed"][...]
 
     row_ids = lax.broadcasted_iota(jnp.int32, (ROWS_SEQ, ROWS_SEQ), 0)
     lane_ids = lax.broadcasted_iota(jnp.int32, (ROWS_SEQ, ROWS_SEQ), 1)
@@ -496,9 +543,9 @@
     ref["allowed"][...] = jnp.where(dot_tn(slots, slots) > 0.5, 0.0, NEGATIVE)
 
     ref["cot_wide"][...] = jnp.zeros_like(ref["cot_wide"])
+    loads["cotangent"].wait()
     for image in range(4 * IMG_SEQ):
-        ref["cot_wide"][image, 0:quarter_len, :] = ref["cotangent"][image]
-    mask_sum = jnp.zeros((8, ref["cotangent"].shape[2]), FULL)
+        ref["cot_wide"][image, 0:quarter_len, :] = ref["cotangent_held"][image]
     for number, axis in enumerate(PEERS + ("self",)):
         if axis == "self":
             source = my_pos
@@ -519,17 +566,14 @@
         else:
             ref["back_out"][number] = back
             begin(remote(ref["back_out"].at[number], ref["back_in"].at[my_pos], "back", number, axis))
-        seen = dot_nt(jnp.ones((8, IMG_SEQ * CAP), LOW), placing_low)
-        mask_sum = mask_sum + dot((1.0 - seen).astype(LOW), cot)
     ref["vec_own"][...] = jnp.zeros_like(ref["vec_own"])
-    ref["vec_own"][MASK : MASK + 1, : mask_sum.shape[1]] = mask_sum[0:1]
 
     lane = lax.broadcasted_iota(jnp.int32, (1, 2 * HEAD_DIM), 1)
     sides_full = [(lane < HEAD_DIM).astype(FULL), (lane >= HEAD_DIM).astype(FULL)]
     sides = [side.astype(LOW) for side in sides_full]
 
     def head_columns(pair, first):
-        return pl.ds(pl.multiple_of(first + pair * 2 * HEAD_DIM, 2 * HEAD_DIM), 2 * HEAD_DIM)
+        return pl.ds(first + pair * 2 * HEAD_DIM, 2 * HEAD_DIM)
 
     def attend(pair, carry):
         queries = ref["qkv"][:, head_columns(pair, 0)]
@@ -546,8 +590,8 @@
         ref["attended"][:, head_columns(pair, 0)] = total.astype(LOW)
         return carry
 
-    lax.fori_loop(0, HEADS // 2, attend, 0)
-    ref["left_out"][...] = ref["attended"][...].T
+    for pair in range(HEADS // 2):
+        attend(pair, 0)
 
     loads["w_out"].wait()
     for number in range(third):
@@ -555,16 +599,16 @@
         ref["residual"][:, columns] = (
             ref["tokens"][:, columns].astype(FULL)
             + dot(ref["attended"][...], ref["w_out_held"][:, columns])
-            + ref["bias_out"][:, columns]
+            + row_of("bias_out", columns)
         )
 
     def second_norm(step, carry):
         rows = pl.ds(pl.multiple_of(step * 64, 64), 64)
         xhat, _ = normalised(ref["residual"][rows, :])
-        ref["normed"][rows, :] = (xhat * ref["ln2_gain"][...] + ref["ln2_bias"][...]).astype(LOW)
+        ref["normed"][rows, :] = (xhat * row_of("ln2_gain") + row_of("ln2_bias")).astype(LOW)
         return carry
 
-    lax.fori_loop(0, 4, second_norm, 0)
+    lax.fori_loop(0, 4, second_norm, 0, unroll=4)
     ref["left_up"][...] = ref["normed"][...].T
 
     loads["w_proj"].wait()
@@ -585,11 +629,17 @@
 
     loads["w_up"].wait()
     loads["w_down"].wait()
-    ref["mlp_out"][...] = jnp.zeros_like(ref["mlp_out"])
-    ref["delta_normed"][...] = jnp.zeros_like(ref["delta_normed"])
-
-    def feed(step, carry):
-        columns = pl.ds(pl.multiple_of(step * 256, 256), 256)
+
+    def chunk_of(slot):
+        high = 1 - me["zh"] if slot < 2 else me["zh"]
+        low = 1 - me["zl"] if slot % 2 == 0 else me["zl"]
+        return high, low, high * 2 + low
+
+    def chunk_columns(slot, start=0, wide=width):
+        return pl.ds(pl.multiple_of(chunk_of(slot)[2] * width + start, 128), wide)
+
+    def feed(slot):
+        columns = chunk_columns(slot)
         up = dot(ref["normed"][...], ref["w_up_held"][:, columns]) + ref["bias_up"][:, columns]
         square = up * up
         bent = jnp.tanh(GELU_COEF * (up + 0.044715 * up * square))
@@ -600,112 +650,227 @@
         back = dot_nt(ref["right_down"][...], ref["w_down_held"][columns, :])
         delta_up = (back * slope).astype(LOW)
         ref["right_up"][:, columns] = delta_up
+        for copy in swap_copies("feed%d" % slot):
+            begin(copy)
         ref["bias_up_sum"][:, columns] = jnp.sum(delta_up.astype(FULL), axis=0, keepdims=True)
-        ref["mlp_out"][...] += dot(hidden, ref["w_down_held"][columns, :])
-        ref["delta_normed"][...] += dot_nt(delta_up, ref["w_up_held"][:, columns])
-        return carry
-
-    lax.fori_loop(0, ff // 256, feed, 0)
-    for number in range(ff // width):
-        ref["vec_own"][BIAS_UP + number : BIAS_UP + number + 1, :] = ref["bias_up_sum"][
-            :, number * width : (number + 1) * width
-        ]
-
-    def half_columns(name, side):
-        wide = ref["right_" + name].shape[1] // 2
-        return pl.ds(pl.multiple_of(side * wide, 128), wide)
-
-    def core_copies(name):
-        spot = MATRICES.index(name)
-        if name == "down":
-            left = ref["left_down"].reshape(8, 2, 192, ROWS_SEQ).at[:, 1 - core]
-            right = ref["right_down"]
+        out = dot(hidden, ref["w_down_held"][columns, :])
+        delta = dot_nt(delta_up, ref["w_up_held"][:, columns])
+        if slot == 0:
+            ref["mlp_out"][...] = out
+            ref["delta_normed"][...] = delta
         else:
-            left = ref["left_" + name]
-            right = ref["right_" + name].at[:, half_columns(name, 1 - core)]
-        return (
-            remote(left, ref["left_in_" + name], "core", (spot, 0), "core"),
-            remote(right, ref["right_in_" + name], "core", (spot, 1), "core"),
+            ref["mlp_out"][...] += out
+            ref["delta_normed"][...] += delta
+
+    swaps = ("early", "feed0", "feed1", "feed2", "feed3", "proj", "out", "qkv")
+
+    def swap_copies(which):
+        other = 1 - core
+        if which == "early":
+            pairs = ((ref["left_up"], ref["left_in_up"]), (ref["right_down"], ref["right_in_down"]))
+        elif which.startswith("feed"):
+            slot = int(which[4:])
+            _, _, chunk = chunk_of(slot)
+            left = ref["left_down"].reshape(8, 2, 192, ROWS_SEQ)
+            right = ref["right_up"].at[:, chunk_columns(slot, other * (width // 2), width // 2)]
+            pairs = (
+                (left.at[pl.ds(chunk * 2, 2), other], ref["left_in_down"].at[pl.ds(chunk * 2, 2)]),
+                (right, ref["right_in_up"].at[slot]),
+            )
+        else:
+            wide = ref["right_" + which].shape[1] // 2
+            right = ref["right_" + which].at[:, pl.ds(pl.multiple_of(other * wide, 128), wide)]
+            pairs = ((ref["left_" + which], ref["left_in_" + which]), (right, ref["right_in_" + which]))
+        spot = swaps.index(which)
+        return [remote(source, target, "core", (spot, part), "core") for part, (source, target) in enumerate(pairs)]
+
+    def swap(which):
+        for copy in swap_copies(which):
+            begin(copy)
+
+    def swapped(which):
+        for copy in swap_copies(which):
+            copy.wait_recv()
+
+    job_names = tuple(JOBS)
+
+    def job_final(job):
+        matrix, slot, first, wide, _ = JOBS[job]
+        final = ref["final_" + matrix]
+        if slot is not None:
+            final = final.at[chunk_of(slot)[2]]
+        return final, pl.ds(first, wide)
+
+    def job_target(job, stage):
+        _, slot, _, _, dims = JOBS[job]
+        if slot is None or stage > 3 or dims[stage] not in ("zl", "zh"):
+            return job
+        return "up%d%s" % (slot ^ (1 if dims[stage] == "zl" else 2), job[3:])
+
+    def job_index(job, stage, part, mine):
+        dims = JOBS[job][4]
+        pick, land = [], []
+        for axis in AXES:
+            if axis in dims[:stage]:
+                pick.append(me[axis])
+            elif axis == dims[stage]:
+                pick.append(me[axis] if mine else 1 - me[axis])
+            elif axis == "zh" and part:
+                pick.append(1 - me[axis] if part == "a" else me[axis])
+                land.append(pick[-1])
+            else:
+                pick.append(slice(None))
+                land.append(slice(None))
+        return tuple(pick), tuple(land)
+
+    def job_copy(job, stage, part):
+        dims = JOBS[job][4]
+        target = job_target(job, stage)
+        spot = stage if part != "b" else 6
+        send_sem = ref["job_send"].at[job_names.index(job), spot]
+        recv_sem = ref["job_recv"].at[job_names.index(target), spot]
+        if stage < 4:
+            pick, land = job_index(job, stage, part, False)
+            source = ref["partial_" + job].at[pick]
+            place = ref["landed_%s_%d" % (target, stage)]
+            place = place.at[land] if land else place
+            axis = dims[stage]
+        else:
+            final, columns = job_final(job)
+            if stage == 4:
+                source = place = final.at[core, me["y"], :, columns]
+            else:
+                source = place = final.at[core, :, :, columns]
+            axis = "y" if stage == 4 else "core"
+        return pltpu.make_async_remote_copy(
+            src_ref=source,
+            dst_ref=place,
+            send_sem=send_sem,
+            recv_sem=recv_sem,
+            device_id=peer(axis),
+            device_id_type=MESH_ID,
         )
 
-    def swap(name):
-        for copy in core_copies(name):
-            begin(copy)
-
-    def job_copy(number, stage):
-        name, first, wide, dims = JOBS[number]
-        columns = pl.ds(first, wide)
+    def first_parts(job):
+        return ("a", "b") if JOBS[job][0] == "down" else ("",)
+
+    def needs(job, stage):
+        if stage == 0:
+            return ()
+        if stage == 1:
+            return tuple((0, part) for part in first_parts(job) if part != "b" or JOBS[job][4][1] != "zh")
+        if stage == 2:
+            return ((1, ""),) + tuple((0, part) for part in first_parts(job))
+        return ((stage - 1, ""),)
+
+    arrived, sent = set(), set()
+
+    def send(job, stage, part=""):
+        sent.add((job, stage, part))
+        begin(job_copy(job, stage, part))
+
+    def arrive(job, stage, part):
+        matrix, slot, _, _, dims = JOBS[job]
+        source = job_copy(job_target(job, stage), stage, part)
+        source.wait_recv()
         if stage < 4:
-            pick = []
-            for axis in AXES:
-                if axis in dims[:stage]:
-                    pick.append(me[axis])
-                elif axis == dims[stage]:
-                    pick.append(1 - me[axis])
+            partial, landed = ref["partial_" + job], ref["landed_%s_%d" % (job, stage)]
+            pick, land = job_index(job, stage, part, True)
+            free = [spot for spot, index in enumerate(pick) if isinstance(index, slice)]
+            for code in range(2 ** len(free)):
+                here, there = list(pick), list(land)
+                for order, spot in enumerate(free):
+                    bit = (code >> (len(free) - 1 - order)) % 2
+                    here[spot] = bit
+                    there[[place for place, axis in enumerate(AXES) if axis not in dims[: stage + 1]].index(spot)] = bit
+                sums = partial[tuple(here)] + (landed[tuple(there)] if there else landed[...])
+                if stage < 3:
+                    partial[tuple(here)] = sums
                 else:
-                    pick.append(slice(None))
-            source = ref["partial%d" % number].at[tuple(pick)]
-            return remote(source, ref["landed%d_%d" % (number, stage)], "job", (number, stage), dims[stage])
-        if stage == 4:
-            place = ref["final_" + name].at[core, me["y"], :, columns]
-            return remote(place, place, "job", (number, stage), "y")
-        place = ref["final_" + name].at[core, :, :, columns]
-        return remote(place, place, "job", (number, stage), "core")
-
-    def multiply(name):
-        numbers = [number for number, job in enumerate(JOBS) if job[0] == name]
-        for copy in core_copies(name):
-            copy.wait_recv()
-        rows = block_rows(name)
-        left, right = ref["left_" + name], ref["right_" + name]
-        left_in, right_in = ref["left_in_" + name], ref["right_in_" + name]
-        if name == "down":
-            for block in range(8):
-                spot = pl.multiple_of(block * 384 + core * 192, 192)
-                total = dot(left[pl.ds(spot, 192), :], right[...]) + dot(left_in[block], right_in[...])
-                total = total.astype(LOW)
-                for number in numbers:
-                    _, first, wide, _ = JOBS[number]
+                    final, columns = job_final(job)
+                    final[core, me["y"], :, columns] = sums
+        arrived.add((job, stage, part))
+        for later in range(1, 6):
+            ready = all((job,) + need in arrived for need in needs(job, later))
+            if (job, later, "") not in sent and ready:
+                send(job, later)
+        if stage == 5:
+            final, columns = job_final(job)
+            _, _, first, wide, _ = JOBS[job]
+            out = ref["grad_" + matrix]
+            for side in range(2):
+                if matrix == "down":
+                    place = out.at[side, :, :, columns]
+                else:
+                    start = side * ref["final_" + matrix].shape[-1] + first
+                    if slot is not None:
+                        place = out.at[:, :, chunk_columns(slot, start, wide)]
+                    else:
+                        place = out.at[:, :, pl.ds(start, wide)]
+                store = pltpu.make_async_copy(
+                    final.at[side, :, :, columns], place, ref["store"].at[job_names.index(job), side]
+                )
+                store.start()
+                stores.append(store)
+
+    stores = []
+
+    def keep(name, number):
+        store = pltpu.make_async_copy(ref[name + "_held"], ref[name], ref["keep"].at[number])
+        store.start()
+        stores.append(store)
+
+    def multiply_feed(slot):
+        if slot == 0:
+            swapped("early")
+        swapped("feed%d" % slot)
+        high, low, chunk = chunk_of(slot)
+        for side in range(2):
+            block = chunk * 2 + side
+            rows = pl.ds(pl.multiple_of(block * 384 + core * 192, 192), 192)
+            total = dot(ref["left_down"][rows, :], ref["right_down"][...]) + dot(
+                ref["left_in_down"][block], ref["right_in_down"][...]
+            )
+            total = total.astype(LOW)
+            for job, (matrix, _, first, wide, _) in JOBS.items():
+                if matrix == "down":
                     for half in range(2):
-                        ref["partial%d" % number][block // 4, (block // 2) % 2, block % 2, half] = total[
-                            half * rows : (half + 1) * rows, first : first + wide
+                        ref["partial_" + job][high, low, side, half] = total[
+                            half * 96 : (half + 1) * 96, first : first + wide
                         ]
-            for number in numbers:
-                begin(job_copy(number, 0))
-            return
-        wide_half = right.shape[1] // 2
-        for number in numbers:
-            _, first, wide, _ = JOBS[number]
-            columns = pl.ds(pl.multiple_of(core * wide_half + first, 128), wide)
-            for high in range(2):
-                span = slice(high * 8 * rows, (high + 1) * 8 * rows)
-                total = dot(left[span, :], right[:, columns]) + dot(
-                    left_in[span, :], right_in[:, first : first + wide]
-                )
-                total = total.astype(LOW)
-                for part in range(8):
-                    ref["partial%d" % number][high, part // 4, (part // 2) % 2, part % 2] = total[
-                        part * rows : (part + 1) * rows
-                    ]
-            begin(job_copy(number, 0))
-
-    def arrive(number, stage):
-        name, first, wide, dims = JOBS[number]
-        job_copy(number, stage).wait_recv()
-        if stage < 4:
-            partial, landed = ref["partial%d" % number], ref["landed%d_%d" % (number, stage)]
-            fixed = dims[: stage + 1]
-            free = [axis for axis in AXES if axis not in fixed]
-            for code in range(2 ** len(free)):
-                bits = {axis: (code >> (len(free) - 1 - spot)) % 2 for spot, axis in enumerate(free)}
-                here = tuple(me[axis] if axis in fixed else bits[axis] for axis in AXES)
-                sums = partial[here] + landed[tuple(bits[axis] for axis in free)]
-                if stage < 3:
-                    partial[here] = sums
-                else:
-                    ref["final_" + name][core, me["y"], :, first : first + wide] = sums
-        if stage < 5:
-            begin(job_copy(number, stage + 1))
+        if slot % 2 == 0:
+            for job in JOBS:
+                if JOBS[job][0] == "down":
+                    send(job, 0, "ab"[slot // 2])
+        for block in range(2):
+            rows = slice(block * 384, (block + 1) * 384)
+            total = dot(
+                ref["left_up"][rows, :], ref["right_up"][:, chunk_columns(slot, core * (width // 2), width // 2)]
+            ) + dot(ref["left_in_up"][rows, :], ref["right_in_up"][slot])
+            total = total.astype(LOW)
+            for job, (matrix, own, first, wide, _) in JOBS.items():
+                if matrix == "up" and own == slot:
+                    for part in range(8):
+                        ref["partial_" + job][block, part // 4, (part // 2) % 2, part % 2] = total[
+                            part * 48 : (part + 1) * 48, first : first + wide
+                        ]
+        for job, (matrix, own, _, _, _) in JOBS.items():
+            if matrix == "up" and own == slot:
+                send(job, 0)
+
+    def multiply(job):
+        matrix, _, first, wide, _ = JOBS[job]
+        wide_half = ref["right_" + matrix].shape[1] // 2
+        columns = pl.ds(pl.multiple_of(core * wide_half + first, 128), wide)
+        for block in range(2):
+            rows = slice(block * 384, (block + 1) * 384)
+            total = dot(ref["left_" + matrix][rows, :], ref["right_" + matrix][:, columns]) + dot(
+                ref["left_in_" + matrix][rows, :], ref["right_in_" + matrix][:, first : first + wide]
+            )
+            total = total.astype(LOW)
+            for part in range(8):
+                ref["partial_" + job][block, part // 4, (part // 2) % 2, part % 2] = total[part * 48 : (part + 1) * 48]
+        send(job, 0)
 
     def vec_copy(stage):
         return remote(ref["vec_held"].at[stage], ref["vec_in"].at[stage], "vec", stage, VEC_STEPS[stage])
@@ -719,47 +884,46 @@
         else:
             ref["vec_sums"][...] = sums
 
-    swap("down")
-    swap("up")
-
-    for number in range(third):
-        columns = slice(number * 256, (number + 1) * 256)
-        ref["block_low"][:, columns] = (
-            ref["residual"][:, columns] + ref["mlp_out"][:, columns] + ref["bias_down"][:, columns]
-        ).astype(LOW)
-    ref["left_proj"][...] = ref["block_low"][...].T
-    swap("proj")
-    projected = (dot(ref["block_low"][...], ref["w_proj_held"][...]) + ref["bias_proj"][...]).astype(LOW)
-    outgoing = dot(chosen_all, projected).astype(LOW)
-    ref["grid_out"][...] = outgoing.reshape(4, IMG_SEQ * CAP, -1)
-    for number, axis in enumerate(PEERS):
-        begin(remote(ref["grid_out"].at[peer(axis)[1]], ref["grid_in"].at[number], "grid", number, axis))
-
-    multiply("down")
-    multiply("up")
-    multiply("proj")
-
-    def second_back(step, sums):
-        rows = pl.ds(pl.multiple_of(step * 64, 64), 64)
-        delta = ref["delta_normed"][rows, :]
-        row_term, gains = norm_rows_back(delta, ref["residual"][rows, :], ref["ln2_gain"][...])
-        total = ref["delta_block"][rows, :] + row_term
-        low = total.astype(LOW)
-        ref["delta_block"][rows, :] = total
-        ref["right_out"][rows, :] = low
-        news = (gains, delta, low.astype(FULL))
-        return tuple(old + jnp.sum(new, axis=0, keepdims=True) for old, new in zip(sums, news))
-
-    zeros = jnp.zeros((1, width), FULL)
-    sums = lax.fori_loop(0, 4, second_back, (zeros, zeros, zeros))
-    for spot, total in zip((LN2_GAIN, LN2_BIAS, BIAS_OUT), sums):
-        ref["vec_own"][spot : spot + 1, :] = total
-    swap("out")
-    for number in range(third):
-        columns = slice(number * 256, (number + 1) * 256)
-        ref["delta_attended"][:, columns] = dot_nt(ref["right_out"][...], ref["w_out_held"][columns, :]).astype(LOW)
-
-    def attend_back(pair, carry):
+    swap("early")
+
+    def project():
+        for number in range(third):
+            columns = slice(number * 256, (number + 1) * 256)
+            ref["block_low"][:, columns] = (
+                ref["residual"][:, columns] + ref["mlp_out"][:, columns] + row_of("bias_down", columns)
+            ).astype(LOW)
+        ref["left_proj"][...] = ref["block_low"][...].T
+        swap("proj")
+        projected = (dot(ref["block_low"][...], ref["w_proj_held"][...]) + ref["bias_proj"][...]).astype(LOW)
+        outgoing = dot(chosen_all, projected).astype(LOW)
+        ref["grid_out"][...] = outgoing.reshape(4, IMG_SEQ * CAP, -1)
+        for number, axis in enumerate(PEERS):
+            begin(remote(ref["grid_out"].at[peer(axis)[1]], ref["grid_in"].at[number], "grid", number, axis))
+
+    def second_back():
+        sums = [jnp.zeros((1, width), FULL)] * 3
+        for step in range(4):
+            rows = slice(step * 64, (step + 1) * 64)
+            delta = ref["delta_normed"][rows, :]
+            row_term, gains = norm_rows_back(delta, ref["residual"][rows, :], row_of("ln2_gain"))
+            total = ref["delta_block"][rows, :] + row_term
+            low = total.astype(LOW)
+            ref["delta_block"][rows, :] = total
+            ref["right_out"][rows, :] = low
+            news = (gains, delta, low.astype(FULL))
+            sums = [old + jnp.sum(new, axis=0, keepdims=True) for old, new in zip(sums, news)]
+        for spot, total in zip((LN2_GAIN, LN2_BIAS, BIAS_OUT), sums):
+            ref["vec_own"][spot : spot + 1, :] = total
+        ref["left_out"][...] = ref["attended"][...].T
+        swap("out")
+
+    def attended_back():
+        for number in range(third):
+            columns = slice(number * 256, (number + 1) * 256)
+            ref["delta_attended"][:, columns] = dot_nt(ref["right_out"][...], ref["w_out_held"][columns, :]).astype(LOW)
+        ref["left_qkv"][...] = ref["normed_one"][...].T
+
+    def attend_back(pair):
         queries = ref["qkv"][:, head_columns(pair, 0)]
         keys = ref["qkv"][:, head_columns(pair, width)]
         values = ref["qkv"][:, head_columns(pair, 2 * width)]
@@ -780,81 +944,118 @@
                 totals[spot] = part if totals[spot] is None else totals[spot] + part
         for spot, total in enumerate(totals):
             ref["right_qkv"][:, head_columns(pair, spot * width)] = total.astype(LOW)
-        return carry
-
-    lax.fori_loop(0, HEADS // 2, attend_back, 0)
-    swap("qkv")
-    multiply("out")
-    for number in range(third):
-        columns = slice(number * 256, (number + 1) * 256)
-        part = dot_nt(ref["right_qkv"][...], ref["w_qkv_held"][columns, :])
-        ref["delta_normed"][:, columns] = part
-    for spot, first in ((BIAS_Q, 0), (BIAS_V, 2 * width)):
-        ref["vec_own"][spot : spot + 1, :] = jnp.sum(
-            ref["right_qkv"][:, first : first + width].astype(FULL), axis=0, keepdims=True
-        )
-    multiply("qkv")
-
-    def first_back(step, sums):
-        rows = pl.ds(pl.multiple_of(step * 64, 64), 64)
-        delta = ref["delta_normed"][rows, :]
-        row_term, gains = norm_rows_back(delta, ref["tokens"][rows, :].astype(FULL), ref["ln1_gain"][...])
-        ref["grad_tokens"][rows, :] = (ref["delta_block"][rows, :] + row_term).astype(LOW)
-        return tuple(old + jnp.sum(new, axis=0, keepdims=True) for old, new in zip(sums, (gains, delta)))
-
-    sums = lax.fori_loop(0, 4, first_back, (zeros, zeros))
-    for spot, total in zip((LN1_GAIN, LN1_BIAS), sums):
-        ref["vec_own"][spot : spot + 1, :] = total
-    ref["vec_held"][0] = ref["vec_own"][...]
-    begin(vec_copy(0))
-
-    for number, axis in enumerate(PEERS + ("self",)):
-        if axis == "self":
-            source = my_pos
-            arrived = ref["grid_out"][my_pos]
+        if pair == HEADS // 2 - 1:
+            swap("qkv")
+
+    def delta_first():
+        for number in range(third):
+            columns = slice(number * 256, (number + 1) * 256)
+            ref["delta_normed"][:, columns] = dot_nt(ref["right_qkv"][...], ref["w_qkv_held"][columns, :])
+        for spot, first in ((BIAS_Q, 0), (BIAS_V, 2 * width)):
+            ref["vec_own"][spot : spot + 1, :] = jnp.sum(
+                ref["right_qkv"][:, first : first + width].astype(FULL), axis=0, keepdims=True
+            )
+
+    def first_back():
+        sums = [jnp.zeros((1, width), FULL)] * 2
+        for step in range(4):
+            rows = slice(step * 64, (step + 1) * 64)
+            delta = ref["delta_normed"][rows, :]
+            row_term, gains = norm_rows_back(delta, ref["tokens"][rows, :].astype(FULL), row_of("ln1_gain"))
+            ref["grad_tokens_held"][rows, :] = (ref["delta_block"][rows, :] + row_term).astype(LOW)
+            sums = [old + jnp.sum(new, axis=0, keepdims=True) for old, new in zip(sums, (gains, delta))]
+        for spot, total in zip((LN1_GAIN, LN1_BIAS), sums):
+            ref["vec_own"][spot : spot + 1, :] = total
+        for number in range(ff // width):
+            ref["vec_own"][BIAS_UP + number : BIAS_UP + number + 1, :] = ref["bias_up_sum"][
+                :, number * width : (number + 1) * width
+            ]
+        mask_sum = jnp.zeros((8, ref["cot_wide"].shape[2]), FULL)
+        for number, axis in enumerate(PEERS + ("self",)):
+            source = my_pos if axis == "self" else peer(axis)[1]
+            cot = ref["cot_wide"][pl.ds(source * IMG_SEQ, IMG_SEQ)].reshape(IMG_SEQ * PLACES, -1)
+            seen = dot_nt(jnp.ones((8, IMG_SEQ * CAP), LOW), ref["placing"][number])
+            mask_sum = mask_sum + dot((1.0 - seen).astype(LOW), cot)
+        ref["vec_own"][MASK : MASK + 1, : mask_sum.shape[1]] = mask_sum[0:1]
+        ref["vec_held"][0] = ref["vec_own"][...]
+        begin(vec_copy(0))
+        keep("grad_tokens", 0)
+
+    def decode():
+        for number, axis in enumerate(PEERS + ("self",)):
+            if axis == "self":
+                source = my_pos
+                arrived_rows = ref["grid_out"][my_pos]
+            else:
+                source = peer(axis)[1]
+                remote(ref["grid_out"].at[source], ref["grid_in"].at[number], "grid", number, axis).wait_recv()
+                arrived_rows = ref["grid_in"][number]
+            placing = ref["placing"][number]
+            visible = jnp.sum(placing.astype(FULL), axis=1, keepdims=True)
+            filled = jnp.where(visible > 0.5, dot(placing, arrived_rows), row_of("mask_token").astype(FULL)).astype(LOW)
+            for image in range(IMG_SEQ):
+                ref["decoder_input_held"][source * IMG_SEQ + image] = filled[
+                    image * PLACES : image * PLACES + quarter_len
+                ]
+        keep("decoder_input", 1)
+
+    segments = {
+        "project": project,
+        "second_back": second_back,
+        "attended_back": attended_back,
+        "delta_first": delta_first,
+        "first_back": first_back,
+        "decode": decode,
+    }
+    for slot in range(4):
+        segments["feed%d" % slot] = functools.partial(feed, slot)
+        segments["multiply_feed%d" % slot] = functools.partial(multiply_feed, slot)
+    for pair in range(HEADS // 2):
+        segments["attend_back%d" % pair] = functools.partial(attend_back, pair)
+    for matrix in ("proj", "out", "qkv"):
+        segments["swapped_" + matrix] = functools.partial(swapped, matrix)
+    for job in JOBS:
+        segments["multiply_" + job] = functools.partial(multiply, job)
+    for step in PLAN:
+        if step[0] == "do":
+            segments[step[1]]()
+        elif step[0] == "vec":
+            arrive_vec(step[1])
         else:
-            source = peer(axis)[1]
-            remote(ref["grid_out"].at[source], ref["grid_in"].at[number], "grid", number, axis).wait_recv()
-            arrived = ref["grid_in"][number]
-        placing = ref["placing"][number]
-        visible = jnp.sum(placing.astype(FULL), axis=1, keepdims=True)
-        filled = jnp.where(visible > 0.5, dot(placing, arrived), ref["mask_token"][...].astype(FULL)).astype(LOW)
-        for image in range(IMG_SEQ):
-            ref["decoder_input"][source * IMG_SEQ + image] = filled[
-                image * PLACES : image * PLACES + quarter_len
-            ]
-
-    for spot, (number, stage) in enumerate(ORDER):
-        arrive(number, stage)
-        if spot % 6 == 5 and spot // 6 < 5:
-            arrive_vec(spot // 6)
-    for name in MATRICES:
-        rows = block_rows(name)
-        final, out = ref["final_" + name], ref["grad_" + name]
-        wide = final.shape[3]
-        for side in range(2):
-            for half in range(2):
-                piece = final[side, half]
-                if name == "down":
-                    out[(side * 2 + half) * rows : (side * 2 + half + 1) * rows, :] = piece
-                else:
-                    out[half * rows : (half + 1) * rows, side * wide : (side + 1) * wide] = piece
+            arrive(*step)
+    for store in stores:
+        store.wait()
     for copy in started:
         copy.wait_send()
 
 
-def finish_kernel(*refs):
-    ins, outs = refs[:8], refs[8:]
-    for source, target in zip(ins[:7], outs[:7]):
-        target[...] = source[...].astype(target.dtype)
-    sums = ins[7]
-    for spot, target in zip(
-        (LN1_GAIN, LN1_BIAS, BIAS_Q, BIAS_V, BIAS_OUT, LN2_GAIN, LN2_BIAS, BIAS_DOWN, BIAS_PROJ, MASK), outs[7:17]
+def finish_kernel(names, *refs):
+    ref = dict(zip(names, refs))
+    loads, stores = [], []
+    for number in range(7):
+        load = pltpu.make_async_copy(ref["in%d" % number], ref["low%d" % number], ref["load"].at[number])
+        load.start()
+        loads.append(load)
+    sums = ref["sums"]
+    for spot, number in zip(
+        (LN1_GAIN, LN1_BIAS, BIAS_Q, BIAS_V, BIAS_OUT, LN2_GAIN, LN2_BIAS, BIAS_DOWN, BIAS_PROJ, MASK), range(10)
     ):
-        target[...] = sums[spot : spot + 1, : target.shape[1]]
+        target = ref["vec%d" % number]
+        target[...] = sums[spot, : target.shape[0]]
     wide = sums.shape[1]
-    for number in range(outs[17].shape[1] // wide):
-        outs[17][:, number * wide : (number + 1) * wide] = sums[BIAS_UP + number : BIAS_UP + number + 1, :]
+    for number in range(ref["vec10"].shape[1] // wide):
+        ref["vec10"][:, number * wide : (number + 1) * wide] = sums[BIAS_UP + number : BIAS_UP + number + 1, :]
+    for number in range(7):
+        loads[number].wait()
+        source = ref["low%d" % number]
+        if number < 5:
+            source = ref["full%d" % number]
+            source[...] = ref["low%d" % number][...].astype(FULL)
+        store = pltpu.make_async_copy(source, ref["out%d" % number], ref["store"].at[number])
+        store.start()
+        stores.append(store)
+    for store in stores:
+        store.wait()
 
 
 def layer_device(
@@ -889,17 +1090,17 @@
         "tokens": tokens,
         "slot": row(image_slot),
         "position": row(patch_position),
-        "ln1_gain": row(ln1_gain),
-        "ln1_bias": row(ln1_bias),
-        "bias_query": row(bias_query),
-        "bias_value": row(bias_value),
-        "bias_out": row(bias_out),
-        "ln2_gain": row(ln2_gain),
-        "ln2_bias": row(ln2_bias),
+        "ln1_gain": ln1_gain,
+        "ln1_bias": ln1_bias,
+        "bias_query": bias_query,
+        "bias_value": bias_value,
+        "bias_out": bias_out,
+        "ln2_gain": ln2_gain,
+        "ln2_bias": ln2_bias,
         "bias_up": row(bias_up),
-        "bias_down": row(bias_down),
+        "bias_down": bias_down,
         "bias_proj": row(bias_proj),
-        "mask_token": row(mask_token),
+        "mask_token": mask_token,
         "cotangent": cotangent,
         "w_qkv": w_qkv,
         "w_out": w_out,
@@ -909,8 +1110,10 @@
     }
     lefts = {"down": ff, "up": width, "proj": width, "out": width, "qkv": width}
     rights = {"down": width, "up": ff, "proj": out_width, "out": width, "qkv": 3 * width}
-    results = {name: jax.ShapeDtypeStruct((lefts[name] // 8, rights[name]), LOW) for name in MATRICES}
-    outs = {"grad_" + name: results[name] for name in MATRICES}
+    outs = {}
+    for name in MATRICES:
+        block = (2, 2, 96) if name == "down" else (2, 48)
+        outs["grad_" + name] = jax.ShapeDtypeStruct(block + (rights[name],), LOW)
     outs["decoder_input"] = jax.ShapeDtypeStruct(cotangent.shape, LOW)
     outs["grad_tokens"] = jax.ShapeDtypeStruct(tokens.shape, LOW)
     outs["vec_sums"] = jax.ShapeDtypeStruct((16, width), FULL)
@@ -921,6 +1124,9 @@
         "w_proj_held": (w_proj.shape, LOW),
         "w_up_held": (w_up.shape, LOW),
         "w_down_held": (w_down.shape, LOW),
+        "cotangent_held": (cotangent.shape, LOW),
+        "decoder_input_held": (cotangent.shape, LOW),
+        "grad_tokens_held": (tokens.shape, LOW),
         "places": ((4, 8, rows), jnp.int32),
         "chosen": ((4, IMG_SEQ * CAP, rows), LOW),
         "placing": ((4, IMG_SEQ * PLACES, IMG_SEQ * CAP), LOW),
@@ -931,6 +1137,7 @@
         "grid_out": ((4, IMG_SEQ * CAP, out_width), LOW),
         "grid_in": ((3, IMG_SEQ * CAP, out_width), LOW),
         "normed": ((rows, width), LOW),
+        "normed_one": ((rows, width), LOW),
         "qkv": ((rows, 3 * width), LOW),
         "probs": ((HEADS, rows, rows), FULL),
         "attended": ((rows, width), LOW),
@@ -944,31 +1151,35 @@
         "vec_own": ((16, width), FULL),
         "vec_held": ((5, 16, width), FULL),
         "vec_in": ((5, 16, width), FULL),
+        "left_in_down": ((8, 192, rows), LOW),
+        "right_in_down": ((rows, width), LOW),
+        "right_in_up": ((4, rows, width // 2), LOW),
+        "final_down": ((2, 2, 96, width), LOW),
+        "final_up": ((4, 2, 2, 48, width // 2), LOW),
     }
     for name in MATRICES:
         room["left_" + name] = ((lefts[name], rows), LOW)
         room["right_" + name] = ((rows, rights[name]), LOW)
-        if name == "down":
-            room["left_in_down"] = ((8, 192, rows), LOW)
-            room["right_in_down"] = ((rows, rights[name]), LOW)
-            room["final_down"] = ((2, 2, 96, rights[name]), LOW)
-        else:
+        if name != "down":
             room["left_in_" + name] = ((lefts[name], rows), LOW)
+        if name in ("proj", "out", "qkv"):
             room["right_in_" + name] = ((rows, rights[name] // 2), LOW)
             room["final_" + name] = ((2, 2, 48, rights[name] // 2), LOW)
-    for number, (name, _, wide, _) in enumerate(JOBS):
-        block = (block_rows(name), wide)
-        room["partial%d" % number] = ((2, 2, 2, 2) + block, LOW)
+    for job, (name, _, _, wide, _) in JOBS.items():
+        block = (96 if name == "down" else 48, wide)
+        room["partial_" + job] = ((2, 2, 2, 2) + block, LOW)
         for stage in range(4):
-            room["landed%d_%d" % (number, stage)] = ((2,) * (3 - stage) + block, LOW)
+            room["landed_%s_%d" % (job, stage)] = ((2,) * (3 - stage) + block, LOW)
     scratch = {name: pltpu.VMEM(shape, dtype) for name, (shape, dtype) in room.items()}
-    scratch["load"] = dma((5,))
+    scratch["load"] = dma((6,))
+    scratch["keep"] = dma((2,))
+    scratch["store"] = dma((len(JOBS), 2))
     for kind, shape in (
         ("place", (3,)),
         ("back", (3,)),
         ("grid", (3,)),
-        ("core", (5, 2)),
-        ("job", (len(JOBS), 6)),
+        ("core", (8, 2)),
+        ("job", (len(JOBS), 7)),
         ("vec", (5,)),
     ):
         scratch[kind + "_send"] = dma(shape)
@@ -977,8 +1188,8 @@
     found = pl.pallas_call(
         functools.partial(layer_kernel, names),
         out_shape=list(outs.values()),
-        in_specs=[hbm if name.startswith("w_") else vmem for name in inputs],
-        out_specs=[vmem] * len(outs),
+        in_specs=[hbm if name.startswith("w_") or name == "cotangent" else vmem for name in inputs],
+        out_specs=[vmem if name == "vec_sums" else hbm for name in outs],
         scratch_shapes=list(scratch.values()),
         compiler_params=pltpu.CompilerParams(
             collective_id=0, has_side_effects=True, vmem_limit_bytes=63 * 2**20
@@ -986,23 +1197,32 @@
         name="layer",
     )(*inputs.values())
     found = dict(zip(outs, found))
-    sources = [found["grad_" + name] for name in MATRICES] + [found["decoder_input"], found["grad_tokens"]]
-    shapes = [jax.ShapeDtypeStruct(source.shape, FULL) for source in sources[:5]]
-    shapes += [jax.ShapeDtypeStruct(source.shape, LOW) for source in sources[5:]]
-    vec_width = [width] * 8 + [out_width] * 2 + [ff]
-    shapes += [jax.ShapeDtypeStruct((1, wide), FULL) for wide in vec_width]
+    sources = [found["grad_" + name].reshape(-1, rights[name]) for name in MATRICES]
+    sources += [found["decoder_input"], found["grad_tokens"]]
+    operands = {"in%d" % number: source for number, source in enumerate(sources)}
+    operands["sums"] = found["vec_sums"]
+    results = {}
+    for number, source in enumerate(sources):
+        results["out%d" % number] = jax.ShapeDtypeStruct(source.shape, FULL if number < 5 else LOW)
+    for number, wide in enumerate([width] * 8 + [out_width] * 2):
+        results["vec%d" % number] = jax.ShapeDtypeStruct((wide,), FULL)
+    results["vec10"] = jax.ShapeDtypeStruct((1, ff), FULL)
+    held = {"low%d" % number: pltpu.VMEM(source.shape, LOW) for number, source in enumerate(sources)}
+    held.update({"full%d" % number: pltpu.VMEM(source.shape, FULL) for number, source in enumerate(sources[:5])})
+    held["load"] = dma((7,))
+    held["store"] = dma((7,))
     done = pl.pallas_call(
-        finish_kernel,
-        out_shape=shapes,
-        in_specs=[vmem] * 8,
-        out_specs=[vmem] * len(shapes),
-        compiler_params=pltpu.CompilerParams(vmem_limit_bytes=40 * 2**20),
+        functools.partial(finish_kernel, tuple(operands) + tuple(results) + tuple(held)),
+        out_shape=list(results.values()),
+        in_specs=[hbm] * 7 + [vmem],
+        out_specs=[hbm] * 7 + [vmem] * 11,
+        scratch_shapes=list(held.values()),
+        compiler_params=pltpu.CompilerParams(vmem_limit_bytes=60 * 2**20),
         name="finish",
-    )(*sources, found["vec_sums"])
+    )(*operands.values())
     down, up, proj, out, qkv, decoder_input, grad_tokens = done[:7]
-    gain1, bias1, b_query, b_value, b_out, gain2, bias2, b_down, b_proj, mask, b_up = [
-        vec.reshape(-1) for vec in done[7:]
-    ]
+    gain1, bias1, b_query, b_value, b_out, gain2, bias2, b_down, b_proj, mask, b_up = done[7:]
+    b_up = b_up.reshape(-1)
     return (
         decoder_input,
         grad_tokens,

time: 144 us -> 96.9 us (0.67); the launches traced: 142 us -> 96.7 us
  Pallas kernels: 117 us -> 95.9 us
  local copies, waits for them, and re-layouts: 19.4 us -> 0 us
  other arithmetic: 4.84 us -> 0 us
    pallas_call x1, Pallas kernels: 114 us -> 90.8 us  [layer_device(): pl.pallas_call(functools.partial(layer_kernel, names), out_shape=list(out...]
    reshape x9 -> x0, local copies, waits for them, and re-layouts: 11.4 us -> none  [layer_device(): row = lambda vec: vec.reshape(1, -1)]
    unnamed x16 -> x0, local copies, waits for them, and re-layouts: 7.99 us -> none
    pallas_call x8 -> x0, other arithmetic: 4.84 us -> none  [layer_device(): pl.pallas_call(finish_kernel, out_shape=shapes, in_specs=[vmem] * 8, out_...]
    pallas_call x1, Pallas kernels: 2.69 us -> 5.07 us  [layer_device(): pl.pallas_call(functools.partial(finish_kernel, tuple(operands) + tuple(r...]
where the time goes in v3:
time: 96.9 us; the launch traced here: 96.7 us
  Pallas kernels  95.9 us (99%)
    pallas_call x1, Pallas kernels, layer_device(): pl.pallas_call(functools.partial(layer_kernel, names), out_shape=list(out...  90.8 us
    pallas_call x1, Pallas kernels, layer_device(): pl.pallas_call(functools.partial(finish_kernel, tuple(operands) + tuple(r...  5.07 us

profile of v3, /device:TPU:1, one launch (start us, length us, event | category | flops | bytes accessed | tf_op | source)
XLA Modules:
  0.0 96.7 jit_solution(12046690233611469785)
XLA Ops:
  0.7 90.8 %layer.1 = (bf16[2,2,96,768]{3,2,1,0:T(8,128)(2,1)}, bf16[2,48,3072]{2,1,0:T(8,128)(2,1)}, bf16[2,48,512]{2,1,0:T(8,128)(2,1)}, bf16[2,48,768]{2,1,0:T(8,128)(2,...) custom-call(bf16[256,768]{1,0:T(8,128)(2,1)} %refs_0_.1, ...), custom_call_target="tpu_custom_call" | custom-call | tf_op jit(solution)/shard_map/layer/pallas_call | solution.py:1188
  91.5 5.1 %finish.1 = (f32[384,768]{1,0:T(8,128)}, f32[96,3072]{1,0:T(8,128)}, f32[96,512]{1,0:T(8,128)}, f32[96,768]{1,0:T(8,128)}, f32[96,2304]{1,0:T(8,128)}, /*index=5...) custom-call(bf16[384,768]{1,0:T(8,128)(2,1)} %bitcast.10, ...), custom_call_target="tpu_custom_call" | custom-call | tf_op jit(solution)/shard_map/finish/pallas_call | solution.py:1214

commit v4 on v3

--- a/solution.py
+++ b/solution.py
@@ -274,135 +274,199 @@
 AXES = ("zh", "zl", "x", "y")
 MATRICES = ("down", "up", "proj", "out", "qkv")
 JOBS = {
-    "down0": ("down", None, 0, 256, ("zl", "y", "zh", "x")),
-    "down1": ("down", None, 256, 256, ("zl", "zh", "x", "y")),
-    "down2": ("down", None, 512, 256, ("zl", "y", "x", "zh")),
-    "up0": ("up", 0, 0, 384, ("x", "y", "zl", "zh")),
-    "up1": ("up", 1, 0, 384, ("x", "y", "zl", "zh")),
-    "up2": ("up", 2, 0, 384, ("x", "y", "zl", "zh")),
-    "up3": ("up", 3, 0, 384, ("x", "y", "zl", "zh")),
-    "proj0": ("proj", None, 0, 256, ("y", "zl", "x", "zh")),
-    "out0": ("out", None, 0, 384, ("x", "y", "zl", "zh")),
-    "qkv0": ("qkv", None, 0, 384, ("x", "y", "zl", "zh")),
-    "qkv1": ("qkv", None, 384, 384, ("y", "zl", "zh", "x")),
-    "qkv2": ("qkv", None, 768, 384, ("x", "y", "zl", "zh")),
+    "down0": ("down", None, 0, 256, ("zl", "zh", "y")),
+    "down1": ("down", None, 256, 256, ("zl", "y", "zh")),
+    "down2": ("down", None, 512, 256, ("zl", "y", "zh")),
+    "up0a": ("up", 0, 0, 256, ("y", "x", "zl", "zh")),
+    "up0b": ("up", 0, 256, 128, ("zl", "zh", "y", "x")),
+    "up1a": ("up", 1, 0, 256, ("y", "x", "zl", "zh")),
+    "up1b": ("up", 1, 256, 128, ("zl", "zh", "y", "x")),
+    "up2a": ("up", 2, 0, 256, ("y", "x", "zl", "zh")),
+    "up2b": ("up", 2, 256, 128, ("zl", "zh", "y", "x")),
+    "up3a": ("up", 3, 0, 256, ("y", "x", "zl", "zh")),
+    "up3b": ("up", 3, 256, 128, ("zl", "zh", "y", "x")),
+    "proj0": ("proj", None, 0, 256, ("zl", "x", "y", "zh")),
+    "out0": ("out", None, 0, 384, ("y", "x", "zl", "zh")),
+    "qkv0": ("qkv", None, 0, 256, ("y", "zl", "x", "zh")),
+    "qkv1": ("qkv", None, 256, 256, ("x", "y", "zl", "zh")),
+    "qkv2": ("qkv", None, 512, 256, ("y", "x", "zl", "zh")),
+    "qkv3": ("qkv", None, 768, 256, ("x", "y", "zl", "zh")),
+    "qkv4": ("qkv", None, 1024, 128, ("x", "y", "zl", "zh")),
 }
 PLAN = (
     ("do", "feed0"),
     ("do", "feed1"),
-    ("do", "multiply_feed0"),
     ("do", "feed2"),
-    ("do", "multiply_feed1"),
     ("do", "feed3"),
-    ("do", "multiply_feed2"),
     ("do", "project"),
-    ("down0", 0, "a"),
-    ("do", "multiply_feed3"),
-    ("up0", 0, ""),
+    ("do", "delta"),
+    ("do", "feed_back0"),
+    ("do", "feed_back1"),
+    ("do", "feed_back2"),
+    ("do", "feed_back3"),
+    ("do", "swapped_proj_left"),
+    ("do", "swapped_proj_right"),
+    ("do", "multiply_proj0"),
+    ("do", "multiply_up0"),
+    ("do", "multiply_up1"),
+    ("do", "multiply_up2"),
+    ("do", "multiply_up3"),
     ("do", "second_back"),
-    ("down1", 0, "a"),
-    ("do", "swapped_proj"),
-    ("do", "multiply_proj0"),
     ("do", "attended_back"),
+    ("do", "transposes"),
     ("do", "attend_back0"),
     ("do", "attend_back1"),
     ("do", "attend_back2"),
+    ("proj0", 0, ""),
     ("do", "attend_back3"),
-    ("up0", 1, ""),
-    ("down2", 0, "a"),
-    ("up1", 0, ""),
+    ("up0a", 0, ""),
     ("do", "attend_back4"),
     ("do", "attend_back5"),
-    ("do", "swapped_out"),
+    ("up1b", 0, ""),
+    ("do", "swapped_out_left"),
+    ("do", "swapped_out_right"),
     ("do", "multiply_out0"),
+    ("do", "pass_delta"),
     ("do", "delta_first"),
-    ("proj0", 0, ""),
-    ("down0", 0, "b"),
-    ("do", "swapped_qkv"),
+    ("do", "first_back"),
+    ("up0b", 0, ""),
+    ("up1a", 0, ""),
+    ("do", "swapped_qkv_left"),
+    ("do", "swapped_qkv_right"),
     ("do", "multiply_qkv0"),
     ("do", "multiply_qkv1"),
     ("do", "multiply_qkv2"),
-    ("up2", 0, ""),
-    ("up1", 1, ""),
-    ("do", "first_back"),
+    ("do", "multiply_qkv3"),
+    ("do", "multiply_qkv4"),
+    ("up3b", 0, ""),
+    ("vec", 0),
+    ("do", "decode"),
+    ("up2b", 0, ""),
+    ("up2a", 0, ""),
+    ("do", "multiply_down0"),
+    ("do", "multiply_down1"),
+    ("do", "multiply_down2"),
+    ("do", "multiply_down3"),
+    ("up3b", 1, ""),
+    ("proj0", 1, ""),
+    ("up3a", 0, ""),
+    ("up2b", 1, ""),
+    ("down0", 0, "a"),
+    ("up0a", 1, ""),
+    ("up1b", 1, ""),
+    ("down1", 0, "a"),
+    ("up1a", 1, ""),
+    ("up0b", 1, ""),
+    ("down2", 0, "a"),
+    ("out0", 0, ""),
+    ("down0", 0, "b"),
+    ("qkv1", 0, ""),
     ("down1", 0, "b"),
-    ("do", "decode"),
-    ("vec", 0),
-    ("down0", 1, ""),
+    ("qkv0", 0, ""),
     ("down2", 0, "b"),
-    ("up3", 0, ""),
-    ("qkv1", 0, ""),
-    ("up1", 2, ""),
-    ("out0", 0, ""),
-    ("proj0", 1, ""),
-    ("up2", 1, ""),
-    ("down1", 1, ""),
-    ("up0", 2, ""),
-    ("down2", 1, ""),
-    ("qkv0", 0, ""),
-    ("down0", 2, ""),
-    ("qkv1", 1, ""),
-    ("up3", 1, ""),
-    ("up3", 2, ""),
-    ("up3", 3, ""),
-    ("out0", 1, ""),
+    ("qkv3", 0, ""),
+    ("qkv4", 0, ""),
     ("qkv2", 0, ""),
     ("vec", 1),
+    ("up1a", 2, ""),
+    ("up3b", 2, ""),
+    ("up0a", 2, ""),
     ("proj0", 2, ""),
-    ("up2", 2, ""),
-    ("up2", 3, ""),
+    ("up2b", 2, ""),
+    ("up2a", 1, ""),
+    ("down0", 1, ""),
+    ("up1b", 2, ""),
+    ("up0b", 2, ""),
     ("qkv0", 1, ""),
-    ("up3", 4, ""),
+    ("up3a", 1, ""),
+    ("qkv1", 1, ""),
+    ("up3a", 2, ""),
+    ("up3a", 3, ""),
+    ("down1", 1, ""),
+    ("up2a", 2, ""),
+    ("up2a", 3, ""),
+    ("out0", 1, ""),
+    ("proj0", 3, ""),
     ("qkv1", 2, ""),
+    ("down2", 1, ""),
+    ("qkv2", 1, ""),
+    ("up3b", 3, ""),
+    ("up2b", 3, ""),
+    ("up1b", 3, ""),
+    ("up1a", 3, ""),
+    ("up0b", 3, ""),
+    ("qkv3", 1, ""),
+    ("qkv0", 2, ""),
+    ("out0", 2, ""),
+    ("qkv4", 1, ""),
     ("down1", 2, ""),
-    ("out0", 2, ""),
-    ("up1", 3, ""),
-    ("up3", 5, ""),
+    ("vec", 2),
+    ("up0a", 3, ""),
+    ("down0", 2, ""),
+    ("up3a", 4, ""),
+    ("qkv1", 3, ""),
+    ("qkv2", 2, ""),
+    ("up2a", 4, ""),
+    ("proj0", 4, ""),
+    ("up3b", 4, ""),
+    ("qkv3", 2, ""),
+    ("up2b", 4, ""),
+    ("up1b", 4, ""),
+    ("up3a", 5, ""),
+    ("up1a", 4, ""),
     ("down2", 2, ""),
-    ("proj0", 3, ""),
-    ("qkv2", 1, ""),
-    ("down0", 3, ""),
-    ("qkv0", 2, ""),
-    ("vec", 2),
-    ("up0", 3, ""),
-    ("qkv1", 3, ""),
-    ("up2", 4, ""),
-    ("down1", 3, ""),
+    ("up0b", 4, ""),
+    ("up2a", 5, ""),
+    ("proj0", 5, ""),
+    ("qkv4", 2, ""),
+    ("up3b", 5, ""),
+    ("qkv0", 3, ""),
+    ("down1", 4, ""),
+    ("up2b", 5, ""),
+    ("vec", 3),
+    ("up1b", 5, ""),
+    ("up0a", 4, ""),
+    ("up1a", 5, ""),
+    ("up0b", 5, ""),
     ("out0", 3, ""),
-    ("up1", 4, ""),
-    ("proj0", 4, ""),
-    ("qkv2", 2, ""),
-    ("up2", 5, ""),
     ("down0", 4, ""),
-    ("down2", 3, ""),
-    ("up0", 4, ""),
-    ("up1", 5, ""),
-    ("vec", 3),
-    ("proj0", 5, ""),
     ("qkv1", 4, ""),
-    ("qkv0", 3, ""),
+    ("down1", 5, ""),
+    ("qkv2", 3, ""),
+    ("up0a", 5, ""),
+    ("down2", 4, ""),
+    ("qkv3", 3, ""),
+    ("qkv0", 4, ""),
     ("down0", 5, ""),
-    ("down1", 4, ""),
-    ("up0", 5, ""),
+    ("qkv4", 3, ""),
+    ("qkv1", 5, ""),
     ("out0", 4, ""),
-    ("qkv2", 3, ""),
-    ("qkv1", 5, ""),
-    ("down2", 4, ""),
-    ("qkv0", 4, ""),
-    ("down1", 5, ""),
-    ("out0", 5, ""),
+    ("qkv2", 4, ""),
     ("vec", 4),
-    ("qkv2", 4, ""),
     ("down2", 5, ""),
     ("qkv0", 5, ""),
+    ("qkv3", 4, ""),
+    ("qkv4", 4, ""),
+    ("out0", 5, ""),
     ("qkv2", 5, ""),
+    ("vec", 5),
+    ("qkv3", 5, ""),
+    ("qkv4", 5, ""),
 )
-VEC_STEPS = ("core", "x", "y", "zl", "zh")
-PEERS = ("y", "core", "diagonal")
+VEC_STEPS = ("core", "x", "y", "zl", "zh", "core")
+PEERS = ("diagonal", "y", "core")
 PLACES = 64
+INPUTS = (
+    "slot", "position", "ln1_gain", "ln1_bias", "tokens", "w_qkv", "cotangent", "bias_query", "bias_value", "w_out",
+    "bias_out", "ln2_gain", "ln2_bias", "bias_up", "w_up", "w_down", "bias_down", "w_proj", "bias_proj", "mask_token",
+)
 LN1_GAIN, LN1_BIAS, BIAS_Q, BIAS_V, BIAS_OUT, LN2_GAIN, LN2_BIAS, BIAS_DOWN, BIAS_UP, BIAS_PROJ, MASK = (
     0, 1, 2, 3, 4, 5, 6, 7, 8, 12, 13,
 )
+
+
+def axes_of(matrix):
+    return ("zh", "zl", "y") if matrix == "down" else AXES
 
 
 def device_coords():
@@ -452,18 +516,20 @@
     ref = dict(zip(names, refs))
 
     def row_of(name, columns=slice(None)):
-        return ref[name][...].reshape(1, -1)[:, columns]
+        return ref[name + "_held"][...].reshape(1, -1)[:, columns]
 
     me = device_coords()
     core = me["core"]
     my_pos = me["y"] * 2 + core
-    width = ref["tokens"].shape[1]
+    width = ref["tokens_held"].shape[1]
     ff = ref["w_up"].shape[1]
     quarter_len = POSITIONS // 4
 
     def peer(axis):
         if axis == "diagonal":
             return device_of({**me, "y": 1 - me["y"], "core": 1 - core})
+        if axis == "across":
+            return device_of({**me, "x": 1 - me["x"], "core": 1 - core})
         return device_of({**me, axis: 1 - me[axis]})
 
     started = []
@@ -482,34 +548,39 @@
         copy.start()
         started.append(copy)
 
+    barrier = pltpu.get_barrier_semaphore()
+    for axis in AXES + ("core", "diagonal", "across"):
+        pl.semaphore_signal(barrier, inc=1, device_id=peer(axis), device_id_type=MESH_ID)
+
     loads = {}
-    for number, name in enumerate(("w_qkv", "cotangent", "w_out", "w_proj", "w_up", "w_down")):
+    for number, name in enumerate(INPUTS):
         loads[name] = pltpu.make_async_copy(ref[name], ref[name + "_held"], ref["load"].at[number])
         loads[name].start()
 
-    barrier = pltpu.get_barrier_semaphore()
-    for axis in AXES + ("core", "diagonal"):
-        pl.semaphore_signal(barrier, inc=1, device_id=peer(axis), device_id_type=MESH_ID)
-
-    ref["places"][my_pos, 0:1, :] = ref["slot"][...]
-    ref["places"][my_pos, 1:2, :] = ref["position"][...]
+    def loaded(*which):
+        for name in which:
+            loads[name].wait()
+
+    loaded("slot", "position", "tokens", "ln1_gain", "ln1_bias")
+    ref["places"][my_pos, 0:1, :] = row_of("slot")
+    ref["places"][my_pos, 1:2, :] = row_of("position")
 
     def first_norm(step, carry):
         rows = pl.ds(pl.multiple_of(step * 64, 64), 64)
-        xhat, _ = normalised(ref["tokens"][rows, :].astype(FULL))
+        xhat, _ = normalised(ref["tokens_held"][rows, :].astype(FULL))
         ref["normed"][rows, :] = (xhat * row_of("ln1_gain") + row_of("ln1_bias")).astype(LOW)
         return carry
 
     lax.fori_loop(0, 4, first_norm, 0, unroll=4)
 
-    pl.semaphore_wait(barrier, 6)
-    for number, axis in enumerate(PEERS):
-        begin(remote(ref["places"].at[my_pos], ref["places"].at[my_pos], "place", number, axis))
-
-    loads["w_qkv"].wait()
+    loaded("w_qkv", "bias_query", "bias_value")
     third = width // 256
     for number in range(3 * third):
         columns = slice(number * 256, (number + 1) * 256)
+        if number == 6:
+            pl.semaphore_wait(barrier, 7)
+            for spot, axis in enumerate(PEERS):
+                begin(remote(ref["places"].at[my_pos], ref["places"].at[my_pos], "place", spot, axis))
         part = dot(ref["normed"][...], ref["w_qkv_held"][:, columns])
         if number < third:
             part = part + row_of("bias_query", columns)
@@ -536,37 +607,11 @@
         return chosen.astype(LOW), jnp.where(inside, slot * PLACES + offset, -1)
 
     for quarter in range(4):
-        chosen, _ = picked(ref["slot"][...], ref["position"][...], quarter)
+        chosen, _ = picked(row_of("slot"), row_of("position"), quarter)
         ref["chosen"][quarter] = chosen
 
-    slots = one_hot(8, ref["slot"][...] + 1).astype(LOW)
+    slots = one_hot(8, row_of("slot") + 1).astype(LOW)
     ref["allowed"][...] = jnp.where(dot_tn(slots, slots) > 0.5, 0.0, NEGATIVE)
-
-    ref["cot_wide"][...] = jnp.zeros_like(ref["cot_wide"])
-    loads["cotangent"].wait()
-    for image in range(4 * IMG_SEQ):
-        ref["cot_wide"][image, 0:quarter_len, :] = ref["cotangent_held"][image]
-    for number, axis in enumerate(PEERS + ("self",)):
-        if axis == "self":
-            source = my_pos
-        else:
-            source = peer(axis)[1]
-            remote(ref["places"].at[source], ref["places"].at[source], "place", number, axis).wait_recv()
-        slot = ref["places"][source, 0:1, :]
-        position = ref["places"][source, 1:2, :]
-        chosen, place = picked(slot, position, my_pos)
-        filled = one_hot(IMG_SEQ * PLACES, place).astype(LOW)
-        placing = dot_nt(filled, chosen)
-        placing_low = placing.astype(LOW)
-        ref["placing"][number] = placing_low
-        cot = ref["cot_wide"][pl.ds(source * IMG_SEQ, IMG_SEQ)].reshape(IMG_SEQ * PLACES, -1)
-        back = dot_tn(placing_low, cot).astype(LOW)
-        if axis == "self":
-            ref["back_in"][my_pos] = back
-        else:
-            ref["back_out"][number] = back
-            begin(remote(ref["back_out"].at[number], ref["back_in"].at[my_pos], "back", number, axis))
-    ref["vec_own"][...] = jnp.zeros_like(ref["vec_own"])
 
     lane = lax.broadcasted_iota(jnp.int32, (1, 2 * HEAD_DIM), 1)
     sides_full = [(lane < HEAD_DIM).astype(FULL), (lane >= HEAD_DIM).astype(FULL)]
@@ -593,11 +638,36 @@
     for pair in range(HEADS // 2):
         attend(pair, 0)
 
-    loads["w_out"].wait()
+    ref["cot_wide"][...] = jnp.zeros_like(ref["cot_wide"])
+    loaded("cotangent")
+    for image in range(4 * IMG_SEQ):
+        ref["cot_wide"][image, 0:quarter_len, :] = ref["cotangent_held"][image]
+    for number, axis in enumerate(PEERS):
+        source = peer(axis)[1]
+        remote(ref["places"].at[source], ref["places"].at[source], "place", number, axis).wait_recv()
+    for number, axis in enumerate(PEERS + ("self",)):
+        source = my_pos if axis == "self" else peer(axis)[1]
+        slot = ref["places"][source, 0:1, :]
+        position = ref["places"][source, 1:2, :]
+        chosen, place = picked(slot, position, my_pos)
+        filled = one_hot(IMG_SEQ * PLACES, place).astype(LOW)
+        placing = dot_nt(filled, chosen).astype(LOW)
+        ref["placing"][number] = placing
+        cot = ref["cot_wide"][pl.ds(source * IMG_SEQ, IMG_SEQ)].reshape(IMG_SEQ * PLACES, -1)
+        back = dot_tn(placing, cot).astype(LOW)
+        if axis == "self":
+            ref["back_in"][my_pos] = back
+        else:
+            ref["back_out"][number] = back
+    for number, axis in enumerate(PEERS):
+        begin(remote(ref["back_out"].at[number], ref["back_in"].at[my_pos], "back", number, axis))
+    ref["vec_own"][...] = jnp.zeros_like(ref["vec_own"])
+
+    loaded("w_out", "bias_out")
     for number in range(third):
         columns = slice(number * 256, (number + 1) * 256)
         ref["residual"][:, columns] = (
-            ref["tokens"][:, columns].astype(FULL)
+            ref["tokens_held"][:, columns].astype(FULL)
             + dot(ref["attended"][...], ref["w_out_held"][:, columns])
             + row_of("bias_out", columns)
         )
@@ -608,27 +678,35 @@
         ref["normed"][rows, :] = (xhat * row_of("ln2_gain") + row_of("ln2_bias")).astype(LOW)
         return carry
 
+    loaded("ln2_gain", "ln2_bias")
     lax.fori_loop(0, 4, second_norm, 0, unroll=4)
     ref["left_up"][...] = ref["normed"][...].T
 
-    loads["w_proj"].wait()
-    for number, axis in enumerate(PEERS):
-        remote(ref["back_out"].at[number], ref["back_in"].at[my_pos], "back", number, axis).wait_recv()
-    chosen_all = ref["chosen"][...].reshape(4 * IMG_SEQ * CAP, ROWS_SEQ)
-    returned = ref["back_in"][...].reshape(4 * IMG_SEQ * CAP, -1)
-    delta_proj = dot_tn(chosen_all, returned)
-    ref["vec_own"][BIAS_PROJ : BIAS_PROJ + 1, : delta_proj.shape[1]] = jnp.sum(delta_proj, axis=0, keepdims=True)
-    ref["right_proj"][...] = delta_proj.astype(LOW)
-    for number in range(third):
-        columns = slice(number * 256, (number + 1) * 256)
-        part = dot_nt(ref["right_proj"][...], ref["w_proj_held"][columns, :])
-        ref["delta_block"][:, columns] = part
-        part = part.astype(LOW)
-        ref["right_down"][:, columns] = part
-        ref["vec_own"][BIAS_DOWN : BIAS_DOWN + 1, columns] = jnp.sum(part.astype(FULL), axis=0, keepdims=True)
-
-    loads["w_up"].wait()
-    loads["w_down"].wait()
+    def delta():
+        for number, axis in enumerate(PEERS):
+            remote(ref["back_out"].at[number], ref["back_in"].at[my_pos], "back", number, axis).wait_recv()
+        chosen_all = ref["chosen"][...].reshape(4 * IMG_SEQ * CAP, ROWS_SEQ)
+        returned = ref["back_in"][...].reshape(4 * IMG_SEQ * CAP, -1)
+        delta_proj = dot_tn(chosen_all, returned)
+        ref["vec_own"][BIAS_PROJ : BIAS_PROJ + 1, : delta_proj.shape[1]] = jnp.sum(delta_proj, axis=0, keepdims=True)
+        ref["right_proj"][...] = delta_proj.astype(LOW)
+        for number in range(third):
+            columns = slice(number * 256, (number + 1) * 256)
+            part = dot_nt(ref["right_proj"][...], ref["w_proj_held"][columns, :])
+            ref["delta_block"][:, columns] = part
+            part = part.astype(LOW)
+            ref["right_down"][:, columns] = part
+            ref["vec_own"][BIAS_DOWN : BIAS_DOWN + 1, columns] = jnp.sum(part.astype(FULL), axis=0, keepdims=True)
+        for which in ("delta_side", "delta_across", "side2", "across2", "side3", "across3", "delta", "proj_right"):
+            swap(which)
+
+    def pass_delta():
+        for which, later in (("delta_side", "on_side"), ("delta_across", "on_across")):
+            swapped(which)
+            swap(later)
+
+    loaded("w_up", "bias_up")
+    ref["bias_up_row"][...] = row_of("bias_up")
 
     def chunk_of(slot):
         high = 1 - me["zh"] if slot < 2 else me["zh"]
@@ -640,57 +718,93 @@
 
     def feed(slot):
         columns = chunk_columns(slot)
-        up = dot(ref["normed"][...], ref["w_up_held"][:, columns]) + ref["bias_up"][:, columns]
+        up = dot(ref["normed"][...], ref["w_up_held"][:, columns]) + ref["bias_up_row"][:, columns]
         square = up * up
         bent = jnp.tanh(GELU_COEF * (up + 0.044715 * up * square))
         half = 0.5 * (1.0 + bent)
-        slope = half + 0.5 * up * (1.0 - bent * bent) * (GELU_COEF * (1.0 + 0.134145 * square))
+        ref["slope"][slot] = half + 0.5 * up * (1.0 - bent * bent) * (GELU_COEF * (1.0 + 0.134145 * square))
         hidden = (up * half).astype(LOW)
         ref["left_down"][columns, :] = hidden.T
+        swap("hidden%d" % slot)
+        if slot < 2:
+            swap("side%d" % slot)
+            swap("across%d" % slot)
+        if slot == 0:
+            loaded("w_down", "bias_down")
+        out = dot(hidden, ref["w_down_held"][columns, :])
+        if slot == 0:
+            ref["mlp_out"][...] = out
+        else:
+            ref["mlp_out"][...] += out
+
+    def feed_back(slot):
+        columns = chunk_columns(slot)
         back = dot_nt(ref["right_down"][...], ref["w_down_held"][columns, :])
-        delta_up = (back * slope).astype(LOW)
+        delta_up = (back * ref["slope"][slot]).astype(LOW)
         ref["right_up"][:, columns] = delta_up
-        for copy in swap_copies("feed%d" % slot):
-            begin(copy)
+        swap("feed%d" % slot)
         ref["bias_up_sum"][:, columns] = jnp.sum(delta_up.astype(FULL), axis=0, keepdims=True)
-        out = dot(hidden, ref["w_down_held"][columns, :])
         delta = dot_nt(delta_up, ref["w_up_held"][:, columns])
         if slot == 0:
-            ref["mlp_out"][...] = out
             ref["delta_normed"][...] = delta
         else:
-            ref["mlp_out"][...] += out
             ref["delta_normed"][...] += delta
 
-    swaps = ("early", "feed0", "feed1", "feed2", "feed3", "proj", "out", "qkv")
-
-    def swap_copies(which):
+    swaps = ("norm", "delta", "proj_left", "proj_right", "out_left", "out_right", "qkv_left", "qkv_right")
+    swaps += tuple("hidden%d" % slot for slot in range(4)) + tuple("feed%d" % slot for slot in range(4))
+    swaps += tuple("side%d" % slot for slot in range(4)) + tuple("across%d" % slot for slot in range(4))
+    swaps += ("delta_side", "delta_across", "on_side", "on_across")
+
+    def swap_copy(which):
         other = 1 - core
-        if which == "early":
-            pairs = ((ref["left_up"], ref["left_in_up"]), (ref["right_down"], ref["right_in_down"]))
+        axis = "core"
+        half = width // 2
+        if which == "norm":
+            source, target = ref["left_up"], ref["left_in_up"]
+        elif which == "delta":
+            source, target = ref["right_down"], ref["right_in_down"].at[0]
+        elif which == "delta_side":
+            source, target = ref["right_down"].at[:, pl.ds(0, half)], ref["right_in_down"].at[1, :, pl.ds(0, half)]
+            axis = "x"
+        elif which == "delta_across":
+            source, target = ref["right_down"].at[:, pl.ds(half, half)], ref["right_in_down"].at[2, :, pl.ds(half, half)]
+            axis = "across"
+        elif which == "on_side":
+            source = ref["right_in_down"].at[1, :, pl.ds(0, half)]
+            target = ref["right_in_down"].at[2, :, pl.ds(0, half)]
+        elif which == "on_across":
+            source = ref["right_in_down"].at[2, :, pl.ds(half, half)]
+            target = ref["right_in_down"].at[1, :, pl.ds(half, half)]
+        elif which[:-1] in ("hidden", "side", "across"):
+            chunk = chunk_of(int(which[-1]))[2]
+            blocks = ref["left_down"].reshape(8, 2, 192, ROWS_SEQ)
+            if which.startswith("hidden"):
+                source, target = blocks.at[chunk * 2 + me["x"], other], ref["left_in_down"].at[0, chunk]
+            elif which.startswith("side"):
+                source, target = blocks.at[chunk * 2 + 1 - me["x"], core], ref["left_in_down"].at[1, chunk]
+                axis = "x"
+            else:
+                source, target = blocks.at[chunk * 2 + 1 - me["x"], other], ref["left_in_down"].at[2, chunk]
+                axis = "across"
         elif which.startswith("feed"):
             slot = int(which[4:])
-            _, _, chunk = chunk_of(slot)
-            left = ref["left_down"].reshape(8, 2, 192, ROWS_SEQ)
-            right = ref["right_up"].at[:, chunk_columns(slot, other * (width // 2), width // 2)]
-            pairs = (
-                (left.at[pl.ds(chunk * 2, 2), other], ref["left_in_down"].at[pl.ds(chunk * 2, 2)]),
-                (right, ref["right_in_up"].at[slot]),
-            )
+            source = ref["right_up"].at[:, chunk_columns(slot, other * half, half)]
+            target = ref["right_in_up"].at[slot]
         else:
-            wide = ref["right_" + which].shape[1] // 2
-            right = ref["right_" + which].at[:, pl.ds(pl.multiple_of(other * wide, 128), wide)]
-            pairs = ((ref["left_" + which], ref["left_in_" + which]), (right, ref["right_in_" + which]))
-        spot = swaps.index(which)
-        return [remote(source, target, "core", (spot, part), "core") for part, (source, target) in enumerate(pairs)]
+            matrix, side = which.split("_")
+            if side == "left":
+                source, target = ref["left_" + matrix], ref["left_in_" + matrix]
+            else:
+                wide = ref["right_" + matrix].shape[1] // 2
+                source = ref["right_" + matrix].at[:, pl.ds(pl.multiple_of(other * wide, 128), wide)]
+                target = ref["right_in_" + matrix]
+        return remote(source, target, "core", swaps.index(which), axis)
 
     def swap(which):
-        for copy in swap_copies(which):
-            begin(copy)
+        begin(swap_copy(which))
 
     def swapped(which):
-        for copy in swap_copies(which):
-            copy.wait_recv()
+        swap_copy(which).wait_recv()
 
     job_names = tuple(JOBS)
 
@@ -710,7 +824,7 @@
     def job_index(job, stage, part, mine):
         dims = JOBS[job][4]
         pick, land = [], []
-        for axis in AXES:
+        for axis in axes_of(JOBS[job][0]):
             if axis in dims[:stage]:
                 pick.append(me[axis])
             elif axis == dims[stage]:
@@ -755,12 +869,14 @@
         return ("a", "b") if JOBS[job][0] == "down" else ("",)
 
     def needs(job, stage):
-        if stage == 0:
-            return ()
+        dims = JOBS[job][4]
+        firsts = tuple((0, part) for part in first_parts(job))
         if stage == 1:
-            return tuple((0, part) for part in first_parts(job) if part != "b" or JOBS[job][4][1] != "zh")
+            return tuple(first for first in firsts if first[1] != "b" or dims[:2] != ("zl", "zh"))
         if stage == 2:
-            return ((1, ""),) + tuple((0, part) for part in first_parts(job))
+            return ((1, ""),) + firsts
+        if stage == 4:
+            return ((len(dims) - 1, ""),) + firsts
         return ((stage - 1, ""),)
 
     arrived, sent = set(), set()
@@ -771,6 +887,8 @@
 
     def arrive(job, stage, part):
         matrix, slot, _, _, dims = JOBS[job]
+        axes = axes_of(matrix)
+        last = len(dims) - 1
         source = job_copy(job_target(job, stage), stage, part)
         source.wait_recv()
         if stage < 4:
@@ -782,15 +900,15 @@
                 for order, spot in enumerate(free):
                     bit = (code >> (len(free) - 1 - order)) % 2
                     here[spot] = bit
-                    there[[place for place, axis in enumerate(AXES) if axis not in dims[: stage + 1]].index(spot)] = bit
+                    there[[place for place, axis in enumerate(axes) if axis not in dims[: stage + 1]].index(spot)] = bit
                 sums = partial[tuple(here)] + (landed[tuple(there)] if there else landed[...])
-                if stage < 3:
+                if stage < last:
                     partial[tuple(here)] = sums
                 else:
                     final, columns = job_final(job)
                     final[core, me["y"], :, columns] = sums
         arrived.add((job, stage, part))
-        for later in range(1, 6):
+        for later in list(range(1, last + 1)) + [4, 5]:
             ready = all((job,) + need in arrived for need in needs(job, later))
             if (job, later, "") not in sent and ready:
                 send(job, later)
@@ -815,33 +933,31 @@
 
     stores = []
 
-    def keep(name, number):
-        store = pltpu.make_async_copy(ref[name + "_held"], ref[name], ref["keep"].at[number])
-        store.start()
-        stores.append(store)
-
-    def multiply_feed(slot):
+    def multiply_down(slot):
         if slot == 0:
-            swapped("early")
-        swapped("feed%d" % slot)
+            for which in ("delta", "on_side", "on_across"):
+                swapped(which)
+        for which in ("hidden", "side", "across"):
+            swapped(which + str(slot))
         high, low, chunk = chunk_of(slot)
-        for side in range(2):
-            block = chunk * 2 + side
-            rows = pl.ds(pl.multiple_of(block * 384 + core * 192, 192), 192)
-            total = dot(ref["left_down"][rows, :], ref["right_down"][...]) + dot(
-                ref["left_in_down"][block], ref["right_in_down"][...]
-            )
-            total = total.astype(LOW)
-            for job, (matrix, _, first, wide, _) in JOBS.items():
-                if matrix == "down":
-                    for half in range(2):
-                        ref["partial_" + job][high, low, side, half] = total[
-                            half * 96 : (half + 1) * 96, first : first + wide
-                        ]
-        if slot % 2 == 0:
+        rows = pl.ds(pl.multiple_of((chunk * 2 + me["x"]) * 384 + core * 192, 192), 192)
+        total = dot(ref["left_down"][rows, :], ref["right_down"][...])
+        for number in range(3):
+            total = total + dot(ref["left_in_down"][number, chunk], ref["right_in_down"][number])
+        total = total.astype(LOW)
+        for job, (matrix, _, first, wide, _) in JOBS.items():
+            if matrix == "down":
+                for half in range(2):
+                    ref["partial_" + job][high, low, half] = total[half * 96 : (half + 1) * 96, first : first + wide]
+        if slot % 2 == 1:
             for job in JOBS:
                 if JOBS[job][0] == "down":
                     send(job, 0, "ab"[slot // 2])
+
+    def multiply_up(slot):
+        if slot == 0:
+            swapped("norm")
+        swapped("feed%d" % slot)
         for block in range(2):
             rows = slice(block * 384, (block + 1) * 384)
             total = dot(
@@ -872,19 +988,25 @@
                 ref["partial_" + job][block, part // 4, (part // 2) % 2, part % 2] = total[part * 48 : (part + 1) * 48]
         send(job, 0)
 
+    def vec_rows(side):
+        return pl.ds(pl.multiple_of(side * 8, 8), 8)
+
     def vec_copy(stage):
-        return remote(ref["vec_held"].at[stage], ref["vec_in"].at[stage], "vec", stage, VEC_STEPS[stage])
+        source = ref["vec_own"].at[vec_rows(1 - core)] if stage == 0 else ref["vec_held"].at[stage]
+        return remote(source, ref["vec_in"].at[stage], "vec", stage, VEC_STEPS[stage])
 
     def arrive_vec(stage):
         vec_copy(stage).wait_recv()
-        sums = ref["vec_held"][stage] + ref["vec_in"][stage]
-        if stage < 4:
-            ref["vec_held"][stage + 1] = sums
-            begin(vec_copy(stage + 1))
-        else:
-            ref["vec_sums"][...] = sums
-
-    swap("early")
+        if stage == 5:
+            ref["vec_sums"][vec_rows(1 - core), :] = ref["vec_in"][5]
+            return
+        own = ref["vec_own"][vec_rows(core), :] if stage == 0 else ref["vec_held"][stage]
+        ref["vec_held"][stage + 1] = own + ref["vec_in"][stage]
+        begin(vec_copy(stage + 1))
+        if stage == 4:
+            ref["vec_sums"][vec_rows(core), :] = ref["vec_held"][5]
+
+    swap("norm")
 
     def project():
         for number in range(third):
@@ -893,9 +1015,10 @@
                 ref["residual"][:, columns] + ref["mlp_out"][:, columns] + row_of("bias_down", columns)
             ).astype(LOW)
         ref["left_proj"][...] = ref["block_low"][...].T
-        swap("proj")
-        projected = (dot(ref["block_low"][...], ref["w_proj_held"][...]) + ref["bias_proj"][...]).astype(LOW)
-        outgoing = dot(chosen_all, projected).astype(LOW)
+        swap("proj_left")
+        loaded("w_proj", "bias_proj")
+        projected = (dot(ref["block_low"][...], ref["w_proj_held"][...]) + row_of("bias_proj")).astype(LOW)
+        outgoing = dot(ref["chosen"][...].reshape(4 * IMG_SEQ * CAP, ROWS_SEQ), projected).astype(LOW)
         ref["grid_out"][...] = outgoing.reshape(4, IMG_SEQ * CAP, -1)
         for number, axis in enumerate(PEERS):
             begin(remote(ref["grid_out"].at[peer(axis)[1]], ref["grid_in"].at[number], "grid", number, axis))
@@ -914,14 +1037,18 @@
             sums = [old + jnp.sum(new, axis=0, keepdims=True) for old, new in zip(sums, news)]
         for spot, total in zip((LN2_GAIN, LN2_BIAS, BIAS_OUT), sums):
             ref["vec_own"][spot : spot + 1, :] = total
-        ref["left_out"][...] = ref["attended"][...].T
-        swap("out")
+        swap("out_right")
 
     def attended_back():
         for number in range(third):
             columns = slice(number * 256, (number + 1) * 256)
             ref["delta_attended"][:, columns] = dot_nt(ref["right_out"][...], ref["w_out_held"][columns, :]).astype(LOW)
+
+    def transposes():
+        ref["left_out"][...] = ref["attended"][...].T
+        swap("out_left")
         ref["left_qkv"][...] = ref["normed_one"][...].T
+        swap("qkv_left")
 
     def attend_back(pair):
         queries = ref["qkv"][:, head_columns(pair, 0)]
@@ -945,7 +1072,7 @@
         for spot, total in enumerate(totals):
             ref["right_qkv"][:, head_columns(pair, spot * width)] = total.astype(LOW)
         if pair == HEADS // 2 - 1:
-            swap("qkv")
+            swap("qkv_right")
 
     def delta_first():
         for number in range(third):
@@ -961,8 +1088,8 @@
         for step in range(4):
             rows = slice(step * 64, (step + 1) * 64)
             delta = ref["delta_normed"][rows, :]
-            row_term, gains = norm_rows_back(delta, ref["tokens"][rows, :].astype(FULL), row_of("ln1_gain"))
-            ref["grad_tokens_held"][rows, :] = (ref["delta_block"][rows, :] + row_term).astype(LOW)
+            row_term, gains = norm_rows_back(delta, ref["tokens_held"][rows, :].astype(FULL), row_of("ln1_gain"))
+            ref["grad_tokens"][rows, :] = (ref["delta_block"][rows, :] + row_term).astype(LOW)
             sums = [old + jnp.sum(new, axis=0, keepdims=True) for old, new in zip(sums, (gains, delta))]
         for spot, total in zip((LN1_GAIN, LN1_BIAS), sums):
             ref["vec_own"][spot : spot + 1, :] = total
@@ -977,11 +1104,10 @@
             seen = dot_nt(jnp.ones((8, IMG_SEQ * CAP), LOW), ref["placing"][number])
             mask_sum = mask_sum + dot((1.0 - seen).astype(LOW), cot)
         ref["vec_own"][MASK : MASK + 1, : mask_sum.shape[1]] = mask_sum[0:1]
-        ref["vec_held"][0] = ref["vec_own"][...]
         begin(vec_copy(0))
-        keep("grad_tokens", 0)
 
     def decode():
+        loaded("mask_token")
         for number, axis in enumerate(PEERS + ("self",)):
             if axis == "self":
                 source = my_pos
@@ -994,13 +1120,15 @@
             visible = jnp.sum(placing.astype(FULL), axis=1, keepdims=True)
             filled = jnp.where(visible > 0.5, dot(placing, arrived_rows), row_of("mask_token").astype(FULL)).astype(LOW)
             for image in range(IMG_SEQ):
-                ref["decoder_input_held"][source * IMG_SEQ + image] = filled[
+                ref["decoder_input"][source * IMG_SEQ + image] = filled[
                     image * PLACES : image * PLACES + quarter_len
                 ]
-        keep("decoder_input", 1)
 
     segments = {
         "project": project,
+        "delta": delta,
+        "pass_delta": pass_delta,
+        "transposes": transposes,
         "second_back": second_back,
         "attended_back": attended_back,
         "delta_first": delta_first,
@@ -1009,13 +1137,16 @@
     }
     for slot in range(4):
         segments["feed%d" % slot] = functools.partial(feed, slot)
-        segments["multiply_feed%d" % slot] = functools.partial(multiply_feed, slot)
+        segments["feed_back%d" % slot] = functools.partial(feed_back, slot)
+        segments["multiply_down%d" % slot] = functools.partial(multiply_down, slot)
+        segments["multiply_up%d" % slot] = functools.partial(multiply_up, slot)
     for pair in range(HEADS // 2):
         segments["attend_back%d" % pair] = functools.partial(attend_back, pair)
-    for matrix in ("proj", "out", "qkv"):
-        segments["swapped_" + matrix] = functools.partial(swapped, matrix)
+    for which in swaps[2:8]:
+        segments["swapped_" + which] = functools.partial(swapped, which)
     for job in JOBS:
-        segments["multiply_" + job] = functools.partial(multiply, job)
+        if JOBS[job][0] not in ("down", "up"):
+            segments["multiply_" + job] = functools.partial(multiply, job)
     for step in PLAN:
         if step[0] == "do":
             segments[step[1]]()
@@ -1031,11 +1162,15 @@
 
 def finish_kernel(names, *refs):
     ref = dict(zip(names, refs))
-    loads, stores = [], []
-    for number in range(7):
-        load = pltpu.make_async_copy(ref["in%d" % number], ref["low%d" % number], ref["load"].at[number])
-        load.start()
-        loads.append(load)
+    stores = []
+    for number in (5, 6, 1, 0, 4, 3, 2):
+        source = ref["in%d" % number]
+        if number < 5:
+            source = ref["full%d" % number]
+            source[...] = ref["in%d" % number][...].astype(FULL)
+        store = pltpu.make_async_copy(source, ref["out%d" % number], ref["store"].at[number])
+        store.start()
+        stores.append(store)
     sums = ref["sums"]
     for spot, number in zip(
         (LN1_GAIN, LN1_BIAS, BIAS_Q, BIAS_V, BIAS_OUT, LN2_GAIN, LN2_BIAS, BIAS_DOWN, BIAS_PROJ, MASK), range(10)
@@ -1045,15 +1180,6 @@
     wide = sums.shape[1]
     for number in range(ref["vec10"].shape[1] // wide):
         ref["vec10"][:, number * wide : (number + 1) * wide] = sums[BIAS_UP + number : BIAS_UP + number + 1, :]
-    for number in range(7):
-        loads[number].wait()
-        source = ref["low%d" % number]
-        if number < 5:
-            source = ref["full%d" % number]
-            source[...] = ref["low%d" % number][...].astype(FULL)
-        store = pltpu.make_async_copy(source, ref["out%d" % number], ref["store"].at[number])
-        store.start()
-        stores.append(store)
     for store in stores:
         store.wait()
 
@@ -1083,13 +1209,12 @@
     rows, width = tokens.shape
     ff = w_up.shape[1]
     out_width = w_proj.shape[1]
-    row = lambda vec: vec.reshape(1, -1)
     vmem = pl.BlockSpec(memory_space=pltpu.VMEM)
     hbm = pl.BlockSpec(memory_space=pl.ANY)
     inputs = {
         "tokens": tokens,
-        "slot": row(image_slot),
-        "position": row(patch_position),
+        "slot": image_slot,
+        "position": patch_position,
         "ln1_gain": ln1_gain,
         "ln1_bias": ln1_bias,
         "bias_query": bias_query,
@@ -1097,9 +1222,9 @@
         "bias_out": bias_out,
         "ln2_gain": ln2_gain,
         "ln2_bias": ln2_bias,
-        "bias_up": row(bias_up),
+        "bias_up": bias_up,
         "bias_down": bias_down,
-        "bias_proj": row(bias_proj),
+        "bias_proj": bias_proj,
         "mask_token": mask_token,
         "cotangent": cotangent,
         "w_qkv": w_qkv,
@@ -1113,20 +1238,15 @@
     outs = {}
     for name in MATRICES:
         block = (2, 2, 96) if name == "down" else (2, 48)
-        outs["grad_" + name] = jax.ShapeDtypeStruct(block + (rights[name],), LOW)
-    outs["decoder_input"] = jax.ShapeDtypeStruct(cotangent.shape, LOW)
-    outs["grad_tokens"] = jax.ShapeDtypeStruct(tokens.shape, LOW)
-    outs["vec_sums"] = jax.ShapeDtypeStruct((16, width), FULL)
+        outs["grad_" + name] = pltpu.VMEM(block + (rights[name],), LOW)
+    outs["decoder_input"] = pltpu.VMEM(cotangent.shape, LOW)
+    outs["grad_tokens"] = pltpu.VMEM(tokens.shape, LOW)
+    outs["vec_sums"] = pltpu.VMEM((16, width), FULL)
     dma = pltpu.SemaphoreType.DMA
-    room = {
-        "w_qkv_held": (w_qkv.shape, LOW),
-        "w_out_held": (w_out.shape, LOW),
-        "w_proj_held": (w_proj.shape, LOW),
-        "w_up_held": (w_up.shape, LOW),
-        "w_down_held": (w_down.shape, LOW),
-        "cotangent_held": (cotangent.shape, LOW),
-        "decoder_input_held": (cotangent.shape, LOW),
-        "grad_tokens_held": (tokens.shape, LOW),
+    room = {name + "_held": (array.shape, array.dtype) for name, array in inputs.items()}
+    room |= {
+        "slope": ((4, rows, width), FULL),
+        "bias_up_row": ((1, ff), FULL),
         "places": ((4, 8, rows), jnp.int32),
         "chosen": ((4, IMG_SEQ * CAP, rows), LOW),
         "placing": ((4, IMG_SEQ * PLACES, IMG_SEQ * CAP), LOW),
@@ -1149,10 +1269,10 @@
         "delta_attended": ((rows, width), LOW),
         "bias_up_sum": ((1, ff), FULL),
         "vec_own": ((16, width), FULL),
-        "vec_held": ((5, 16, width), FULL),
-        "vec_in": ((5, 16, width), FULL),
-        "left_in_down": ((8, 192, rows), LOW),
-        "right_in_down": ((rows, width), LOW),
+        "vec_held": ((6, 8, width), FULL),
+        "vec_in": ((6, 8, width), FULL),
+        "left_in_down": ((3, 4, 192, rows), LOW),
+        "right_in_down": ((3, rows, width), LOW),
         "right_in_up": ((4, rows, width // 2), LOW),
         "final_down": ((2, 2, 96, width), LOW),
         "final_up": ((4, 2, 2, 48, width // 2), LOW),
@@ -1167,20 +1287,20 @@
             room["final_" + name] = ((2, 2, 48, rights[name] // 2), LOW)
     for job, (name, _, _, wide, _) in JOBS.items():
         block = (96 if name == "down" else 48, wide)
-        room["partial_" + job] = ((2, 2, 2, 2) + block, LOW)
-        for stage in range(4):
-            room["landed_%s_%d" % (job, stage)] = ((2,) * (3 - stage) + block, LOW)
+        count = len(axes_of(name))
+        room["partial_" + job] = ((2,) * count + block, LOW)
+        for stage in range(count):
+            room["landed_%s_%d" % (job, stage)] = ((2,) * (count - 1 - stage) + block, LOW)
     scratch = {name: pltpu.VMEM(shape, dtype) for name, (shape, dtype) in room.items()}
-    scratch["load"] = dma((6,))
-    scratch["keep"] = dma((2,))
+    scratch["load"] = dma((len(inputs),))
     scratch["store"] = dma((len(JOBS), 2))
     for kind, shape in (
         ("place", (3,)),
         ("back", (3,)),
         ("grid", (3,)),
-        ("core", (8, 2)),
+        ("core", (28,)),
         ("job", (len(JOBS), 7)),
-        ("vec", (5,)),
+        ("vec", (6,)),
     ):
         scratch[kind + "_send"] = dma(shape)
         scratch[kind + "_recv"] = dma(shape)
@@ -1188,11 +1308,11 @@
     found = pl.pallas_call(
         functools.partial(layer_kernel, names),
         out_shape=list(outs.values()),
-        in_specs=[hbm if name.startswith("w_") or name == "cotangent" else vmem for name in inputs],
-        out_specs=[vmem if name == "vec_sums" else hbm for name in outs],
+        in_specs=[hbm] * len(inputs),
+        out_specs=[vmem] * len(outs),
         scratch_shapes=list(scratch.values()),
         compiler_params=pltpu.CompilerParams(
-            collective_id=0, has_side_effects=True, vmem_limit_bytes=63 * 2**20
+            collective_id=0, has_side_effects=True, vmem_limit_bytes=59 * 2**20
         ),
         name="layer",
     )(*inputs.values())
@@ -1207,17 +1327,15 @@
     for number, wide in enumerate([width] * 8 + [out_width] * 2):
         results["vec%d" % number] = jax.ShapeDtypeStruct((wide,), FULL)
     results["vec10"] = jax.ShapeDtypeStruct((1, ff), FULL)
-    held = {"low%d" % number: pltpu.VMEM(source.shape, LOW) for number, source in enumerate(sources)}
-    held.update({"full%d" % number: pltpu.VMEM(source.shape, FULL) for number, source in enumerate(sources[:5])})
-    held["load"] = dma((7,))
+    held = {"full%d" % number: pltpu.VMEM(source.shape, FULL) for number, source in enumerate(sources[:5])}
     held["store"] = dma((7,))
     done = pl.pallas_call(
         functools.partial(finish_kernel, tuple(operands) + tuple(results) + tuple(held)),
         out_shape=list(results.values()),
-        in_specs=[hbm] * 7 + [vmem],
+        in_specs=[vmem] * 8,
         out_specs=[hbm] * 7 + [vmem] * 11,
         scratch_shapes=list(held.values()),
-        compiler_params=pltpu.CompilerParams(vmem_limit_bytes=60 * 2**20),
+        compiler_params=pltpu.CompilerParams(vmem_limit_bytes=24 * 2**20),
         name="finish",
     )(*operands.values())
     down, up, proj, out, qkv, decoder_input, grad_tokens = done[:7]

time: 96.9 us -> 91.7 us (0.946)
  Pallas kernels: 95.9 us -> 90.7 us
    pallas_call x1, Pallas kernels: 90.8 us -> 87.7 us  [layer_device(): pl.pallas_call(functools.partial(layer_kernel, names), out_shape=list(out...]
    pallas_call x1, Pallas kernels: 5.07 us -> 3.05 us  [layer_device(): pl.pallas_call(functools.partial(finish_kernel, tuple(operands) + tuple(r...]
where the time goes in v4:
time: 91.7 us; the launch traced here: 91.6 us
  Pallas kernels  90.7 us (99%)
    pallas_call x1, Pallas kernels, layer_device(): pl.pallas_call(functools.partial(layer_kernel, names), out_shape=list(out...  87.7 us
    pallas_call x1, Pallas kernels, layer_device(): pl.pallas_call(functools.partial(finish_kernel, tuple(operands) + tuple(r...  3.05 us

profile of v4, /device:TPU:1, one launch (start us, length us, event | category | flops | bytes accessed | tf_op | source)
XLA Modules:
  0.0 91.6 jit_solution(16384588392633257112)
XLA Ops:
  0.7 87.7 %layer.1 = (bf16[2,2,96,768]{3,2,1,0:T(8,128)(2,1)S(1)}, bf16[2,48,3072]{2,1,0:T(8,128)(2,1)S(1)}, bf16[2,48,512]{2,1,0:T(8,128)(2,1)S(1)}, bf16[2,48,768]{2,1,0...) custom-call(bf16[256,768]{1,0:T(8,128)(2,1)} %refs_0_.1, ...), custom_call_target="tpu_custom_call" | custom-call | tf_op jit(solution)/shard_map/layer/pallas_call | solution.py:1308
  88.3 3.1 %finish.1 = (f32[384,768]{1,0:T(8,128)}, f32[96,3072]{1,0:T(8,128)}, f32[96,512]{1,0:T(8,128)}, f32[96,768]{1,0:T(8,128)}, f32[96,2304]{1,0:T(8,128)}, /*index=5...) custom-call(bf16[384,768]{1,0:T(8,128)(2,1)S(1)} %bitcast.6, ...), custom_call_target="tpu_custom_call" | custom-call | tf_op jit(solution)/shard_map/finish/pallas_call | solution.py:1332

commit v5 on v4

--- a/solution.py
+++ b/solution.py
@@ -274,22 +274,19 @@
 AXES = ("zh", "zl", "x", "y")
 MATRICES = ("down", "up", "proj", "out", "qkv")
 JOBS = {
-    "down0": ("down", None, 0, 256, ("zl", "zh", "y")),
-    "down1": ("down", None, 256, 256, ("zl", "y", "zh")),
-    "down2": ("down", None, 512, 256, ("zl", "y", "zh")),
-    "up0a": ("up", 0, 0, 256, ("y", "x", "zl", "zh")),
-    "up0b": ("up", 0, 256, 128, ("zl", "zh", "y", "x")),
-    "up1a": ("up", 1, 0, 256, ("y", "x", "zl", "zh")),
-    "up1b": ("up", 1, 256, 128, ("zl", "zh", "y", "x")),
-    "up2a": ("up", 2, 0, 256, ("y", "x", "zl", "zh")),
-    "up2b": ("up", 2, 256, 128, ("zl", "zh", "y", "x")),
-    "up3a": ("up", 3, 0, 256, ("y", "x", "zl", "zh")),
-    "up3b": ("up", 3, 256, 128, ("zl", "zh", "y", "x")),
-    "proj0": ("proj", None, 0, 256, ("zl", "x", "y", "zh")),
-    "out0": ("out", None, 0, 384, ("y", "x", "zl", "zh")),
-    "qkv0": ("qkv", None, 0, 256, ("y", "zl", "x", "zh")),
-    "qkv1": ("qkv", None, 256, 256, ("x", "y", "zl", "zh")),
-    "qkv2": ("qkv", None, 512, 256, ("y", "x", "zl", "zh")),
+    "down0": ("down", None, 0, 256, ("y", "zl", "zh")),
+    "down1": ("down", None, 256, 256, ("y", "zl", "zh")),
+    "down2": ("down", None, 512, 256, ("zl", "zh", "y")),
+    "up0a": ("up", 0, 0, 256, ("y", "zl", "zh", "x")),
+    "up0b": ("up", 0, 256, 128, ("zl", "x", "zh", "y")),
+    "up1a": ("up", 1, 0, 384, ("x", "zl", "y", "zh")),
+    "up2a": ("up", 2, 0, 384, ("zl", "y", "zh", "x")),
+    "up3a": ("up", 3, 0, 384, ("y", "zl", "zh", "x")),
+    "proj0": ("proj", None, 0, 256, ("zl", "y", "x", "zh")),
+    "out0": ("out", None, 0, 384, ("x", "y", "zl", "zh")),
+    "qkv0": ("qkv", None, 0, 256, ("y", "x", "zl", "zh")),
+    "qkv1": ("qkv", None, 256, 256, ("y", "zl", "zh", "x")),
+    "qkv2": ("qkv", None, 512, 256, ("x", "y", "zl", "zh")),
     "qkv3": ("qkv", None, 768, 256, ("x", "y", "zl", "zh")),
     "qkv4": ("qkv", None, 1024, 128, ("x", "y", "zl", "zh")),
 }
@@ -299,38 +296,40 @@
     ("do", "feed2"),
     ("do", "feed3"),
     ("do", "project"),
+    ("do", "delta_rows"),
     ("do", "delta"),
     ("do", "feed_back0"),
     ("do", "feed_back1"),
-    ("do", "feed_back2"),
-    ("do", "feed_back3"),
     ("do", "swapped_proj_left"),
     ("do", "swapped_proj_right"),
     ("do", "multiply_proj0"),
+    ("do", "feed_back2"),
     ("do", "multiply_up0"),
-    ("do", "multiply_up1"),
-    ("do", "multiply_up2"),
-    ("do", "multiply_up3"),
+    ("do", "feed_back3"),
     ("do", "second_back"),
     ("do", "attended_back"),
+    ("do", "attend_back0"),
+    ("do", "multiply_up1"),
+    ("do", "multiply_up3"),
+    ("do", "multiply_up2"),
     ("do", "transposes"),
-    ("do", "attend_back0"),
+    ("proj0", 0, ""),
     ("do", "attend_back1"),
     ("do", "attend_back2"),
-    ("proj0", 0, ""),
+    ("up0a", 0, ""),
     ("do", "attend_back3"),
-    ("up0a", 0, ""),
+    ("up0b", 0, ""),
     ("do", "attend_back4"),
     ("do", "attend_back5"),
-    ("up1b", 0, ""),
+    ("do", "delta_first"),
+    ("do", "pass_delta"),
+    ("do", "decode"),
     ("do", "swapped_out_left"),
     ("do", "swapped_out_right"),
     ("do", "multiply_out0"),
-    ("do", "pass_delta"),
-    ("do", "delta_first"),
-    ("do", "first_back"),
-    ("up0b", 0, ""),
-    ("up1a", 0, ""),
+    ("do", "multiply_down0"),
+    ("do", "multiply_down1"),
+    ("up3a", 0, ""),
     ("do", "swapped_qkv_left"),
     ("do", "swapped_qkv_right"),
     ("do", "multiply_qkv0"),
@@ -338,119 +337,100 @@
     ("do", "multiply_qkv2"),
     ("do", "multiply_qkv3"),
     ("do", "multiply_qkv4"),
-    ("up3b", 0, ""),
+    ("up2a", 0, ""),
+    ("proj0", 1, ""),
+    ("do", "first_back"),
+    ("up0a", 1, ""),
+    ("down0", 0, "a"),
+    ("down2", 0, "a"),
     ("vec", 0),
-    ("do", "decode"),
-    ("up2b", 0, ""),
-    ("up2a", 0, ""),
-    ("do", "multiply_down0"),
-    ("do", "multiply_down1"),
     ("do", "multiply_down2"),
     ("do", "multiply_down3"),
-    ("up3b", 1, ""),
-    ("proj0", 1, ""),
-    ("up3a", 0, ""),
-    ("up2b", 1, ""),
-    ("down0", 0, "a"),
-    ("up0a", 1, ""),
-    ("up1b", 1, ""),
     ("down1", 0, "a"),
+    ("up3a", 1, ""),
+    ("qkv0", 0, ""),
+    ("up0a", 2, ""),
+    ("down2", 0, "b"),
+    ("up1a", 0, ""),
+    ("up0b", 1, ""),
+    ("qkv1", 0, ""),
+    ("up3a", 2, ""),
+    ("up2a", 1, ""),
     ("up1a", 1, ""),
-    ("up0b", 1, ""),
-    ("down2", 0, "a"),
     ("out0", 0, ""),
+    ("down2", 1, ""),
     ("down0", 0, "b"),
-    ("qkv1", 0, ""),
+    ("up0b", 2, ""),
+    ("qkv1", 1, ""),
     ("down1", 0, "b"),
-    ("qkv0", 0, ""),
-    ("down2", 0, "b"),
+    ("qkv2", 0, ""),
+    ("up1a", 2, ""),
+    ("down0", 1, ""),
+    ("up2a", 2, ""),
+    ("out0", 1, ""),
     ("qkv3", 0, ""),
+    ("qkv1", 2, ""),
+    ("down1", 1, ""),
+    ("down2", 2, ""),
+    ("up0b", 3, ""),
     ("qkv4", 0, ""),
-    ("qkv2", 0, ""),
+    ("qkv2", 1, ""),
+    ("proj0", 2, ""),
+    ("up1a", 3, ""),
     ("vec", 1),
-    ("up1a", 2, ""),
-    ("up3b", 2, ""),
-    ("up0a", 2, ""),
-    ("proj0", 2, ""),
-    ("up2b", 2, ""),
-    ("up2a", 1, ""),
-    ("down0", 1, ""),
-    ("up1b", 2, ""),
-    ("up0b", 2, ""),
+    ("out0", 2, ""),
+    ("qkv3", 1, ""),
+    ("down0", 2, ""),
     ("qkv0", 1, ""),
-    ("up3a", 1, ""),
-    ("qkv1", 1, ""),
-    ("up3a", 2, ""),
+    ("qkv2", 2, ""),
+    ("down2", 4, ""),
+    ("up0a", 3, ""),
+    ("up0b", 4, ""),
     ("up3a", 3, ""),
-    ("down1", 1, ""),
-    ("up2a", 2, ""),
+    ("down1", 2, ""),
+    ("qkv4", 1, ""),
     ("up2a", 3, ""),
-    ("out0", 1, ""),
+    ("down2", 5, ""),
+    ("up0b", 5, ""),
+    ("up1a", 4, ""),
+    ("qkv1", 3, ""),
     ("proj0", 3, ""),
-    ("qkv1", 2, ""),
-    ("down2", 1, ""),
-    ("qkv2", 1, ""),
-    ("up3b", 3, ""),
-    ("up2b", 3, ""),
-    ("up1b", 3, ""),
-    ("up1a", 3, ""),
-    ("up0b", 3, ""),
-    ("qkv3", 1, ""),
+    ("qkv3", 2, ""),
+    ("vec", 2),
     ("qkv0", 2, ""),
-    ("out0", 2, ""),
-    ("qkv4", 1, ""),
-    ("down1", 2, ""),
-    ("vec", 2),
-    ("up0a", 3, ""),
-    ("down0", 2, ""),
+    ("down0", 4, ""),
+    ("up1a", 5, ""),
+    ("out0", 3, ""),
+    ("up0a", 4, ""),
+    ("qkv4", 2, ""),
     ("up3a", 4, ""),
-    ("qkv1", 3, ""),
-    ("qkv2", 2, ""),
+    ("down0", 5, ""),
+    ("qkv2", 3, ""),
+    ("vec", 3),
+    ("up0a", 5, ""),
+    ("down1", 4, ""),
+    ("qkv3", 3, ""),
+    ("up3a", 5, ""),
     ("up2a", 4, ""),
+    ("qkv1", 4, ""),
+    ("qkv0", 3, ""),
+    ("down1", 5, ""),
     ("proj0", 4, ""),
-    ("up3b", 4, ""),
-    ("qkv3", 2, ""),
-    ("up2b", 4, ""),
-    ("up1b", 4, ""),
-    ("up3a", 5, ""),
-    ("up1a", 4, ""),
-    ("down2", 2, ""),
-    ("up0b", 4, ""),
+    ("qkv4", 3, ""),
     ("up2a", 5, ""),
+    ("out0", 4, ""),
+    ("qkv1", 5, ""),
+    ("qkv2", 4, ""),
     ("proj0", 5, ""),
-    ("qkv4", 2, ""),
-    ("up3b", 5, ""),
-    ("qkv0", 3, ""),
-    ("down1", 4, ""),
-    ("up2b", 5, ""),
-    ("vec", 3),
-    ("up1b", 5, ""),
-    ("up0a", 4, ""),
-    ("up1a", 5, ""),
-    ("up0b", 5, ""),
-    ("out0", 3, ""),
-    ("down0", 4, ""),
-    ("qkv1", 4, ""),
-    ("down1", 5, ""),
-    ("qkv2", 3, ""),
-    ("up0a", 5, ""),
-    ("down2", 4, ""),
-    ("qkv3", 3, ""),
+    ("qkv3", 4, ""),
+    ("vec", 4),
     ("qkv0", 4, ""),
-    ("down0", 5, ""),
-    ("qkv4", 3, ""),
-    ("qkv1", 5, ""),
-    ("out0", 4, ""),
-    ("qkv2", 4, ""),
-    ("vec", 4),
-    ("down2", 5, ""),
+    ("out0", 5, ""),
+    ("qkv4", 4, ""),
+    ("qkv2", 5, ""),
+    ("qkv3", 5, ""),
+    ("vec", 5),
     ("qkv0", 5, ""),
-    ("qkv3", 4, ""),
-    ("qkv4", 4, ""),
-    ("out0", 5, ""),
-    ("qkv2", 5, ""),
-    ("vec", 5),
-    ("qkv3", 5, ""),
     ("qkv4", 5, ""),
 )
 VEC_STEPS = ("core", "x", "y", "zl", "zh", "core")
@@ -532,21 +512,24 @@
             return device_of({**me, "x": 1 - me["x"], "core": 1 - core})
         return device_of({**me, axis: 1 - me[axis]})
 
-    started = []
-
-    def remote(source, target, kind, spot, axis):
+    leaving = {}
+
+    def remote(source, target, kind, spot, axis, leave=None):
+        leave = ref["small_send"].at[spot] if leave is None else leave
         return pltpu.make_async_remote_copy(
             src_ref=source,
             dst_ref=target,
-            send_sem=ref[kind + "_send"].at[spot],
+            send_sem=leave,
             recv_sem=ref[kind + "_recv"].at[spot],
             device_id=peer(axis),
             device_id_type=MESH_ID,
         )
 
-    def begin(copy):
+    def begin(copy, use):
+        if use in leaving:
+            leaving.pop(use).wait_send()
         copy.start()
-        started.append(copy)
+        leaving[use] = copy
 
     barrier = pltpu.get_barrier_semaphore()
     for axis in AXES + ("core", "diagonal", "across"):
@@ -580,7 +563,7 @@
         if number == 6:
             pl.semaphore_wait(barrier, 7)
             for spot, axis in enumerate(PEERS):
-                begin(remote(ref["places"].at[my_pos], ref["places"].at[my_pos], "place", spot, axis))
+                begin(remote(ref["places"].at[my_pos], ref["places"].at[my_pos], "place", spot, axis), spot)
         part = dot(ref["normed"][...], ref["w_qkv_held"][:, columns])
         if number < third:
             part = part + row_of("bias_query", columns)
@@ -660,7 +643,7 @@
         else:
             ref["back_out"][number] = back
     for number, axis in enumerate(PEERS):
-        begin(remote(ref["back_out"].at[number], ref["back_in"].at[my_pos], "back", number, axis))
+        begin(remote(ref["back_out"].at[number], ref["back_in"].at[my_pos], "back", number, axis), number)
     ref["vec_own"][...] = jnp.zeros_like(ref["vec_own"])
 
     loaded("w_out", "bias_out")
@@ -682,7 +665,7 @@
     lax.fori_loop(0, 4, second_norm, 0, unroll=4)
     ref["left_up"][...] = ref["normed"][...].T
 
-    def delta():
+    def delta_rows():
         for number, axis in enumerate(PEERS):
             remote(ref["back_out"].at[number], ref["back_in"].at[my_pos], "back", number, axis).wait_recv()
         chosen_all = ref["chosen"][...].reshape(4 * IMG_SEQ * CAP, ROWS_SEQ)
@@ -690,6 +673,9 @@
         delta_proj = dot_tn(chosen_all, returned)
         ref["vec_own"][BIAS_PROJ : BIAS_PROJ + 1, : delta_proj.shape[1]] = jnp.sum(delta_proj, axis=0, keepdims=True)
         ref["right_proj"][...] = delta_proj.astype(LOW)
+        swap("proj_right")
+
+    def delta():
         for number in range(third):
             columns = slice(number * 256, (number + 1) * 256)
             part = dot_nt(ref["right_proj"][...], ref["w_proj_held"][columns, :])
@@ -697,7 +683,7 @@
             part = part.astype(LOW)
             ref["right_down"][:, columns] = part
             ref["vec_own"][BIAS_DOWN : BIAS_DOWN + 1, columns] = jnp.sum(part.astype(FULL), axis=0, keepdims=True)
-        for which in ("delta_side", "delta_across", "side2", "across2", "side3", "across3", "delta", "proj_right"):
+        for which in ("delta_side", "delta_across", "side2", "across2", "side3", "across3", "delta"):
             swap(which)
 
     def pass_delta():
@@ -708,13 +694,10 @@
     loaded("w_up", "bias_up")
     ref["bias_up_row"][...] = row_of("bias_up")
 
-    def chunk_of(slot):
-        high = 1 - me["zh"] if slot < 2 else me["zh"]
-        low = 1 - me["zl"] if slot % 2 == 0 else me["zl"]
-        return high, low, high * 2 + low
-
     def chunk_columns(slot, start=0, wide=width):
-        return pl.ds(pl.multiple_of(chunk_of(slot)[2] * width + start, 128), wide)
+        if isinstance(start, int):
+            return pl.ds(slot * width + start, wide)
+        return pl.ds(pl.multiple_of(slot * width + start, 128), wide)
 
     def feed(slot):
         columns = chunk_columns(slot)
@@ -776,7 +759,7 @@
             source = ref["right_in_down"].at[2, :, pl.ds(half, half)]
             target = ref["right_in_down"].at[1, :, pl.ds(half, half)]
         elif which[:-1] in ("hidden", "side", "across"):
-            chunk = chunk_of(int(which[-1]))[2]
+            chunk = int(which[-1])
             blocks = ref["left_down"].reshape(8, 2, 192, ROWS_SEQ)
             if which.startswith("hidden"):
                 source, target = blocks.at[chunk * 2 + me["x"], other], ref["left_in_down"].at[0, chunk]
@@ -798,10 +781,16 @@
                 wide = ref["right_" + matrix].shape[1] // 2
                 source = ref["right_" + matrix].at[:, pl.ds(pl.multiple_of(other * wide, 128), wide)]
                 target = ref["right_in_" + matrix]
-        return remote(source, target, "core", swaps.index(which), axis)
+        leave = swap_leave[which] if which in swap_leave else 0
+        return remote(source, target, "core", swaps.index(which), axis, ref["core_send"].at[leave])
+
+    swap_leave = {}
 
     def swap(which):
-        begin(swap_copy(which))
+        far = which[:-1] in ("side", "across") or which.startswith("delta_")
+        many = sum(spot < 6 if not far else spot >= 6 for spot in swap_leave.values())
+        swap_leave[which] = 6 + many if far else many % 6
+        begin(swap_copy(which), ("core", swap_leave[which]))
 
     def swapped(which):
         swap_copy(which).wait_recv()
@@ -812,14 +801,8 @@
         matrix, slot, first, wide, _ = JOBS[job]
         final = ref["final_" + matrix]
         if slot is not None:
-            final = final.at[chunk_of(slot)[2]]
+            final = final.at[slot]
         return final, pl.ds(first, wide)
-
-    def job_target(job, stage):
-        _, slot, _, _, dims = JOBS[job]
-        if slot is None or stage > 3 or dims[stage] not in ("zl", "zh"):
-            return job
-        return "up%d%s" % (slot ^ (1 if dims[stage] == "zl" else 2), job[3:])
 
     def job_index(job, stage, part, mine):
         dims = JOBS[job][4]
@@ -830,23 +813,26 @@
             elif axis == dims[stage]:
                 pick.append(me[axis] if mine else 1 - me[axis])
             elif axis == "zh" and part:
-                pick.append(1 - me[axis] if part == "a" else me[axis])
+                pick.append("ab".index(part))
                 land.append(pick[-1])
             else:
                 pick.append(slice(None))
                 land.append(slice(None))
         return tuple(pick), tuple(land)
 
+    def job_send_spot(job, stage, part):
+        spot = job_names.index(job)
+        return 2 * len(job_names) + spot if part == "b" else 2 * spot + stage % 2
+
     def job_copy(job, stage, part):
         dims = JOBS[job][4]
-        target = job_target(job, stage)
-        spot = stage if part != "b" else 6
-        send_sem = ref["job_send"].at[job_names.index(job), spot]
-        recv_sem = ref["job_recv"].at[job_names.index(target), spot]
+        spot = stage if part != "b" else 3
+        send_sem = ref["job_send"].at[job_send_spot(job, stage, part)]
+        recv_sem = ref["job_recv"].at[job_names.index(job), spot]
         if stage < 4:
             pick, land = job_index(job, stage, part, False)
             source = ref["partial_" + job].at[pick]
-            place = ref["landed_%s_%d" % (target, stage)]
+            place = ref["landed_%s_%d" % (job, stage)]
             place = place.at[land] if land else place
             axis = dims[stage]
         else:
@@ -872,7 +858,7 @@
         dims = JOBS[job][4]
         firsts = tuple((0, part) for part in first_parts(job))
         if stage == 1:
-            return tuple(first for first in firsts if first[1] != "b" or dims[:2] != ("zl", "zh"))
+            return firsts
         if stage == 2:
             return ((1, ""),) + firsts
         if stage == 4:
@@ -883,14 +869,13 @@
 
     def send(job, stage, part=""):
         sent.add((job, stage, part))
-        begin(job_copy(job, stage, part))
+        begin(job_copy(job, stage, part), ("job", job_send_spot(job, stage, part)))
 
     def arrive(job, stage, part):
         matrix, slot, _, _, dims = JOBS[job]
         axes = axes_of(matrix)
         last = len(dims) - 1
-        source = job_copy(job_target(job, stage), stage, part)
-        source.wait_recv()
+        job_copy(job, stage, part).wait_recv()
         if stage < 4:
             partial, landed = ref["partial_" + job], ref["landed_%s_%d" % (job, stage)]
             pick, land = job_index(job, stage, part, True)
@@ -918,20 +903,11 @@
             out = ref["grad_" + matrix]
             for side in range(2):
                 if matrix == "down":
-                    place = out.at[side, :, :, columns]
+                    out[side, :, :, columns] = final[side, :, :, columns]
                 else:
                     start = side * ref["final_" + matrix].shape[-1] + first
-                    if slot is not None:
-                        place = out.at[:, :, chunk_columns(slot, start, wide)]
-                    else:
-                        place = out.at[:, :, pl.ds(start, wide)]
-                store = pltpu.make_async_copy(
-                    final.at[side, :, :, columns], place, ref["store"].at[job_names.index(job), side]
-                )
-                store.start()
-                stores.append(store)
-
-    stores = []
+                    place = pl.ds(start, wide) if slot is None else chunk_columns(slot, start, wide)
+                    out[:, :, place] = final[side, :, :, columns]
 
     def multiply_down(slot):
         if slot == 0:
@@ -939,16 +915,15 @@
                 swapped(which)
         for which in ("hidden", "side", "across"):
             swapped(which + str(slot))
-        high, low, chunk = chunk_of(slot)
-        rows = pl.ds(pl.multiple_of((chunk * 2 + me["x"]) * 384 + core * 192, 192), 192)
+        rows = pl.ds(pl.multiple_of((slot * 2 + me["x"]) * 384 + core * 192, 192), 192)
         total = dot(ref["left_down"][rows, :], ref["right_down"][...])
         for number in range(3):
-            total = total + dot(ref["left_in_down"][number, chunk], ref["right_in_down"][number])
+            total = total + dot(ref["left_in_down"][number, slot], ref["right_in_down"][number])
         total = total.astype(LOW)
         for job, (matrix, _, first, wide, _) in JOBS.items():
             if matrix == "down":
                 for half in range(2):
-                    ref["partial_" + job][high, low, half] = total[half * 96 : (half + 1) * 96, first : first + wide]
+                    ref["partial_" + job][slot // 2, slot % 2, half] = total[half * 96 : (half + 1) * 96, first : first + wide]
         if slot % 2 == 1:
             for job in JOBS:
                 if JOBS[job][0] == "down":
@@ -993,7 +968,7 @@
 
     def vec_copy(stage):
         source = ref["vec_own"].at[vec_rows(1 - core)] if stage == 0 else ref["vec_held"].at[stage]
-        return remote(source, ref["vec_in"].at[stage], "vec", stage, VEC_STEPS[stage])
+        return remote(source, ref["vec_in"].at[stage], "vec", stage, VEC_STEPS[stage], ref["vec_send"].at[0])
 
     def arrive_vec(stage):
         vec_copy(stage).wait_recv()
@@ -1002,7 +977,7 @@
             return
         own = ref["vec_own"][vec_rows(core), :] if stage == 0 else ref["vec_held"][stage]
         ref["vec_held"][stage + 1] = own + ref["vec_in"][stage]
-        begin(vec_copy(stage + 1))
+        begin(vec_copy(stage + 1), "vec")
         if stage == 4:
             ref["vec_sums"][vec_rows(core), :] = ref["vec_held"][5]
 
@@ -1021,7 +996,7 @@
         outgoing = dot(ref["chosen"][...].reshape(4 * IMG_SEQ * CAP, ROWS_SEQ), projected).astype(LOW)
         ref["grid_out"][...] = outgoing.reshape(4, IMG_SEQ * CAP, -1)
         for number, axis in enumerate(PEERS):
-            begin(remote(ref["grid_out"].at[peer(axis)[1]], ref["grid_in"].at[number], "grid", number, axis))
+            begin(remote(ref["grid_out"].at[peer(axis)[1]], ref["grid_in"].at[number], "grid", number, axis), number)
 
     def second_back():
         sums = [jnp.zeros((1, width), FULL)] * 3
@@ -1104,7 +1079,7 @@
             seen = dot_nt(jnp.ones((8, IMG_SEQ * CAP), LOW), ref["placing"][number])
             mask_sum = mask_sum + dot((1.0 - seen).astype(LOW), cot)
         ref["vec_own"][MASK : MASK + 1, : mask_sum.shape[1]] = mask_sum[0:1]
-        begin(vec_copy(0))
+        begin(vec_copy(0), "vec")
 
     def decode():
         loaded("mask_token")
@@ -1126,6 +1101,7 @@
 
     segments = {
         "project": project,
+        "delta_rows": delta_rows,
         "delta": delta,
         "pass_delta": pass_delta,
         "transposes": transposes,
@@ -1154,9 +1130,7 @@
             arrive_vec(step[1])
         else:
             arrive(*step)
-    for store in stores:
-        store.wait()
-    for copy in started:
+    for copy in leaving.values():
         copy.wait_send()
 
 
@@ -1293,16 +1267,17 @@
             room["landed_%s_%d" % (job, stage)] = ((2,) * (count - 1 - stage) + block, LOW)
     scratch = {name: pltpu.VMEM(shape, dtype) for name, (shape, dtype) in room.items()}
     scratch["load"] = dma((len(inputs),))
-    scratch["store"] = dma((len(JOBS), 2))
+    downs = sum(job[0] == "down" for job in JOBS.values())
+    for kind, shape in (("small", (3,)), ("core", (16,)), ("job", (2 * len(JOBS) + downs,)), ("vec", (1,))):
+        scratch[kind + "_send"] = dma(shape)
     for kind, shape in (
         ("place", (3,)),
         ("back", (3,)),
         ("grid", (3,)),
         ("core", (28,)),
-        ("job", (len(JOBS), 7)),
+        ("job", (len(JOBS), 6)),
         ("vec", (6,)),
     ):
-        scratch[kind + "_send"] = dma(shape)
         scratch[kind + "_recv"] = dma(shape)
     names = tuple(inputs) + tuple(outs) + tuple(scratch)
     found = pl.pallas_call(

time: 91.7 us -> 87.5 us (0.954)
  Pallas kernels: 90.7 us -> 86.5 us
    pallas_call x1, Pallas kernels: 87.7 us -> 83.4 us  [layer_device(): pl.pallas_call(functools.partial(layer_kernel, names), out_shape=list(out...]
where the time goes in v5:
time: 87.5 us; the launch traced here: 87.3 us
  Pallas kernels  86.5 us (99%)
    pallas_call x1, Pallas kernels, layer_device(): pl.pallas_call(functools.partial(layer_kernel, names), out_shape=list(out...  83.4 us
    pallas_call x1, Pallas kernels, layer_device(): pl.pallas_call(functools.partial(finish_kernel, tuple(operands) + tuple(r...  3.05 us

profile of v5, /device:TPU:1, one launch (start us, length us, event | category | flops | bytes accessed | tf_op | source)
XLA Modules:
  0.0 87.3 jit_solution(11027526939131435173)
XLA Ops:
  0.7 83.4 %layer.1 = (bf16[2,2,96,768]{3,2,1,0:T(8,128)(2,1)S(1)}, bf16[2,48,3072]{2,1,0:T(8,128)(2,1)S(1)}, bf16[2,48,512]{2,1,0:T(8,128)(2,1)S(1)}, bf16[2,48,768]{2,1,0...) custom-call(bf16[256,768]{1,0:T(8,128)(2,1)} %refs_0_.1, ...), custom_call_target="tpu_custom_call" | custom-call | tf_op jit(solution)/shard_map/layer/pallas_call | solution.py:1283
  84.1 3.1 %finish.1 = (f32[384,768]{1,0:T(8,128)}, f32[96,3072]{1,0:T(8,128)}, f32[96,512]{1,0:T(8,128)}, f32[96,768]{1,0:T(8,128)}, f32[96,2304]{1,0:T(8,128)}, /*index=5...) custom-call(bf16[384,768]{1,0:T(8,128)(2,1)S(1)} %bitcast.6, ...), custom_call_target="tpu_custom_call" | custom-call | tf_op jit(solution)/shard_map/finish/pallas_call | solution.py:1307

commit v6 on v5

--- a/solution.py
+++ b/solution.py
@@ -274,12 +274,12 @@
 AXES = ("zh", "zl", "x", "y")
 MATRICES = ("down", "up", "proj", "out", "qkv")
 JOBS = {
-    "down0": ("down", None, 0, 256, ("y", "zl", "zh")),
+    "down0": ("down", None, 0, 256, ("zl", "y", "zh")),
     "down1": ("down", None, 256, 256, ("y", "zl", "zh")),
     "down2": ("down", None, 512, 256, ("zl", "zh", "y")),
     "up0a": ("up", 0, 0, 256, ("y", "zl", "zh", "x")),
     "up0b": ("up", 0, 256, 128, ("zl", "x", "zh", "y")),
-    "up1a": ("up", 1, 0, 384, ("x", "zl", "y", "zh")),
+    "up1a": ("up", 1, 0, 384, ("x", "y", "zl", "zh")),
     "up2a": ("up", 2, 0, 384, ("zl", "y", "zh", "x")),
     "up3a": ("up", 3, 0, 384, ("y", "zl", "zh", "x")),
     "proj0": ("proj", None, 0, 256, ("zl", "y", "x", "zh")),
@@ -341,98 +341,101 @@
     ("proj0", 1, ""),
     ("do", "first_back"),
     ("up0a", 1, ""),
+    ("down1", 0, "a"),
     ("down0", 0, "a"),
-    ("down2", 0, "a"),
     ("vec", 0),
     ("do", "multiply_down2"),
     ("do", "multiply_down3"),
-    ("down1", 0, "a"),
+    ("down2", 0, "a"),
+    ("qkv0", 0, ""),
     ("up3a", 1, ""),
-    ("qkv0", 0, ""),
-    ("up0a", 2, ""),
-    ("down2", 0, "b"),
     ("up1a", 0, ""),
     ("up0b", 1, ""),
     ("qkv1", 0, ""),
+    ("up0a", 2, ""),
+    ("down0", 0, "b"),
+    ("down2", 0, "b"),
+    ("up2a", 1, ""),
+    ("down1", 0, "b"),
+    ("out0", 0, ""),
     ("up3a", 2, ""),
-    ("up2a", 1, ""),
+    ("qkv1", 1, ""),
+    ("up0b", 2, ""),
     ("up1a", 1, ""),
-    ("out0", 0, ""),
+    ("qkv2", 0, ""),
+    ("down0", 1, ""),
     ("down2", 1, ""),
-    ("down0", 0, "b"),
-    ("up0b", 2, ""),
-    ("qkv1", 1, ""),
-    ("down1", 0, "b"),
-    ("qkv2", 0, ""),
+    ("down1", 1, ""),
+    ("out0", 1, ""),
+    ("up0b", 3, ""),
+    ("qkv3", 0, ""),
+    ("up2a", 2, ""),
     ("up1a", 2, ""),
-    ("down0", 1, ""),
-    ("up2a", 2, ""),
-    ("out0", 1, ""),
-    ("qkv3", 0, ""),
+    ("qkv2", 1, ""),
+    ("qkv4", 0, ""),
+    ("down2", 2, ""),
     ("qkv1", 2, ""),
-    ("down1", 1, ""),
-    ("down2", 2, ""),
-    ("up0b", 3, ""),
-    ("qkv4", 0, ""),
-    ("qkv2", 1, ""),
+    ("up0b", 4, ""),
     ("proj0", 2, ""),
-    ("up1a", 3, ""),
     ("vec", 1),
     ("out0", 2, ""),
+    ("up0b", 5, ""),
+    ("down0", 2, ""),
     ("qkv3", 1, ""),
-    ("down0", 2, ""),
     ("qkv0", 1, ""),
+    ("qkv4", 1, ""),
     ("qkv2", 2, ""),
+    ("up0a", 3, ""),
+    ("down1", 2, ""),
     ("down2", 4, ""),
-    ("up0a", 3, ""),
-    ("up0b", 4, ""),
     ("up3a", 3, ""),
-    ("down1", 2, ""),
-    ("qkv4", 1, ""),
+    ("vec", 2),
     ("up2a", 3, ""),
+    ("qkv1", 3, ""),
+    ("up1a", 3, ""),
+    ("qkv3", 2, ""),
+    ("down0", 4, ""),
     ("down2", 5, ""),
-    ("up0b", 5, ""),
+    ("up0a", 4, ""),
+    ("proj0", 3, ""),
+    ("qkv0", 2, ""),
+    ("qkv4", 2, ""),
+    ("down1", 4, ""),
+    ("down0", 5, ""),
+    ("up0a", 5, ""),
+    ("up3a", 4, ""),
+    ("out0", 3, ""),
+    ("vec", 3),
+    ("up2a", 4, ""),
+    ("down1", 5, ""),
+    ("qkv2", 3, ""),
+    ("qkv1", 4, ""),
+    ("up3a", 5, ""),
     ("up1a", 4, ""),
-    ("qkv1", 3, ""),
-    ("proj0", 3, ""),
-    ("qkv3", 2, ""),
-    ("vec", 2),
-    ("qkv0", 2, ""),
-    ("down0", 4, ""),
+    ("qkv3", 3, ""),
+    ("up2a", 5, ""),
+    ("proj0", 4, ""),
+    ("qkv1", 5, ""),
+    ("qkv0", 3, ""),
+    ("out0", 4, ""),
     ("up1a", 5, ""),
-    ("out0", 3, ""),
-    ("up0a", 4, ""),
-    ("qkv4", 2, ""),
-    ("up3a", 4, ""),
-    ("down0", 5, ""),
-    ("qkv2", 3, ""),
-    ("vec", 3),
-    ("up0a", 5, ""),
-    ("down1", 4, ""),
-    ("qkv3", 3, ""),
-    ("up3a", 5, ""),
-    ("up2a", 4, ""),
-    ("qkv1", 4, ""),
-    ("qkv0", 3, ""),
-    ("down1", 5, ""),
-    ("proj0", 4, ""),
     ("qkv4", 3, ""),
-    ("up2a", 5, ""),
-    ("out0", 4, ""),
-    ("qkv1", 5, ""),
     ("qkv2", 4, ""),
     ("proj0", 5, ""),
     ("qkv3", 4, ""),
     ("vec", 4),
+    ("out0", 5, ""),
+    ("qkv2", 5, ""),
     ("qkv0", 4, ""),
-    ("out0", 5, ""),
     ("qkv4", 4, ""),
-    ("qkv2", 5, ""),
     ("qkv3", 5, ""),
     ("vec", 5),
     ("qkv0", 5, ""),
+    ("qkv0", 6, ""),
     ("qkv4", 5, ""),
+    ("qkv4", 6, ""),
 )
+DIRECT = ("qkv0", "qkv4",)
 VEC_STEPS = ("core", "x", "y", "zl", "zh", "core")
 PEERS = ("diagonal", "y", "core")
 PLACES = 64
@@ -822,13 +825,15 @@
 
     def job_send_spot(job, stage, part):
         spot = job_names.index(job)
+        if stage == 6:
+            return job
         return 2 * len(job_names) + spot if part == "b" else 2 * spot + stage % 2
 
     def job_copy(job, stage, part):
         dims = JOBS[job][4]
         spot = stage if part != "b" else 3
-        send_sem = ref["job_send"].at[job_send_spot(job, stage, part)]
-        recv_sem = ref["job_recv"].at[job_names.index(job), spot]
+        send_sem = ref["job_send"].at[job_send_spot(job, min(stage, 5), part)]
+        recv_sem = ref["job_recv"].at[job_names.index(job), min(spot, 5)]
         if stage < 4:
             pick, land = job_index(job, stage, part, False)
             source = ref["partial_" + job].at[pick]
@@ -837,11 +842,14 @@
             axis = dims[stage]
         else:
             final, columns = job_final(job)
-            if stage == 4:
+            if stage == 4 or job in DIRECT:
                 source = place = final.at[core, me["y"], :, columns]
             else:
                 source = place = final.at[core, :, :, columns]
-            axis = "y" if stage == 4 else "core"
+            axis = ("y", "core", "diagonal")[stage - 4]
+        if stage == 6:
+            send_sem = ref["direct_send"].at[DIRECT.index(job)]
+            recv_sem = ref["direct_recv"].at[DIRECT.index(job)]
         return pltpu.make_async_remote_copy(
             src_ref=source,
             dst_ref=place,
@@ -861,7 +869,7 @@
             return firsts
         if stage == 2:
             return ((1, ""),) + firsts
-        if stage == 4:
+        if stage == 4 or job in DIRECT and stage > 4:
             return ((len(dims) - 1, ""),) + firsts
         return ((stage - 1, ""),)
 
@@ -893,11 +901,12 @@
                     final, columns = job_final(job)
                     final[core, me["y"], :, columns] = sums
         arrived.add((job, stage, part))
-        for later in list(range(1, last + 1)) + [4, 5]:
+        for later in list(range(1, last + 1)) + ([4, 6, 5] if job in DIRECT else [4, 5]):
             ready = all((job,) + need in arrived for need in needs(job, later))
             if (job, later, "") not in sent and ready:
                 send(job, later)
-        if stage == 5:
+        ends = (4, 5, 6) if job in DIRECT else (5,)
+        if stage in ends and all((job, end, "") in arrived for end in ends):
             final, columns = job_final(job)
             _, _, first, wide, _ = JOBS[job]
             out = ref["grad_" + matrix]
@@ -1267,6 +1276,8 @@
             room["landed_%s_%d" % (job, stage)] = ((2,) * (count - 1 - stage) + block, LOW)
     scratch = {name: pltpu.VMEM(shape, dtype) for name, (shape, dtype) in room.items()}
     scratch["load"] = dma((len(inputs),))
+    scratch["direct_send"] = dma((len(DIRECT),))
+    scratch["direct_recv"] = dma((len(DIRECT),))
     downs = sum(job[0] == "down" for job in JOBS.values())
     for kind, shape in (("small", (3,)), ("core", (16,)), ("job", (2 * len(JOBS) + downs,)), ("vec", (1,))):
         scratch[kind + "_send"] = dma(shape)

time: 87.5 us -> 87.1 us (level)
  no operation moved by 1% of the time
where the time goes in v6:
time: 87.1 us; the launch traced here: 86.6 us
  Pallas kernels  85.8 us (99%)
    pallas_call x1, Pallas kernels, layer_device(): pl.pallas_call(functools.partial(layer_kernel, names), out_shape=list(out...  82.7 us
    pallas_call x1, Pallas kernels, layer_device(): pl.pallas_call(functools.partial(finish_kernel, tuple(operands) + tuple(r...  3.05 us

profile of v6, /device:TPU:1, one launch (start us, length us, event | category | flops | bytes accessed | tf_op | source)
XLA Modules:
  0.0 86.6 jit_solution(1206941653415546860)
XLA Ops:
  0.7 82.7 %layer.1 = (bf16[2,2,96,768]{3,2,1,0:T(8,128)(2,1)S(1)}, bf16[2,48,3072]{2,1,0:T(8,128)(2,1)S(1)}, bf16[2,48,512]{2,1,0:T(8,128)(2,1)S(1)}, bf16[2,48,768]{2,1,0...) custom-call(bf16[256,768]{1,0:T(8,128)(2,1)} %refs_0_.1, ...), custom_call_target="tpu_custom_call" | custom-call | tf_op jit(solution)/shard_map/layer/pallas_call | solution.py:1294
  83.4 3.1 %finish.1 = (f32[384,768]{1,0:T(8,128)}, f32[96,3072]{1,0:T(8,128)}, f32[96,512]{1,0:T(8,128)}, f32[96,768]{1,0:T(8,128)}, f32[96,2304]{1,0:T(8,128)}, /*index=5...) custom-call(bf16[384,768]{1,0:T(8,128)(2,1)S(1)} %bitcast.6, ...), custom_call_target="tpu_custom_call" | custom-call | tf_op jit(solution)/shard_map/finish/pallas_call | solution.py:1318

commit v7 on v5

--- a/solution.py
+++ b/solution.py
@@ -274,9 +274,9 @@
 AXES = ("zh", "zl", "x", "y")
 MATRICES = ("down", "up", "proj", "out", "qkv")
 JOBS = {
-    "down0": ("down", None, 0, 256, ("y", "zl", "zh")),
+    "down0": ("down", None, 0, 256, ("zl", "zh", "y")),
     "down1": ("down", None, 256, 256, ("y", "zl", "zh")),
-    "down2": ("down", None, 512, 256, ("zl", "zh", "y")),
+    "down2": ("down", None, 512, 256, ("y", "zl", "zh")),
     "up0a": ("up", 0, 0, 256, ("y", "zl", "zh", "x")),
     "up0b": ("up", 0, 256, 128, ("zl", "x", "zh", "y")),
     "up1a": ("up", 1, 0, 384, ("x", "zl", "y", "zh")),
@@ -341,16 +341,16 @@
     ("proj0", 1, ""),
     ("do", "first_back"),
     ("up0a", 1, ""),
+    ("down1", 0, "a"),
     ("down0", 0, "a"),
-    ("down2", 0, "a"),
     ("vec", 0),
     ("do", "multiply_down2"),
     ("do", "multiply_down3"),
-    ("down1", 0, "a"),
+    ("down2", 0, "a"),
     ("up3a", 1, ""),
     ("qkv0", 0, ""),
     ("up0a", 2, ""),
-    ("down2", 0, "b"),
+    ("down0", 0, "b"),
     ("up1a", 0, ""),
     ("up0b", 1, ""),
     ("qkv1", 0, ""),
@@ -358,20 +358,20 @@
     ("up2a", 1, ""),
     ("up1a", 1, ""),
     ("out0", 0, ""),
-    ("down2", 1, ""),
-    ("down0", 0, "b"),
+    ("down0", 1, ""),
+    ("down1", 0, "b"),
     ("up0b", 2, ""),
     ("qkv1", 1, ""),
-    ("down1", 0, "b"),
+    ("down2", 0, "b"),
     ("qkv2", 0, ""),
     ("up1a", 2, ""),
-    ("down0", 1, ""),
+    ("down1", 1, ""),
     ("up2a", 2, ""),
     ("out0", 1, ""),
     ("qkv3", 0, ""),
     ("qkv1", 2, ""),
-    ("down1", 1, ""),
-    ("down2", 2, ""),
+    ("down2", 1, ""),
+    ("down0", 2, ""),
     ("up0b", 3, ""),
     ("qkv4", 0, ""),
     ("qkv2", 1, ""),
@@ -380,17 +380,17 @@
     ("vec", 1),
     ("out0", 2, ""),
     ("qkv3", 1, ""),
-    ("down0", 2, ""),
+    ("down1", 2, ""),
     ("qkv0", 1, ""),
     ("qkv2", 2, ""),
-    ("down2", 4, ""),
+    ("down0", 4, ""),
     ("up0a", 3, ""),
     ("up0b", 4, ""),
     ("up3a", 3, ""),
-    ("down1", 2, ""),
+    ("down2", 2, ""),
     ("qkv4", 1, ""),
     ("up2a", 3, ""),
-    ("down2", 5, ""),
+    ("down0", 5, ""),
     ("up0b", 5, ""),
     ("up1a", 4, ""),
     ("qkv1", 3, ""),
@@ -398,23 +398,23 @@
     ("qkv3", 2, ""),
     ("vec", 2),
     ("qkv0", 2, ""),
-    ("down0", 4, ""),
+    ("down1", 4, ""),
     ("up1a", 5, ""),
     ("out0", 3, ""),
     ("up0a", 4, ""),
     ("qkv4", 2, ""),
     ("up3a", 4, ""),
-    ("down0", 5, ""),
+    ("down1", 5, ""),
     ("qkv2", 3, ""),
     ("vec", 3),
     ("up0a", 5, ""),
-    ("down1", 4, ""),
+    ("down2", 4, ""),
     ("qkv3", 3, ""),
     ("up3a", 5, ""),
     ("up2a", 4, ""),
     ("qkv1", 4, ""),
     ("qkv0", 3, ""),
-    ("down1", 5, ""),
+    ("down2", 5, ""),
     ("proj0", 4, ""),
     ("qkv4", 3, ""),
     ("up2a", 5, ""),
@@ -431,8 +431,11 @@
     ("qkv3", 5, ""),
     ("vec", 5),
     ("qkv0", 5, ""),
+    ("qkv0", 6, ""),
     ("qkv4", 5, ""),
+    ("qkv4", 6, ""),
 )
+DIRECT = ("qkv0", "qkv4",)
 VEC_STEPS = ("core", "x", "y", "zl", "zh", "core")
 PEERS = ("diagonal", "y", "core")
 PLACES = 64
@@ -822,13 +825,15 @@
 
     def job_send_spot(job, stage, part):
         spot = job_names.index(job)
+        if stage == 6:
+            return job
         return 2 * len(job_names) + spot if part == "b" else 2 * spot + stage % 2
 
     def job_copy(job, stage, part):
         dims = JOBS[job][4]
         spot = stage if part != "b" else 3
-        send_sem = ref["job_send"].at[job_send_spot(job, stage, part)]
-        recv_sem = ref["job_recv"].at[job_names.index(job), spot]
+        send_sem = ref["job_send"].at[job_send_spot(job, min(stage, 5), part)]
+        recv_sem = ref["job_recv"].at[job_names.index(job), min(spot, 5)]
         if stage < 4:
             pick, land = job_index(job, stage, part, False)
             source = ref["partial_" + job].at[pick]
@@ -837,11 +842,14 @@
             axis = dims[stage]
         else:
             final, columns = job_final(job)
-            if stage == 4:
+            if stage == 4 or job in DIRECT:
                 source = place = final.at[core, me["y"], :, columns]
             else:
                 source = place = final.at[core, :, :, columns]
-            axis = "y" if stage == 4 else "core"
+            axis = ("y", "core", "diagonal")[stage - 4]
+        if stage == 6:
+            send_sem = ref["direct_send"].at[DIRECT.index(job)]
+            recv_sem = ref["direct_recv"].at[DIRECT.index(job)]
         return pltpu.make_async_remote_copy(
             src_ref=source,
             dst_ref=place,
@@ -861,7 +869,7 @@
             return firsts
         if stage == 2:
             return ((1, ""),) + firsts
-        if stage == 4:
+        if stage == 4 or job in DIRECT and stage > 4:
             return ((len(dims) - 1, ""),) + firsts
         return ((stage - 1, ""),)
 
@@ -893,11 +901,12 @@
                     final, columns = job_final(job)
                     final[core, me["y"], :, columns] = sums
         arrived.add((job, stage, part))
-        for later in list(range(1, last + 1)) + [4, 5]:
+        for later in list(range(1, last + 1)) + ([4, 6, 5] if job in DIRECT else [4, 5]):
             ready = all((job,) + need in arrived for need in needs(job, later))
             if (job, later, "") not in sent and ready:
                 send(job, later)
-        if stage == 5:
+        ends = (4, 5, 6) if job in DIRECT else (5,)
+        if stage in ends and all((job, end, "") in arrived for end in ends):
             final, columns = job_final(job)
             _, _, first, wide, _ = JOBS[job]
             out = ref["grad_" + matrix]
@@ -1267,6 +1276,8 @@
             room["landed_%s_%d" % (job, stage)] = ((2,) * (count - 1 - stage) + block, LOW)
     scratch = {name: pltpu.VMEM(shape, dtype) for name, (shape, dtype) in room.items()}
     scratch["load"] = dma((len(inputs),))
+    scratch["direct_send"] = dma((len(DIRECT),))
+    scratch["direct_recv"] = dma((len(DIRECT),))
     downs = sum(job[0] == "down" for job in JOBS.values())
     for kind, shape in (("small", (3,)), ("core", (16,)), ("job", (2 * len(JOBS) + downs,)), ("vec", (1,))):
         scratch[kind + "_send"] = dma(shape)

time: 87.5 us -> 87.1 us (level)
  no operation moved by 1% of the time
where the time goes in v7:
time: 87.1 us; the launch traced here: 86.9 us
  Pallas kernels  86.1 us (99%)
    pallas_call x1, Pallas kernels, layer_device(): pl.pallas_call(functools.partial(layer_kernel, names), out_shape=list(out...  83 us
    pallas_call x1, Pallas kernels, layer_device(): pl.pallas_call(functools.partial(finish_kernel, tuple(operands) + tuple(r...  3.05 us

profile of v7, /device:TPU:1, one launch (start us, length us, event | category | flops | bytes accessed | tf_op | source)
XLA Modules:
  0.0 86.9 jit_solution(1467639461757800253)
XLA Ops:
  0.7 83.0 %layer.1 = (bf16[2,2,96,768]{3,2,1,0:T(8,128)(2,1)S(1)}, bf16[2,48,3072]{2,1,0:T(8,128)(2,1)S(1)}, bf16[2,48,512]{2,1,0:T(8,128)(2,1)S(1)}, bf16[2,48,768]{2,1,0...) custom-call(bf16[256,768]{1,0:T(8,128)(2,1)} %refs_0_.1, ...), custom_call_target="tpu_custom_call" | custom-call | tf_op jit(solution)/shard_map/layer/pallas_call | solution.py:1294
  83.7 3.1 %finish.1 = (f32[384,768]{1,0:T(8,128)}, f32[96,3072]{1,0:T(8,128)}, f32[96,512]{1,0:T(8,128)}, f32[96,768]{1,0:T(8,128)}, f32[96,2304]{1,0:T(8,128)}, /*index=5...) custom-call(bf16[384,768]{1,0:T(8,128)(2,1)S(1)} %bitcast.6, ...), custom_call_target="tpu_custom_call" | custom-call | tf_op jit(solution)/shard_map/finish/pallas_call | solution.py:1318
